TPU v7x, 32 devices: a whole 2x2x4 slice. The times are simulated.
32 devices in a mesh: gx: 8 (over y, x, core), gy: 4 (over z).
Axes of the slice: x: 2, y: 2, z: 4, core: 2. Of those that a mesh axis runs over, the one named last changes fastest.
Arguments:
- velocity: float32 [3, 512, 64, 512], P(None, 'gx', None, 'gy'), may hold values from -6 to 6
- cotangent: float32 [3, 512, 64, 512], P(None, 'gx', None, 'gy'), may hold values from -6 to 6
- coefficient: float32 [512, 64, 512], P('gx', None, 'gy'), may hold values from 0.5 to 1.5
- level_profile: float32 [64], replicated, may hold values from 0.1 to 1
- vert_deriv: float32 [64, 64], replicated, may hold values from -0.75 to 0.75
- eigen_vectors: float32 [64, 64], replicated, may hold values from -0.75 to 0.75
- eigen_inverse: float32 [64, 64], replicated, may hold values from -0.75 to 0.75
- eigen_rates: float32 [64], replicated, may hold values from 0.25 to 4
Outputs:
- new_velocity: float32 [3, 512, 64, 512], P(None, 'gx', None, 'gy')
- adjoint_velocity: float32 [3, 512, 64, 512], P(None, 'gx', None, 'gy')
- viscosity_gradient: float32 [512, 64, 512], P('gx', None, 'gy')
All inputs are finite; a program needn't handle non-finite values.
Results may differ from a plain program's by a relative error of at most 0.00005.
Values sent between devices are 32-bit elements; how exact they have to be, the bound alone decides.
No kernel may reach another device: no remote copies, remote signals or barrier semaphores. Data moves between devices by JAX's collectives and lax.ppermute only.
A program may use at most 256 MiB of HBM per device.

v0:
```python
import math

import jax
import jax.numpy as jnp
from jax import lax
from jax.sharding import PartitionSpec as P

step_weight = 0.3 * 8.0 / 15.0
precise = lax.Precision.HIGHEST


def padded_2(cells, sides, width):
    for axis, dim in sides:
        count = lax.axis_size(axis)
        head = lax.slice_in_dim(cells, 0, width, axis=dim)
        tail = lax.slice_in_dim(cells, cells.shape[dim] - width, cells.shape[dim], axis=dim)
        cells = jnp.concatenate(
            [
                lax.ppermute(tail, axis, [(i, (i + 1) % count) for i in range(count)]),
                cells,
                lax.ppermute(head, axis, [((i + 1) % count, i) for i in range(count)]),
            ],
            axis=dim,
        )
    return cells


def levels(matrix, field):
    return jnp.einsum("mz,xzy->xmy", matrix, field, precision=precise)


def wavenumbers(count, start, length):
    modes = start + jnp.arange(length, dtype=jnp.int32)
    signed = jnp.where(modes < count // 2, modes, modes - count)
    signed = jnp.where(modes == count // 2, jnp.zeros_like(signed), signed)
    return signed.astype(jnp.float32) * (2.0 * math.pi / count)


def angles(first_count, second_count, count):
    first = jnp.arange(first_count, dtype=jnp.int32)
    second = jnp.arange(second_count, dtype=jnp.int32)
    product = first[:, None] * second[None, :] % count
    return product.astype(jnp.float32) * (2.0 * math.pi / count)


def along_x(field, table):
    return jnp.einsum("cxzy,xk->ckzy", field, table, precision=precise)


def along_y(field, table):
    return jnp.einsum("ckzy,yq->ckzq", field, table, precision=precise)


def forward_x(columns):
    full_x = columns.shape[1]
    angle = angles(full_x, full_x, full_x)
    real_x = along_x(columns, jnp.cos(angle))
    imag_x = -along_x(columns, jnp.sin(angle))
    return (real_x, imag_x)


def inverse_tables(modes, full_x):
    angle = angles(modes, full_x, full_x)
    cos_back = jnp.cos(angle)
    sin_back = jnp.sin(angle)
    return (cos_back, sin_back)


def solve_terms(real_y, imag_y, wave_x, wave_y, factor):
    out_real = []
    out_imag = []
    div_real = real_y[2] - wave_x * imag_y[0] - wave_y * imag_y[1]
    div_imag = imag_y[2] + wave_x * real_y[0] + wave_y * real_y[1]
    solved_real = factor * div_real
    solved_imag = factor * div_imag
    out_real += [-wave_x * solved_imag, -wave_y * solved_imag, solved_real]
    out_imag += [wave_x * solved_real, wave_y * solved_real, solved_imag]
    return (jnp.stack(out_real), jnp.stack(out_imag))


def spectral(passes, eigen_rates):
    joined = passes[0]
    columns = lax.all_to_all(joined, "gx", split_axis=2, concat_axis=1, tiled=True)
    full_x = columns.shape[1]
    real_x, imag_x = forward_x(columns)
    pieces = []
    pieces += [real_x[0], imag_x[0], real_x[1], imag_x[1], real_x[2], imag_x[2]]
    rows = lax.all_to_all(jnp.stack(pieces), "gy", split_axis=1, concat_axis=3, tiled=True)
    part_x = rows.shape[1]
    part_z = rows.shape[2]
    full_y = rows.shape[3]
    angle_y = angles(full_y, full_y, full_y)
    cos_y = jnp.cos(angle_y)
    sin_y = jnp.sin(angle_y)
    real_in = rows[0::2]
    imag_in = rows[1::2]
    real_y = along_y(real_in, cos_y) + along_y(imag_in, sin_y)
    imag_y = along_y(imag_in, cos_y) - along_y(real_in, sin_y)
    wave_x = wavenumbers(full_x, lax.axis_index("gy") * part_x, part_x)[:, None, None]
    wave_y = wavenumbers(full_y, 0, full_y)[None, None, :]
    rates = lax.dynamic_slice_in_dim(eigen_rates, lax.axis_index("gx") * part_z, part_z)
    factor = -1.0 / (rates[None, :, None] + wave_x * wave_x + wave_y * wave_y)
    spec_real, spec_imag = solve_terms(real_y, imag_y, wave_x, wave_y, factor)
    back_real = (along_y(spec_real, cos_y) - along_y(spec_imag, sin_y)) / full_y
    back_imag = (along_y(spec_imag, cos_y) + along_y(spec_real, sin_y)) / full_y
    returned = lax.all_to_all(
        jnp.concatenate([back_real, back_imag], axis=0),
        "gy",
        split_axis=3,
        concat_axis=1,
        tiled=True,
    )
    total = spec_real.shape[0]
    ret_real = returned[:total]
    ret_imag = returned[total:]
    cos_back, sin_back = inverse_tables(ret_real.shape[1], full_x)
    physical = (along_x(ret_real, cos_back) - along_x(ret_imag, sin_back)) / full_x
    placed = lax.all_to_all(physical, "gx", split_axis=1, concat_axis=2, tiled=True)
    return [placed]


def body(
    velocity,
    cotangent,
    coefficient,
    level_profile,
    vert_deriv,
    eigen_vectors,
    eigen_inverse,
    eigen_rates,
):
    padded = padded_2(velocity, (("gx", 1), ("gy", 3)), 1)
    east = padded[:, 2:, :, 1:-1]
    west = padded[:, :-2, :, 1:-1]
    north = padded[:, 1:-1, :, 2:]
    south = padded[:, 1:-1, :, :-2]
    slope_x = 0.5 * (east - west)
    slope_y = 0.5 * (north - south)
    laplace = east + west + north + south - 4.0 * velocity
    slope_z = jnp.einsum("mz,cxzy->cxmy", vert_deriv, velocity, precision=precise)
    advect = -(velocity[0] * slope_x + velocity[1] * slope_y + velocity[2] * slope_z)
    viscosity = coefficient * level_profile[None, :, None]
    section = velocity + step_weight * (advect + viscosity * laplace)
    forward_in = jnp.stack(
        [
            levels(eigen_inverse, section[0]),
            levels(eigen_inverse, section[1]),
            levels(eigen_inverse, levels(vert_deriv, section[2])),
        ]
    )
    vectors_t = eigen_vectors.T
    inverse_t = eigen_inverse.T
    deriv_t = vert_deriv.T
    adjoint_in = jnp.stack(
        [
            -levels(vectors_t, cotangent[0]),
            -levels(vectors_t, cotangent[1]),
            levels(vectors_t, levels(deriv_t, cotangent[2])),
        ]
    )
    forward_out = spectral([forward_in], eigen_rates)[0]
    adjoint_out = spectral([adjoint_in], eigen_rates)[0]
    pressure = jnp.stack(
        [
            levels(eigen_vectors, forward_out[0]),
            levels(eigen_vectors, forward_out[1]),
            levels(vert_deriv, levels(eigen_vectors, forward_out[2])),
        ]
    )
    new_velocity = section - pressure
    adjoint_velocity = cotangent + jnp.stack(
        [
            levels(inverse_t, adjoint_out[0]),
            levels(inverse_t, adjoint_out[1]),
            -levels(deriv_t, levels(inverse_t, adjoint_out[2])),
        ]
    )
    gradient = (
        step_weight * level_profile[None, :, None] * jnp.sum(adjoint_velocity * laplace, axis=0)
    )
    return (new_velocity, adjoint_velocity, gradient)


def solution(mesh):
    in_specs = (
        P(None, "gx", None, "gy"),
        P(None, "gx", None, "gy"),
        P("gx", None, "gy"),
        P(),
        P(),
        P(),
        P(),
        P(),
    )
    out_specs = (P(None, "gx", None, "gy"), P(None, "gx", None, "gy"), P("gx", None, "gy"))
    return jax.shard_map(body, mesh=mesh, in_specs=in_specs, out_specs=out_specs, check_vma=False)
```

profile of v0, /device:TPU:0, one launch (start us, length us, event | category | flops | bytes accessed | tf_op | source)
XLA Modules:
  0.0 1776.4 jit_solution(6801159558390557658)
XLA Ops:
  36.2 63.1 %collective-permute-done.1 = f32[3,1,64,128]{3,2,1,0:T(8,128)S(1)} collective-permute-done((f32[3,1,64,128]{3,2,1,0:T(8,128)S(1)}, f32[3,1,64,128]{3,2,1,0:T(8,128)S(1)}, u32[]{:S(2)}, u32[]{:S(2)}) %collective-permute-start.1) | collective-permute-done | bytes 98336 | tf_op jit(solution)/shard_map/ppermute | solution.py:19
  103.9 11.3 fusion.314
  145.8 25.7 %fusion.4 = f32[3,64,64,128]{3,2,1,0:T(8,128)S(1)} fusion(f32[3,64,64,128]{3,2,1,0:T(8,128)} %param.8, f32[3,1,64,128]{3,2,1,0:T(8,128)S(1)} %collective-permute-done, f32[3,1,64,128]{3,2,1,0:T(8,128)S(1)} %collective-permute-done.1, f32[64,64,128]{2,1,0:T(8,128)} %broadcast_multiply_fusion.9, f32[64,64,128]{2,1,0:T(8,128)} %get-tuple-element.31, ...), kind=kOutput, calls=%fused_computation.21 | convolution fusion | flops 1240989696 | bytes 27773952 | tf_op jit(solution)/shard_map/mz,cxzy->cxmy/dot_general | solution.py:140
  195.8 14.7 convolution_bitcast_fusion
  211.9 14.9 negate_bitcast_fusion
  234.5 16.6 copy.148
  251.2 12.8 all-to-all-done
  273.7 14.9 convolution_bitcast_fusion.1
  290.0 14.7 negate_bitcast_fusion.1
  312.2 16.9 copy.125
  329.0 211.6 %all-to-all-done.5 = f32[6,512,8,128]{3,2,0,1:T(8,128)} async-done(((f32[6,512,8,128]{3,2,0,1:T(8,128)}), f32[6,512,8,128]{3,2,0,1:T(8,128)}, u32[]{:S(2)}, u32[]{:S(2)}) %all-to-all-start.5) | async-done | bytes 12582944 | tf_op jit(solution)/shard_map/all_to_all | solution.py:88
  547.1 16.3 copy.254
  563.4 15.2 all_to_all.117
  578.6 17.9 %fusion.7 = f32[3,128,8,512]{3,1,2,0:T(8,128)S(1)} fusion(f32[6,128,8,512]{3,1,2,0:T(8,128)} %all_to_all.117), kind=kOutput, calls=%fused_computation.34 | convolution fusion | flops 9667346432 | bytes 12582912 | tf_op jit(solution)/shard_map/ckzy,yq->ckzq/dot_general | solution.py:51
  596.5 15.3 fusion.5
  611.7 16.1 fusion.35
  627.9 16.6 fusion.38
  644.5 174.5 %all-to-all-done.1 = f32[6,512,8,128]{3,2,0,1:T(8,128)} async-done(((f32[6,512,8,128]{3,2,0,1:T(8,128)}), f32[6,512,8,128]{3,2,0,1:T(8,128)}, u32[]{:S(2)}, u32[]{:S(2)}) %all-to-all-start.1) | async-done | bytes 12582944 | tf_op jit(solution)/shard_map/all_to_all | solution.py:88
  818.9 16.5 copy.255
  835.4 15.3 all_to_all.103
  850.7 18.2 %fusion.13 = f32[3,128,8,512]{3,1,2,0:T(8,128)S(1)} fusion(f32[6,128,8,512]{3,1,2,0:T(8,128)} %all_to_all.103), kind=kOutput, calls=%fused_computation.40 | convolution fusion | flops 9667346432 | bytes 12582912 | tf_op jit(solution)/shard_map/ckzy,yq->ckzq/dot_general | solution.py:51
  869.0 15.2 fusion.15
  884.2 16.2 fusion.32
  900.4 16.3 fusion.29
  916.7 10.9 broadcast_multiply_fusion.6
  931.3 15.2 fusion.22
  946.6 15.2 fusion.21
  963.9 17.1 subtract_multiply_fusion
  981.0 17.3 add_multiply_fusion
  998.3 11.9 pad_maximum_fusion.1
  1010.2 12.7 copy.158
  1029.4 18.0 %fusion.26 = f32[3,128,8,512]{3,1,2,0:T(8,128)S(1)} fusion(f32[1,128,8,512]{3,1,2,0:T(8,128)} %copy-done.6, f32[1,128,8,512]{3,1,2,0:T(8,128)} %get-tuple-element.41, f32[1,128,8,512]{3,1,2,0:T(8,128)} %get-tuple-element.11), kind=kOutput, calls=%fused_computation.53 | convolution fusion | flops 9670492160 | bytes 12582912 | tf_op jit(solution)/shard_map/ckzy,yq->ckzq/dot_general | solution.py:51
  1047.4 15.5 fusion.25
  1063.0 17.2 subtract_multiply_fusion.1
  1080.2 17.1 add_multiply_fusion.1
  1097.3 11.8 pad_maximum_fusion
  1109.1 12.7 copy.135
  1121.8 179.8 %all-to-all-done.6 = f32[6,128,8,512]{1,2,0,3:T(8,128)} async-done(((f32[6,128,8,512]{1,2,0,3:T(8,128)}), f32[6,128,8,512]{1,2,0,3:T(8,128)}, u32[]{:S(2)}, u32[]{:S(2)}) %all-to-all-start.6) | async-done | bytes 12582944 | tf_op jit(solution)/shard_map/all_to_all | solution.py:106
  1307.9 13.1 copy.159
  1330.0 14.6 fusion.143
  1344.6 15.1 multiply_bitcast_fusion
  1365.9 214.4 %all-to-all-done.2 = f32[6,128,8,512]{1,2,0,3:T(8,128)} async-done(((f32[6,128,8,512]{1,2,0,3:T(8,128)}), f32[6,128,8,512]{1,2,0,3:T(8,128)}, u32[]{:S(2)}, u32[]{:S(2)}) %all-to-all-start.2) | async-done | bytes 12582944 | tf_op jit(solution)/shard_map/all_to_all | solution.py:106
  1585.9 13.2 copy.136
  1608.1 14.6 fusion.146
  1622.7 15.1 multiply_bitcast_fusion.1
  1644.2 13.5 all-to-all-done.7
  1677.5 56.5 %all-to-all-done.3 = f32[3,512,8,128]{3,2,0,1:T(8,128)} async-done(((f32[3,512,8,128]{3,2,0,1:T(8,128)}), f32[3,512,8,128]{3,2,0,1:T(8,128)}, u32[]{:S(2)}, u32[]{:S(2)}) %all-to-all-start.3) | async-done | bytes 6291488 | tf_op jit(solution)/shard_map/all_to_all | solution.py:118
  1751.5 14.2 multiply_reduce_fusion
  (160 shorter events, 231.2 us)
Async XLA Ops:
  0.6 7.1 copy-start
  0.6 10.6 copy-start.19
  21.2 166.5 %all-to-all-start.4 = ((f32[3,64,64,128]{3,1,0,2:T(8,128)}), f32[3,64,64,128]{3,1,0,2:T(8,128)}, u32[]{:S(2)}, u32[]{:S(2)}) async-start(f32[3,64,64,128]{3,1,0,2:T(8,128)} %copy.146), calls=%async_computation.4 | async-start | bytes 12582912 | tf_op jit(solution)/shard_map/all_to_all | solution.py:83
  27.3 72.1 %collective-permute-start.1 = (f32[3,1,64,128]{3,2,1,0:T(8,128)S(1)}, f32[3,1,64,128]{3,2,1,0:T(8,128)S(1)}, u32[]{:S(2)}, u32[]{:S(2)}) collective-permute-start(f32[3,1,64,128]{3,2,1,0:T(8,128)S(1)} %get-tuple-element.32), channel_id=1, source_target_pairs={{0,4},{4,8},{8,12},{12,16},{16,20},{20,24},{24,28},{28,0},{1,5},{5... | collective-permute-start | bytes 294920 | tf_op jit(solution)/shard_map/ppermute | solution.py:19
  27.8 72.2 %slice-start = ((s8[6291456]{0:T(1024)(128)(4,1)}), s8[4194304]{0:T(1024)(128)(4,1)S(1)}, s32[]{:S(2)}) async-start(s8[6291456]{0:T(1024)(128)(4,1)} %bitcast.311), calls=%async_computation.8 | async-start | bytes 8388608
  27.8 72.2 %slice-start.1 = ((s8[6291456]{0:T(1024)(128)(4,1)}), s8[2097152]{0:T(1024)(128)(4,1)S(1)}, s32[]{:S(2)}) async-start(s8[6291456]{0:T(1024)(128)(4,1)} %bitcast.311), calls=%async_computation.9 | async-start | bytes 4194304
  27.8 75.4 %collective-permute-start = (f32[3,1,64,128]{3,2,1,0:T(8,128)S(1)}, f32[3,1,64,128]{3,2,1,0:T(8,128)S(1)}, u32[]{:S(2)}, u32[]{:S(2)}) collective-permute-start(f32[3,1,64,128]{3,2,1,0:T(8,128)S(1)} %get-tuple-element.33), channel_id=1, source_target_pairs={{4,0},{8,4},{12,8},{16,12},{20,16},{24,20},{28,24},{0,28},{5,1},{9... | collective-permute-start | bytes 294920 | tf_op jit(solution)/shard_map/ppermute | solution.py:21
  99.3 46.5 %copy-start.21 = (f32[3,1,64,128]{3,2,1,0:T(8,128)}, f32[3,1,64,128]{3,2,1,0:T(8,128)S(1)}, u32[]{:S(2)}) copy-start(f32[3,1,64,128]{3,2,1,0:T(8,128)S(1)} %collective-permute-done.1) | copy-start | bytes 294916
  103.2 42.6 %copy-start.23 = (f32[3,1,64,128]{3,2,1,0:T(8,128)}, f32[3,1,64,128]{3,2,1,0:T(8,128)S(1)}, u32[]{:S(2)}) copy-start(f32[3,1,64,128]{3,2,1,0:T(8,128)S(1)} %collective-permute-done) | copy-start | bytes 294916
  115.2 16.1 copy-start.16
  115.2 16.1 copy-start.25
  121.0 12.0 collective-permute-start.2
  131.3 8.1 collective-permute-start.3
  145.8 25.8 %copy-start.17 = (f32[64,64]{1,0:T(8,128)S(1)}, f32[64,64]{1,0:T(8,128)}, u32[]{:S(2)}) copy-start(f32[64,64]{1,0:T(8,128)} %param.14) | copy-start | bytes 49156
  171.6 6.1 copy-start.3
  187.6 76.4 %all-to-all-start = ((f32[3,64,64,128]{3,1,0,2:T(8,128)}), f32[3,64,64,128]{3,1,0,2:T(8,128)}, u32[]{:S(2)}, u32[]{:S(2)}) async-start(f32[3,64,64,128]{3,1,0,2:T(8,128)} %copy.123), calls=%async_computation | async-start | bytes 12582912 | tf_op jit(solution)/shard_map/all_to_all | solution.py:83
  264.0 276.6 %all-to-all-start.5 = ((f32[6,512,8,128]{3,2,0,1:T(8,128)}), f32[6,512,8,128]{3,2,0,1:T(8,128)}, u32[]{:S(2)}, u32[]{:S(2)}) async-start(f32[6,512,8,128]{3,2,0,1:T(8,128)} %copy.148), calls=%async_computation.5 | async-start | bytes 25165824 | tf_op jit(solution)/shard_map/all_to_all | solution.py:88
  329.0 217.9 %copy-start.27 = (f32[64]{0:T(128)S(1)}, f32[64]{0:T(128)}, u32[]{:S(2)}) copy-start(f32[64]{0:T(128)} %param.15) | copy-start | bytes 772
  540.6 278.3 %all-to-all-start.1 = ((f32[6,512,8,128]{3,2,0,1:T(8,128)}), f32[6,512,8,128]{3,2,0,1:T(8,128)}, u32[]{:S(2)}, u32[]{:S(2)}) async-start(f32[6,512,8,128]{3,2,0,1:T(8,128)} %copy.125), calls=%async_computation.1 | async-start | bytes 25165824 | tf_op jit(solution)/shard_map/all_to_all | solution.py:88
  578.6 17.9 %copy-start.1 = (f32[6,128,8,512]{3,1,2,0:T(8,128)S(1)}, f32[6,128,8,512]{3,1,2,0:T(8,128)}, u32[]{:S(2)}) copy-start(f32[6,128,8,512]{3,1,2,0:T(8,128)} %all_to_all.117) | copy-start | bytes 37748740
  850.7 18.3 %copy-start.2 = (f32[6,128,8,512]{3,1,2,0:T(8,128)S(1)}, f32[6,128,8,512]{3,1,2,0:T(8,128)}, u32[]{:S(2)}) copy-start(f32[6,128,8,512]{3,1,2,0:T(8,128)} %all_to_all.103) | copy-start | bytes 37748740
  884.2 32.5 %slice-start.8 = ((s8[6291456]{0:T(1024)(128)(4,1)}), s8[2097152]{0:T(1024)(128)(4,1)S(1)}, s32[]{:S(2)}) async-start(s8[6291456]{0:T(1024)(128)(4,1)} %bitcast.327), calls=%async_computation.16 | async-start | bytes 4194304
  900.4 16.3 slice-start.9
  927.6 34.2 %copy-start.6 = (f32[1,128,8,512]{3,1,2,0:T(8,128)}, f32[1,128,8,512]{3,1,2,0:T(8,128)S(1)}, u32[]{:S(2)}) copy-start(f32[1,128,8,512]{3,1,2,0:T(8,128)S(1)} %get-tuple-element.16) | copy-start | bytes 6291460
  927.6 3.1 copy-start.8
  927.6 3.7 copy-start.15
  961.8 2.1 copy-start.14
  1022.9 278.8 %all-to-all-start.6 = ((f32[6,128,8,512]{1,2,0,3:T(8,128)}), f32[6,128,8,512]{1,2,0,3:T(8,128)}, u32[]{:S(2)}, u32[]{:S(2)}) async-start(f32[6,128,8,512]{1,2,0,3:T(8,128)} %copy.158), calls=%async_computation.6 | async-start | bytes 25165824 | tf_op jit(solution)/shard_map/all_to_all | solution.py:106
  1029.3 18.0 %copy-start.7 = (f32[1,128,8,512]{3,1,2,0:T(8,128)S(1)}, f32[1,128,8,512]{3,1,2,0:T(8,128)}, u32[]{:S(2)}) copy-start(f32[1,128,8,512]{3,1,2,0:T(8,128)} %copy-done.6) | copy-start | bytes 6291460
  1029.4 18.0 %copy-start.11 = (f32[1,128,8,512]{3,1,2,0:T(8,128)S(1)}, f32[1,128,8,512]{3,1,2,0:T(8,128)}, u32[]{:S(2)}) copy-start(f32[1,128,8,512]{3,1,2,0:T(8,128)} %get-tuple-element.11) | copy-start | bytes 6291460
  1029.4 18.0 %copy-start.12 = (f32[1,128,8,512]{3,1,2,0:T(8,128)S(1)}, f32[1,128,8,512]{3,1,2,0:T(8,128)}, u32[]{:S(2)}) copy-start(f32[1,128,8,512]{3,1,2,0:T(8,128)} %get-tuple-element.41) | copy-start | bytes 6291460
  1047.4 15.5 copy-start.10
  1047.4 15.5 copy-start.13
  1301.6 278.7 %all-to-all-start.2 = ((f32[6,128,8,512]{1,2,0,3:T(8,128)}), f32[6,128,8,512]{1,2,0,3:T(8,128)}, u32[]{:S(2)}, u32[]{:S(2)}) async-start(f32[6,128,8,512]{1,2,0,3:T(8,128)} %copy.135), calls=%async_computation.2 | async-start | bytes 25165824 | tf_op jit(solution)/shard_map/all_to_all | solution.py:106
  1329.9 14.6 copy-start.4
  1580.4 77.3 %all-to-all-start.7 = ((f32[3,512,8,128]{3,2,0,1:T(8,128)}), f32[3,512,8,128]{3,2,0,1:T(8,128)}, u32[]{:S(2)}, u32[]{:S(2)}) async-start(f32[3,512,8,128]{3,2,0,1:T(8,128)} %copy.160), calls=%async_computation.7 | async-start | bytes 12582912 | tf_op jit(solution)/shard_map/all_to_all | solution.py:118
  1608.1 14.6 copy-start.5
  1644.2 18.7 %copy-start.26 = (f32[64]{0:T(128)S(1)}, f32[64]{0:T(128)}, u32[]{:S(2)}) copy-start(f32[64]{0:T(128)} %param.11) | copy-start | bytes 772
  1657.6 76.4 %all-to-all-start.3 = ((f32[3,512,8,128]{3,2,0,1:T(8,128)}), f32[3,512,8,128]{3,2,0,1:T(8,128)}, u32[]{:S(2)}, u32[]{:S(2)}) async-start(f32[3,512,8,128]{3,2,0,1:T(8,128)} %copy.137), calls=%async_computation.3 | async-start | bytes 12582912 | tf_op jit(solution)/shard_map/all_to_all | solution.py:118
  1737.2 14.2 slice-start.4
  1737.2 14.2 slice-start.6
  1739.1 5.6 copy-start.9
  1739.1 12.3 slice-start.5
  1739.1 12.3 slice-start.7
  1741.1 10.3 slice-start.2
  1741.2 10.3 copy-start.22
  1741.2 10.3 copy-start.24
  1744.7 6.8 slice-start.3
  (2 other events, 2.6 us)
where the time goes:
time: 1790 us; the launch traced here: 1780 us
  waiting for transfers between devices  926 us (52%)
  matrix products  452 us (25%)
  local copies, waits for them, and re-layouts  269 us (15%)
  other arithmetic  73.1 us (4%)
  starting transfers between devices  53.9 us (3%)
    all_to_all x2, waiting for transfers between devices, spectral(): lax.all_to_all(jnp.concatenate([back_real, back_imag], axis=0), 'gy', spl...  394 us
    all_to_all x2, waiting for transfers between devices, spectral(): lax.all_to_all(jnp.stack(pieces), 'gy', split_axis=1, concat_axis=3, tile...  386 us
    dot_general x16, matrix products, along_y(): return jnp.einsum('ckzy,yq->ckzq', field, table, precision=precise)  264 us
    dot_general x8, matrix products, along_x(): return jnp.einsum('cxzy,xk->ckzy', field, table, precision=precise)  119 us
    all_to_all x2, waiting for transfers between devices, spectral(): lax.all_to_all(physical, 'gx', split_axis=1, concat_axis=2, tiled=True)  70 us
    all_to_all x4, local copies, waits for them, and re-layouts, spectral(): lax.all_to_all(jnp.stack(pieces), 'gy', split_axis=1, concat_axis=3, tile...  63.3 us
    ppermute x2, waiting for transfers between devices, padded_2(): lax.ppermute(tail, axis, [(i, (i + 1) % count) for i in range(count)])  63.1 us
    dot_general x16, matrix products, levels(): return jnp.einsum('mz,xzy->xmy', matrix, field, precision=precise)  43.6 us
  transfers between devices with their start and end apart: 12, of which 8 were waited for; matrix products, arithmetic and copies ran while one was open for 29% of the time, Pallas kernels for 0%

commit v1 on v0

v1 whole, which is shorter than its diff:
```python
import functools
import math

import jax
import jax.numpy as jnp
import numpy as np
from jax import lax
from jax.experimental import pallas as pl
from jax.experimental.pallas import tpu as pltpu
from jax.sharding import PartitionSpec as P

step_weight = 0.3 * 8.0 / 15.0
precise = lax.Precision.HIGHEST
half = jnp.bfloat16
vmem_bytes = 60 * 1024 * 1024


def line_transform(count):
    modes = count // 2
    points = np.arange(count)
    angle = (np.arange(modes)[:, None] * points[None, :] % count) * (2.0 * np.pi / count)
    real = np.cos(angle)
    imag = -np.sin(angle)
    imag[0] = np.where(points % 2 == 0, 1.0, -1.0)
    scale = np.full((modes, 1), 2.0 / count)
    scale[0] = 1.0 / count
    wave = (np.arange(modes) * (2.0 * np.pi / count))[:, None]
    forward = np.stack([real, imag])
    forward_slope = np.stack([-wave * imag, wave * real])
    inverse = np.stack([scale * real, scale * imag])
    inverse_slope = np.stack([scale * wave * imag, -scale * wave * real])
    return forward, forward_slope, inverse, inverse_slope


def grouped(table, groups):
    parts, modes, points = table.shape
    split = table.reshape(parts, groups, modes // groups, points)
    return np.swapaxes(split, 0, 1).reshape(groups, parts * modes // groups, points)


def halves(table):
    table = table.astype(np.float32)
    high = table.astype(half)
    low = (table - high.astype(np.float32)).astype(half)
    return np.stack([high, low])


def split(values):
    high = values.astype(half)
    low = (values - high.astype(jnp.float32)).astype(half)
    return high, low


def product(left, right):
    def dot(a, b):
        return jnp.dot(a, b, preferred_element_type=jnp.float32)

    return dot(left[0], right[0]) + (dot(left[0], right[1]) + dot(left[1], right[0]))


def parameters(flops, read, written):
    return dict(
        compiler_params=pltpu.CompilerParams(vmem_limit_bytes=vmem_bytes),
        cost_estimate=pl.CostEstimate(
            flops=100 * flops, bytes_accessed=400 * (read + written), transcendentals=0
        ),
    )


def block_x(part_x):
    return 16 if part_x % 16 == 0 else 8


def wide(matrix):
    high = lax.reduce_precision(matrix, exponent_bits=8, mantissa_bits=7)
    low = (matrix - high).astype(half)
    high = high.astype(half)
    return jnp.concatenate([high, high, low], axis=-1)


def narrow_product(matrix, field):
    high, low = split(field)
    return jnp.dot(
        matrix, jnp.concatenate([high, low, high], axis=0), preferred_element_type=jnp.float32
    )


anywhere = pl.BlockSpec(memory_space=pl.ANY)
scalars = pl.BlockSpec(memory_space=pltpu.SMEM)


def into_kernel(field_ref, matrix_ref, *refs):
    out_ref, rows_ref = refs[-2:]
    sublanes, levels, part_y = field_ref.shape[1:]
    for pair in range(0, sublanes, 2):
        fields = jnp.concatenate([field_ref[0, pair], field_ref[0, pair + 1]], axis=1)
        turned = narrow_product(matrix_ref[0], fields)
        for x in (pair, pair + 1):
            rows_ref[pl.ds(x, levels, stride=sublanes), :] = turned[
                :, (x - pair) * part_y : (x - pair + 1) * part_y
            ]
    out_ref[...] = rows_ref[...].reshape(out_ref.shape)


def into_levels(fields, matrices, components, groups, *follow):
    _, part_x, levels, part_y = fields.shape
    sublanes = block_x(part_x)
    count = len(components)
    per = levels // groups
    first, step = components[0], (components[1] - components[0] if count > 1 else 1)
    size = count * part_x * levels * part_y
    return pl.pallas_call(
        into_kernel,
        grid=(count, part_x // sublanes),
        in_specs=[
            pl.BlockSpec(
                (1, sublanes, levels, part_y), lambda f, i: (first + f * step, i, 0, 0)
            ),
            pl.BlockSpec((1, levels, 3 * levels), lambda f, i: (f, 0, 0)),
        ]
        + [anywhere] * len(follow),
        out_specs=pl.BlockSpec((groups, 1, per, sublanes, part_y), lambda f, i: (0, f, 0, i, 0)),
        out_shape=jax.ShapeDtypeStruct((groups, count, per, part_x, part_y), jnp.float32),
        scratch_shapes=[pltpu.VMEM((levels * sublanes, part_y), jnp.float32)],
        name="into_levels",
        **parameters(6 * size * levels, size, size),
    )(fields, wide(matrices), *follow)


def edges_kernel(field_ref, _, low_ref, high_ref, first_ref, last_ref):
    sublanes, levels, part_y = field_ref.shape[1:]
    step = pl.program_id(0)
    lane = lax.broadcasted_iota(jnp.int32, (levels, low_ref.shape[2]), 1)
    for c in range(3):
        low = low_ref[c]
        high = high_ref[c]
        for x in range(sublanes):
            here = lane == step * sublanes + x
            low = jnp.where(here, field_ref[c, x, :, 0:1], low)
            high = jnp.where(here, field_ref[c, x, :, part_y - 1 : part_y], high)
        low_ref[c] = low
        high_ref[c] = high

    @pl.when(step == 0)
    def _():
        first_ref[...] = field_ref[:, 0:1]

    @pl.when(step == pl.num_programs(0) - 1)
    def _():
        last_ref[...] = field_ref[:, sublanes - 1 :]


def edges_of(field, follow):
    _, part_x, levels, part_y = field.shape
    sublanes = block_x(part_x)
    size = part_x * levels * part_y
    shapes = [(3, levels, part_x)] * 2 + [(3, 1, levels, part_y)] * 2
    return pl.pallas_call(
        edges_kernel,
        grid=(part_x // sublanes,),
        in_specs=[
            pl.BlockSpec((3, sublanes, levels, part_y), lambda i: (0, i, 0, 0)),
            anywhere,
        ],
        out_specs=[pl.BlockSpec(shapes[0], lambda i: (0, 0, 0))] * 2
        + [pl.BlockSpec(shapes[2], lambda i: (0, 0, 0, 0))] * 2,
        out_shape=[jax.ShapeDtypeStruct(shape, jnp.float32) for shape in shapes],
        name="edges_of",
        **parameters(0, 3 * size, 0),
    )(field, follow)


def section_kernel(*refs):
    field_ref, own_ref, before_ref, after_ref, west_ref, east_ref, south_ref, north_ref = refs[:8]
    coefficient_ref, profile_ref, deriv_ref, matrix_ref = refs[8:12]
    section_ref, laplace_ref, out_ref, rows_ref = refs[-4:]
    sublanes, levels, part_y = field_ref.shape[1:]
    edges = south_ref.shape[2]
    step = pl.program_id(1)
    last = pl.num_programs(1) - 1
    lane = lax.broadcasted_iota(jnp.int32, (levels, part_y), 1)
    profile = step_weight * profile_ref[...]
    for pair in range(0, sublanes, 2):
        own = jnp.concatenate([own_ref[0, pair], own_ref[0, pair + 1]], axis=1)
        slopes = narrow_product(deriv_ref[...], own)
        sections = []
        for x in (pair, pair + 1):
            place = step * sublanes + x
            field = own_ref[0, x]
            if x == 0:
                west = jnp.where(step == 0, west_ref[0, 0], before_ref[0, 0])
            else:
                west = own_ref[0, x - 1]
            if x == sublanes - 1:
                east = jnp.where(step == last, east_ref[0, 0], after_ref[0, 0])
            else:
                east = own_ref[0, x + 1]
            low = pltpu.roll(south_ref[0], lax.rem(edges - place, edges), 1)[:, :part_y]
            high = pltpu.roll(north_ref[0], lax.rem(edges + part_y - 1 - place, edges), 1)
            south = jnp.where(lane == 0, low, pltpu.roll(field, 1, 1))
            north = jnp.where(
                lane == part_y - 1, high[:, :part_y], pltpu.roll(field, part_y - 1, 1)
            )
            laplace = east + west + north + south - 4.0 * field
            slope_z = slopes[:, (x - pair) * part_y : (x - pair + 1) * part_y]
            advect = (0.5 * field_ref[0, x]) * (east - west)
            advect = advect + (0.5 * field_ref[1, x]) * (north - south)
            advect = advect + field_ref[2, x] * slope_z
            viscosity = profile * coefficient_ref[x]
            section = field + (viscosity * laplace - step_weight * advect)
            laplace_ref[0, x] = laplace
            section_ref[0, x] = section
            sections.append(section)
        turned = narrow_product(matrix_ref[0], jnp.concatenate(sections, axis=1))
        for x in (pair, pair + 1):
            rows_ref[pl.ds(x, levels, stride=sublanes), :] = turned[
                :, (x - pair) * part_y : (x - pair + 1) * part_y
            ]
    out_ref[...] = rows_ref[...].reshape(out_ref.shape)


def make_section(
    field, sides, edges, coefficient, profile, deriv, matrices, groups, components, done, follow
):
    _, part_x, levels, part_y = field.shape
    sublanes = block_x(part_x)
    per = levels // groups
    count = len(components)
    first, step = components[0], (components[1] - components[0] if count > 1 else 1)
    size = count * part_x * levels * part_y
    whole = pl.BlockSpec((3, sublanes, levels, part_y), lambda f, i: (0, i, 0, 0))
    own = pl.BlockSpec((1, sublanes, levels, part_y), lambda f, i: (first + f * step, i, 0, 0))
    plane = (1, 1, levels, part_y)
    fixed = pl.BlockSpec(plane, lambda f, i: (first + f * step, 0, 0, 0))
    edge = pl.BlockSpec((1, *edges[0].shape[1:]), lambda f, i: (first + f * step, 0, 0))
    full = jax.ShapeDtypeStruct(field.shape, jnp.float32)
    return pl.pallas_call(
        section_kernel,
        grid=(count, part_x // sublanes),
        in_specs=[
            whole,
            own,
            pl.BlockSpec(
                plane, lambda f, i: (first + f * step, jnp.maximum(i * sublanes - 1, 0), 0, 0)
            ),
            pl.BlockSpec(
                plane,
                lambda f, i: (
                    first + f * step,
                    jnp.minimum((i + 1) * sublanes, part_x - 1),
                    0,
                    0,
                ),
            ),
            fixed,
            fixed,
            edge,
            edge,
            pl.BlockSpec((sublanes, levels, part_y), lambda f, i: (i, 0, 0)),
            pl.BlockSpec((levels, part_y), lambda f, i: (0, 0)),
            pl.BlockSpec((levels, 3 * levels), lambda f, i: (0, 0)),
            pl.BlockSpec((1, levels, 3 * levels), lambda f, i: (f, 0, 0)),
        ]
        + [anywhere] * (len(done) + len(follow)),
        out_specs=[
            own,
            own,
            pl.BlockSpec((groups, 1, per, sublanes, part_y), lambda f, i: (0, f, 0, i, 0)),
        ],
        out_shape=[
            full,
            full,
            jax.ShapeDtypeStruct((groups, count, per, part_x, part_y), jnp.float32),
        ],
        input_output_aliases={12 + i: i for i in range(len(done))},
        scratch_shapes=[pltpu.VMEM((levels * sublanes, part_y), jnp.float32)],
        name="make_section",
        **parameters(12 * size * levels, 6 * size, 3 * size),
    )(
        field,
        field,
        field,
        field,
        *sides,
        *edges,
        coefficient,
        profile,
        wide(deriv),
        wide(matrices),
        *done,
        *follow,
    )


def x_kernel(me_ref, rows_ref, table_ref, *refs):
    targets = table_ref.shape[1]
    out_refs = refs[-targets:]
    groups, count, block, part_x, part_y = rows_ref.shape
    columns = []
    for m in range(block):
        lines = [rows_ref[:, f, m].reshape(groups * part_x, part_y) for f in range(count)]
        columns.append(jnp.concatenate(lines, axis=0))
    data = split(jnp.concatenate(columns, axis=1))
    for s, out_ref in enumerate(out_refs):
        target = lax.rem(me_ref[0] + s, targets)
        spectrum = product((table_ref[0, target], table_ref[1, target]), data)
        for m in range(block):
            out_ref[m] = spectrum[:, m * part_y : (m + 1) * part_y]


def block_of(levels):
    return 2 if levels % 2 == 0 else 1


def x_forward(me, rows, table, *follow):
    groups, count, levels, part_x, part_y = rows.shape
    targets, lines, depth = table.shape[1:]
    block = block_of(levels)
    size = groups * count * levels * part_x * part_y
    return pl.pallas_call(
        x_kernel,
        grid=(levels // block,),
        in_specs=[
            scalars,
            pl.BlockSpec((groups, count, block, part_x, part_y), lambda i: (0, 0, i, 0, 0)),
            pl.BlockSpec(table.shape, lambda i: (0, 0, 0, 0)),
        ]
        + [anywhere] * len(follow),
        out_specs=[pl.BlockSpec((block, lines, part_y), lambda i: (i, 0, 0))] * targets,
        out_shape=[jax.ShapeDtypeStruct((levels, lines, part_y), jnp.float32)] * targets,
        name="x_forward",
        **parameters(6 * size * targets * lines, size + table.size // 2, size // count),
    )(me, rows, table, *follow)


def solve_kernel(sources, full, group_ref, rates_ref, _, *refs):
    full_x, full_y = full
    in_refs = refs[: 2 * sources]
    forward_ref, inverse_ref = refs[2 * sources : 2 * sources + 2]
    out_refs = refs[2 * sources + 2 :]
    block, lines, part_y = in_refs[0].shape
    me = group_ref[0]
    data = split(
        jnp.concatenate([ref[...].reshape(block * lines, part_y) for ref in in_refs], axis=1)
    )
    origins = [lax.rem(me + sources - s, sources) for s in range(sources)]
    diverg = product(
        data,
        [
            jnp.concatenate([forward_ref[h, p, o] for p in range(2) for o in origins], axis=0)
            for h in range(2)
        ],
    )
    shape = (lines, full_y)
    pairs = lines // 2
    mode_x = me * pairs + lax.broadcasted_iota(jnp.int32, shape, 0) % pairs
    mode_y = lax.broadcasted_iota(jnp.int32, shape, 1) % (full_y // 2)
    wave_x = mode_x.astype(jnp.float32) * (2.0 * math.pi / full_x)
    wave_y = mode_y.astype(jnp.float32) * (2.0 * math.pi / full_y)
    squares = wave_x * wave_x + wave_y * wave_y
    solved = []
    for m in range(block):
        rate = rates_ref[pl.program_id(0) * block + m]
        solved.append(-diverg[m * lines : (m + 1) * lines] / (rate + squares))
    solved = split(jnp.concatenate(solved, axis=0))
    for s, out_ref in enumerate(out_refs):
        place = (s // sources, lax.rem(me + s, sources))
        result = product(solved, (inverse_ref[(0, *place)], inverse_ref[(1, *place)]))
        out_ref[...] = result.reshape(block, lines, part_y)


def y_solve(plain, sloped, rates, group, forward, inverse, full, follow):
    levels, lines, part_y = plain[0].shape
    sources = len(plain)
    block = block_of(levels)
    size = levels * lines * part_y * sources
    targets = 2 * sources
    spec = pl.BlockSpec((block, lines, part_y), lambda i: (i, 0, 0))
    fixed = pl.BlockSpec(forward.shape, lambda i: (0, 0, 0, 0, 0))
    outs = pl.pallas_call(
        functools.partial(solve_kernel, sources, full),
        grid=(levels // block,),
        in_specs=[scalars, scalars, anywhere]
        + [spec] * (2 * sources)
        + [fixed, pl.BlockSpec(inverse.shape, lambda i: (0, 0, 0, 0, 0))],
        out_specs=[spec] * targets,
        out_shape=[jax.ShapeDtypeStruct((levels, lines, part_y), jnp.float32)] * targets,
        name="y_solve",
        **parameters(
            24 * size * full[1], 2 * size + forward.size // 2 + inverse.size // 2, 2 * size
        ),
    )(group, rates, follow, *plain, *sloped, forward, inverse)
    return outs[:sources], outs[sources:]


def x_inverse_kernel(sources, me_ref, _, *refs):
    in_refs = refs[:sources]
    table_ref, out_ref, high_ref, low_ref, rows_ref = refs[sources:]
    _, _, part_x, levels, part_y = out_ref.shape

    @pl.when((pl.program_id(0) == 0) & (pl.program_id(1) == 0))
    def _():
        for m in range(levels):
            high, low = split(jnp.concatenate([ref[m] for ref in in_refs], axis=0))
            high_ref[:, m * part_y : (m + 1) * part_y] = high
            low_ref[:, m * part_y : (m + 1) * part_y] = low

    origins = [lax.rem(me_ref[0] + sources - s, sources) for s in range(sources)]
    table = [
        jnp.concatenate([table_ref[h, 0, o] for o in origins], axis=1) for h in range(2)
    ]
    lines = table[0].shape[0]
    for m in range(levels):
        cut = slice(m * part_y, (m + 1) * part_y)
        rows_ref[pl.ds(m, lines, stride=levels), :] = product(
            table, (high_ref[:, cut], low_ref[:, cut])
        )
    out_ref[...] = rows_ref[...].reshape(out_ref.shape)


def x_inverse(me, pieces, table, groups, follow):
    sources = len(pieces)
    levels, lines, part_y = pieces[0].shape
    count, full_x = table.shape[1], table.shape[3]
    part_x = full_x // groups
    steps = 2 if groups % 2 == 0 else 1
    rows = full_x // steps
    size = levels * full_x * part_y
    return pl.pallas_call(
        functools.partial(x_inverse_kernel, sources),
        grid=(count, steps),
        in_specs=[scalars, anywhere]
        + [pl.BlockSpec((levels, lines, part_y), lambda f, i: (0, 0, 0))] * sources
        + [pl.BlockSpec((2, 1, sources, rows, lines), lambda f, i: (0, f, 0, i, 0))],
        out_specs=pl.BlockSpec(
            (groups // steps, 1, part_x, levels, part_y), lambda f, i: (i, f, 0, 0, 0)
        ),
        out_shape=jax.ShapeDtypeStruct((groups, count, part_x, levels, part_y), jnp.float32),
        scratch_shapes=[pltpu.VMEM((full_x, levels * part_y), half)] * 2
        + [pltpu.VMEM((rows * levels, part_y), jnp.float32)],
        name="x_inverse",
        **parameters(6 * size * full_x * count, size + table.size // 2, size * count),
    )(me, follow, *pieces, table)


def column(rows_ref, component, x):
    groups = rows_ref.shape[0]
    return jnp.concatenate([rows_ref[g, component, x] for g in range(groups)], axis=0)


def from_kernel(rows_ref, matrix_ref, base_ref, out_ref):
    part_y = base_ref.shape[3]
    for pair in range(0, base_ref.shape[1], 2):
        fields = [column(rows_ref, 0, x) for x in (pair, pair + 1)]
        turned = narrow_product(matrix_ref[0], jnp.concatenate(fields, axis=1))
        out_ref[0, pair] = base_ref[0, pair] + turned[:, :part_y]
        out_ref[0, pair + 1] = base_ref[0, pair + 1] + turned[:, part_y:]


def from_levels(rows, matrices, base, components, in_place):
    groups, count, part_x, per, part_y = rows.shape
    levels = groups * per
    sublanes = block_x(part_x)
    first, step = components[0], (components[1] - components[0] if count > 1 else 1)
    size = count * part_x * levels * part_y
    spec = pl.BlockSpec((1, sublanes, levels, part_y), lambda f, i: (first + f * step, i, 0, 0))
    return pl.pallas_call(
        from_kernel,
        grid=(count, part_x // sublanes),
        in_specs=[
            pl.BlockSpec((groups, 1, sublanes, per, part_y), lambda f, i: (0, f, i, 0, 0)),
            pl.BlockSpec((1, levels, 3 * levels), lambda f, i: (f, 0, 0)),
            spec,
        ],
        out_specs=spec,
        out_shape=jax.ShapeDtypeStruct(base.shape, jnp.float32),
        input_output_aliases={2: 0} if in_place else {},
        name="from_levels",
        **parameters(6 * size * levels, 2 * size, size),
    )(rows, wide(matrices), base)


def gradient_kernel(
    rows_ref, matrix_ref, base_ref, done_ref, laplace_ref, profile_ref, _, out_ref, gradient_ref
):
    profile = step_weight * profile_ref[...]
    part_y = base_ref.shape[3]
    for pair in range(0, base_ref.shape[1], 2):
        fields = [column(rows_ref, 0, x) for x in (pair, pair + 1)]
        turned = narrow_product(matrix_ref[0], jnp.concatenate(fields, axis=1))
        for x in (pair, pair + 1):
            value = base_ref[0, x] + turned[:, (x - pair) * part_y : (x - pair + 1) * part_y]
            first, last = done_ref[0, x], done_ref[2, x]
            out_ref[0, x], out_ref[1, x], out_ref[2, x] = first, value, last
            total = first * laplace_ref[0, x] + value * laplace_ref[1, x]
            gradient_ref[x] = profile * (total + last * laplace_ref[2, x])


def gradient_of(rows, matrix, base, done, laplace, profile, follow):
    groups, _, part_x, per, part_y = rows.shape
    levels = groups * per
    sublanes = block_x(part_x)
    size = part_x * levels * part_y

    whole = pl.BlockSpec((3, sublanes, levels, part_y), lambda i: (0, i, 0, 0))
    return pl.pallas_call(
        gradient_kernel,
        grid=(part_x // sublanes,),
        in_specs=[
            pl.BlockSpec((groups, 1, sublanes, per, part_y), lambda i: (0, 0, i, 0, 0)),
            pl.BlockSpec((1, levels, 3 * levels), lambda i: (0, 0, 0)),
            pl.BlockSpec((1, sublanes, levels, part_y), lambda i: (1, i, 0, 0)),
            whole,
            whole,
            pl.BlockSpec((levels, part_y), lambda i: (0, 0)),
            anywhere,
        ],
        out_specs=[whole, pl.BlockSpec((sublanes, levels, part_y), lambda i: (i, 0, 0))],
        out_shape=[
            jax.ShapeDtypeStruct(base.shape, jnp.float32),
            jax.ShapeDtypeStruct(base.shape[1:], jnp.float32),
        ],
        input_output_aliases={3: 0},
        name="gradient_of",
        **parameters(6 * size * levels, 7 * size, 2 * size),
    )(rows, wide(matrix[None]), base, done, laplace, profile, follow)


def shifted(cells, axis, shift):
    count = lax.axis_size(axis)
    return lax.ppermute(cells, axis, [(i, (i + shift) % count) for i in range(count)])


def swap_x(rows):
    return lax.all_to_all(rows, "gx", split_axis=0, concat_axis=0, tiled=True)


def gate_kernel(*refs):
    del refs


def gate(pieces, before, weight=0):
    count = len(pieces)
    return pl.pallas_call(
        gate_kernel,
        in_specs=[anywhere] * (count + len(before)),
        out_specs=[anywhere] * count,
        out_shape=[jax.ShapeDtypeStruct(p.shape, p.dtype) for p in pieces],
        input_output_aliases={i: i for i in range(count)},
        cost_estimate=pl.CostEstimate(
            flops=0, bytes_accessed=weight * pieces[0].size, transcendentals=0
        ),
        name="gate",
    )(*pieces, *before)


def swap_y(pieces, before, weight=0):
    own, *sent = pieces
    if before:
        sent = gate(sent, before, weight)
    return [own] + [shifted(piece, "gy", s) for s, piece in enumerate(sent, 1)]


def matmul(a, b):
    return jnp.dot(a, b, precision=precise)


def body(
    velocity,
    cotangent,
    coefficient,
    level_profile,
    vert_deriv,
    eigen_vectors,
    eigen_inverse,
    eigen_rates,
):
    count_x = lax.axis_size("gx")
    count_y = lax.axis_size("gy")
    full_x = count_x * velocity.shape[1]
    full_y = count_y * velocity.shape[3]
    per = velocity.shape[2] // count_x
    me = lax.axis_index("gy").astype(jnp.int32).reshape(1)
    rates = lax.dynamic_slice_in_dim(eigen_rates, lax.axis_index("gx") * per, per)

    forward, forward_slope, inverse, inverse_slope = line_transform(full_x)
    plain_x = grouped(forward, count_y)
    joint_x = np.concatenate([grouped(forward_slope, count_y), plain_x], axis=2)
    table_plain, table_joint = halves(plain_x), halves(joint_x)

    def columns(*tables):
        turned = [np.swapaxes(grouped(table, count_y), 1, 2) for table in tables]
        return halves(np.stack(turned))

    back_plain, back_joint = columns(inverse), columns(inverse_slope, inverse)

    forward, forward_slope, inverse, inverse_slope = line_transform(full_y)

    def points(table):
        return table.reshape(full_y, count_y, full_y // count_y).transpose(1, 2, 0)

    y_forward = halves(np.stack([points(forward), points(forward_slope)]))
    y_inverse = halves(
        np.stack([np.swapaxes(points(table), 1, 2) for table in (inverse, inverse_slope)])
    )

    vectors_t = eigen_vectors.T
    inverse_t = eigen_inverse.T
    deriv_t = vert_deriv.T

    profile = jnp.broadcast_to(level_profile[:, None], velocity.shape[2:])

    a_one = into_levels(cotangent, -vectors_t[None], (1,), count_x)
    last = matmul(vectors_t, deriv_t)
    a_two = into_levels(cotangent, jnp.stack([-vectors_t, last]), (0, 2), count_x, a_one)
    low, high, first, final = edges_of(velocity, a_one)
    sides = (shifted(final, "gx", 1), shifted(first, "gx", -1))
    lanes = -(-velocity.shape[1] // 128) * 128
    edges = [
        jnp.pad(edge, ((0, 0), (0, 0), (0, lanes - edge.shape[2])))
        for edge in (shifted(high, "gy", 1), shifted(low, "gy", -1))
    ]
    a_one = swap_x(a_one)
    a_sloped = x_forward(me, a_one, table_plain, *sides, *edges)
    a_two = swap_x(*gate([a_two], [a_one]))
    last = matmul(eigen_inverse, vert_deriv)
    common = (velocity, sides, edges, coefficient, profile, vert_deriv)
    section, laplace, f_one = make_section(
        *common, eigen_inverse[None], count_x, (1,), (), (a_sloped[0],)
    )
    section, laplace, f_two = make_section(
        *common, jnp.stack([eigen_inverse, last]), count_x, (0, 2), (section, laplace), ()
    )
    a_sloped = swap_y(a_sloped, ())
    a_plain = x_forward(me, a_two, table_joint, f_two)
    f_one = swap_x(*gate([f_one], [a_plain[0], *a_sloped]))
    a_plain = swap_y(a_plain, a_sloped)
    f_sloped = x_forward(me, f_one, table_plain, *a_sloped)
    f_two = swap_x(*gate([f_two], [f_sloped[0]]))
    f_sloped = swap_y(f_sloped, a_plain)
    def solve(plain, sloped, follow):
        full = (full_x, full_y)
        return y_solve(plain, sloped, rates, me, y_forward, y_inverse, full, follow)

    a_flat, a_bent = solve(a_plain, a_sloped, f_sloped[0])
    a_flat = swap_y(a_flat, f_sloped)
    f_plain = x_forward(me, f_two, table_joint, *f_sloped)
    f_plain = swap_y(f_plain, a_flat)
    a_two = x_inverse(me, a_flat, back_joint, count_x, f_plain[0])
    a_bent = swap_y(a_bent, (*f_plain, a_two))
    a_two = swap_x(a_two)
    f_flat, f_bent = solve(f_plain, f_sloped, a_bent[0])
    f_flat = swap_y(f_flat, a_bent)
    a_one = x_inverse(me, a_bent, back_plain, count_x, f_flat[0])
    last = -matmul(deriv_t, inverse_t)
    adjoint = from_levels(a_two, jnp.stack([inverse_t, last]), cotangent, (0, 2), False)
    f_bent = swap_y(f_bent, (*f_flat, adjoint))
    a_one = swap_x(*gate([a_one], [a_two]))
    f_two = x_inverse(me, f_flat, back_joint, count_x, a_one)
    f_one = x_inverse(me, f_bent, back_plain, count_x, f_two)
    f_two = swap_x(f_two)
    f_one = swap_x(*gate([f_one], [f_two]))

    adjoint_velocity, gradient = gradient_of(
        a_one, inverse_t, cotangent, adjoint, laplace, profile, f_bent[1]
    )
    last = -matmul(vert_deriv, eigen_vectors)
    new_velocity = from_levels(
        f_two, jnp.stack([-eigen_vectors, last]), section, (0, 2), True
    )
    new_velocity = from_levels(f_one, -eigen_vectors[None], new_velocity, (1,), True)
    return (new_velocity, adjoint_velocity, gradient)


def solution(mesh):
    in_specs = (
        P(None, "gx", None, "gy"),
        P(None, "gx", None, "gy"),
        P("gx", None, "gy"),
        P(),
        P(),
        P(),
        P(),
        P(),
    )
    out_specs = (P(None, "gx", None, "gy"), P(None, "gx", None, "gy"), P("gx", None, "gy"))
    return jax.shard_map(body, mesh=mesh, in_specs=in_specs, out_specs=out_specs, check_vma=False)
```

time: 1790 us -> 503 us (0.28)
  waiting for transfers between devices: 926 us -> 181 us
  matrix products: 452 us -> 0.71 us
  local copies, waits for them, and re-layouts: 269 us -> 10 us
  Pallas kernels: 0 us -> 166 us
  starting transfers between devices: 53.9 us -> 137 us
  other arithmetic: 73.1 us -> 6.47 us
    all_to_all x8, waiting for transfers between devices: 863 us -> 70.7 us  [swap_x(): return lax.all_to_all(rows, 'gx', split_axis=0, concat_axis=0, tiled=True)]
    dot_general x41 -> x4, matrix products: 452 us -> 0.71 us  [matmul(): return jnp.dot(a, b, precision=precise)]
    pallas_call x0 -> x31, Pallas kernels: none -> 166 us  [the longest x4 37.3 us: x_inverse(): pl.pallas_call(functools.partial(x_inverse_kernel, sources), grid=(count,...]
    all_to_all x10 -> x0, local copies, waits for them, and re-layouts: 103 us -> none  [the longest x4 63.3 us: spectral(): lax.all_to_all(jnp.stack(pieces), 'gy', split_axis=1, concat_axis=3, tile...]
    ppermute x4 -> x28, starting transfers between devices: 7.83 us -> 102 us  [shifted(): lax.ppermute(cells, axis, [(i, (i + shift) % count) for i in range(count)])]
    another operation x6 -> x0, local copies, waits for them, and re-layouts: 50.1 us -> none  [the longest x4 36.6 us: spectral(): jnp.stack(pieces)]
    ppermute x4 -> x28, waiting for transfers between devices: 63.1 us -> 110 us  [shifted(): lax.ppermute(cells, axis, [(i, (i + shift) % count) for i in range(count)])]
    slice x8 -> x0, local copies, waits for them, and re-layouts: 43.9 us -> none  [the longest x2 17.9 us: spectral(): ret_imag = returned[total:]]
  transfers between devices with their start and end apart: 12 -> 36, of which waited for: 8 -> 13; matrix products, arithmetic and copies ran while one was open for 29% -> 2% of each run, Pallas kernels for 0% -> 31%
where the time goes in v1:
time: 503 us; the launch traced here: 501 us
  waiting for transfers between devices  181 us (36%)
  Pallas kernels  166 us (33%)
  starting transfers between devices  137 us (27%)
  local copies, waits for them, and re-layouts  10 us (2%)
  other arithmetic  6.47 us (1%)
    ppermute x28, waiting for transfers between devices, shifted(): lax.ppermute(cells, axis, [(i, (i + shift) % count) for i in range(count)])  110 us
    ppermute x28, starting transfers between devices, shifted(): lax.ppermute(cells, axis, [(i, (i + shift) % count) for i in range(count)])  102 us
    all_to_all x8, waiting for transfers between devices, swap_x(): return lax.all_to_all(rows, 'gx', split_axis=0, concat_axis=0, tiled=True)  70.7 us
    pallas_call x4, Pallas kernels, x_inverse(): pl.pallas_call(functools.partial(x_inverse_kernel, sources), grid=(count,...  37.3 us
    all_to_all x8, starting transfers between devices, swap_x(): return lax.all_to_all(rows, 'gx', split_axis=0, concat_axis=0, tiled=True)  34.6 us
    pallas_call x2, Pallas kernels, y_solve(): pl.pallas_call(functools.partial(solve_kernel, sources, full), grid=(leve...  29.3 us
    pallas_call x2, Pallas kernels, make_section(): pl.pallas_call(section_kernel, grid=(count, part_x // sublanes), in_specs...  25.4 us
    pallas_call x4, Pallas kernels, x_forward(): pl.pallas_call(x_kernel, grid=(levels // block,), in_specs=[scalars, pl.B...  24.2 us
  transfers between devices with their start and end apart: 36, of which 13 were waited for; matrix products, arithmetic and copies ran while one was open for 2% of the time, Pallas kernels for 31%

profile of v1, /device:TPU:0, one launch (start us, length us, event | category | flops | bytes accessed | tf_op | source)
XLA Modules:
  0.0 501.1 jit_solution(633632910858138183)
XLA Ops:
  2.1 4.4 into_levels.2._.refs_0_
  6.5 5.2 %all-to-all-start = ((f32[8,1,8,64,128]{4,3,2,1,0:T(8,128)}), f32[8,1,8,64,128]{4,3,2,1,0:T(8,128)S(1)}, u32[]{:S(2)}, u32[]{:S(2)}) async-start(f32[8,1,8,64,128]{4,3,2,1,0:T(8,128)} %into_levels.2._.refs_0_), calls=%async_computation | async-start | bytes 4194304 | tf_op jit(solution)/shard_map/all_to_all | solution.py:535
  11.7 6.8 %edges_of.1 = (f32[3,64,64]{2,1,0:T(8,128)}, f32[3,64,64]{2,1,0:T(8,128)}, f32[3,1,64,128]{3,2,1,0:T(8,128)}, f32[3,1,64,128]{3,2,1,0:T(8,128)}) custom-call(f32[3,64,64,128]{3,2,1,0:T(8,128)} %refs_3_.3, f32[8,1,8,64,128]{4,3,2,1,0:T(8,128)} %into_levels.2._.refs_0_), custom_call_target="tpu_custom_call" | custom-call | bytes 629145600 | tf_op jit(solution)/shard_map/edges_of/pallas_call | solution.py:158
  22.4 2.6 collective-permute-start.1
  26.6 7.7 %into_levels.3.refs_0_ = f32[8,2,8,64,128]{4,3,2,1,0:T(8,128)} custom-call(f32[3,64,64,128]{3,2,1,0:T(8,128)} %base_ref.3, bf16[2,64,192]{2,1,0:T(8,128)(2,1)} %copy.50.matrix_ref, f32[8,1,8,64,128]{4,3,2,1,0:T(8,128)} %into_levels.2._.refs_0_), custom_call_target="tpu_custom_call" | custom-call | flops 40265318400 | bytes 838860800 | tf_op jit(solution)/shard_map/into_levels/pallas_call | solution.py:112
  40.1 4.6 all-to-all-start.1
  45.4 5.1 %x_forward.4 = (f32[8,128,128]{2,1,0:T(8,128)}, f32[8,128,128]{2,1,0:T(8,128)}, f32[8,128,128]{2,1,0:T(8,128)}, f32[8,128,128]{2,1,0:T(8,128)}) custom-call(s32[1]{0:T(128)} %bitcast.me_ref.group_ref, f32[8,1,8,64,128]{4,3,2,1,0:T(8,128)} %copy-done, bf16[2,4,128,512]{3,2,1,0:T(8,128)(2,1)} %constant.29.clone.table_ref, f32[3,1,64,128]{3,2,1,0:T(8,128)} %copy-done.14, ...), custom_call_target="tpu_custom_call" | custom-call | flops 161061273600 | bytes 524288000 | tf_op jit(solution)/shard_map/x_forward/pallas_call | solution.py:320
  52.1 2.6 collective-permute-start.5
  56.7 9.1 %make_section.2 = (f32[3,64,64,128]{3,2,1,0:T(8,128)}, f32[3,64,64,128]{3,2,1,0:T(8,128)}, f32[8,1,8,64,128]{4,3,2,1,0:T(8,128)}) custom-call(f32[3,64,64,128]{3,2,1,0:T(8,128)} %refs_3_.3, f32[3,64,64,128]{3,2,1,0:T(8,128)} %refs_3_.3, f32[3,64,64,128]{3,2,1,0:T(8,128)} %refs_3_.3, f32[3,64,64,128]{3,2,1,0:T(8,128)} %refs_3_.3, ...), custom_call_target="tpu_custom_call" | custom-call | flops 40265318400 | bytes 1887436800 | tf_op jit(solution)/shard_map/make_section/pallas_call | solution.py:237
  65.8 16.3 %make_section.3 = (f32[3,64,64,128]{3,2,1,0:T(8,128)}, f32[3,64,64,128]{3,2,1,0:T(8,128)}, f32[8,2,8,64,128]{4,3,2,1,0:T(8,128)}) custom-call(f32[3,64,64,128]{3,2,1,0:T(8,128)} %refs_3_.3, f32[3,64,64,128]{3,2,1,0:T(8,128)} %refs_3_.3, f32[3,64,64,128]{3,2,1,0:T(8,128)} %refs_3_.3, ...), custom_call_target="tpu_custom_call", output_to_operand_aliasing={{0}: (12, {}), {1}: (13, {})} | custom-call | flops 80530636800 | bytes 3774873600 | tf_op jit(solution)/shard_map/make_section/pallas_call | solution.py:237
  82.1 11.8 %all-to-all-done.1.rows_ref = f32[8,2,8,64,128]{4,3,2,1,0:T(8,128)} async-done(((f32[8,2,8,64,128]{4,3,2,1,0:T(8,128)}), f32[8,2,8,64,128]{4,3,2,1,0:T(8,128)}, u32[]{:S(2)}, u32[]{:S(2)}) %all-to-all-start.1) | async-done | bytes 4194336 | tf_op jit(solution)/shard_map/all_to_all | solution.py:535
  93.8 7.0 %x_forward.5 = (f32[8,128,128]{2,1,0:T(8,128)}, f32[8,128,128]{2,1,0:T(8,128)}, f32[8,128,128]{2,1,0:T(8,128)}, f32[8,128,128]{2,1,0:T(8,128)}) custom-call(s32[1]{0:T(128)} %bitcast.me_ref.group_ref, f32[8,2,8,64,128]{4,3,2,1,0:T(8,128)} %all-to-all-done.1.rows_ref, bf16[2,4,128,1024]{3,2,1,0:T(8,128)(2,1)} %constant.30.clone.table_ref, ...), custom_call_target="tpu_custom_call" | custom-call | flops 322122547200 | bytes 838860800 | tf_op jit(solution)/shard_map/x_forward/pallas_call | solution.py:320
  101.0 3.7 all-to-all-start.2
  110.3 2.6 collective-permute-start.8
  114.3 17.1 %all-to-all-done.2.rows_ref = f32[8,1,8,64,128]{4,3,2,1,0:T(8,128)S(1)} async-done(((f32[8,1,8,64,128]{4,3,2,1,0:T(8,128)}), f32[8,1,8,64,128]{4,3,2,1,0:T(8,128)S(1)}, u32[]{:S(2)}, u32[]{:S(2)}) %all-to-all-start.2) | async-done | bytes 2097184 | tf_op jit(solution)/shard_map/all_to_all | solution.py:535
  132.6 5.1 %x_forward.6 = (f32[8,128,128]{2,1,0:T(8,128)}, f32[8,128,128]{2,1,0:T(8,128)}, f32[8,128,128]{2,1,0:T(8,128)}, f32[8,128,128]{2,1,0:T(8,128)}) custom-call(s32[1]{0:T(128)} %bitcast.me_ref.group_ref, f32[8,1,8,64,128]{4,3,2,1,0:T(8,128)} %copy-done.1, bf16[2,4,128,512]{3,2,1,0:T(8,128)(2,1)} %constant.29.clone.table_ref, ...), custom_call_target="tpu_custom_call" | custom-call | flops 161061273600 | bytes 524288000 | tf_op jit(solution)/shard_map/x_forward/pallas_call | solution.py:320
  137.7 10.0 %collective-permute-done.8.refs_2_.refs_5_ = f32[8,128,128]{2,1,0:T(8,128)} collective-permute-done((f32[8,128,128]{2,1,0:T(8,128)}, f32[8,128,128]{2,1,0:T(8,128)}, u32[]{:S(2)}, u32[]{:S(2)}) %collective-permute-start.8) | collective-permute-done | bytes 524320 | tf_op jit(solution)/shard_map/ppermute | solution.py:531
  147.7 11.7 %collective-permute-start.10 = (f32[8,128,128]{2,1,0:T(8,128)}, f32[8,128,128]{2,1,0:T(8,128)}, u32[]{:S(2)}, u32[]{:S(2)}) collective-permute-start(f32[8,128,128]{2,1,0:T(8,128)} %get-tuple-element.92), channel_id=1, source_target_pairs={{0,1},{1,2},{2,3},{3,0},{4,5},{5,6},{6,7},{7,4},{8,9},{9,10},{10,1... | collective-permute-start | bytes 1572872 | tf_op jit(solution)/shard_map/ppermute | solution.py:531
  161.8 4.6 all-to-all-start.3
  166.4 14.7 %y_solve.2 = (f32[8,128,128]{2,1,0:T(8,128)}, f32[8,128,128]{2,1,0:T(8,128)}, f32[8,128,128]{2,1,0:T(8,128)}, f32[8,128,128]{2,1,0:T(8,128)}, f32[8,128,128]{2,1...) custom-call(s32[1]{0:T(128)} %bitcast.me_ref.group_ref, ...), custom_call_target="tpu_custom_call" | custom-call | flops 644245094400 | bytes 1258291200 | tf_op jit(solution)/shard_map/y_solve/pallas_call | solution.py:380
  181.1 14.1 %collective-permute-done.11.refs_2_.refs_5_.refs_6_ = f32[8,128,128]{2,1,0:T(8,128)} collective-permute-done((f32[8,128,128]{2,1,0:T(8,128)}, f32[8,128,128]{2,1,0:T(8,128)}, u32[]{:S(2)}, u32[]{:S(2)}) %collective-permute-start.11) | collective-permute-done | bytes 524320 | tf_op jit(solution)/shard_map/ppermute | solution.py:531
  195.2 11.7 %collective-permute-start.13 = (f32[8,128,128]{2,1,0:T(8,128)}, f32[8,128,128]{2,1,0:T(8,128)}, u32[]{:S(2)}, u32[]{:S(2)}) collective-permute-start(f32[8,128,128]{2,1,0:T(8,128)} %get-tuple-element.103), channel_id=1, source_target_pairs={{0,1},{1,2},{2,3},{3,0},{4,5},{5,6},{6,7},{7,4},{8,9},{9,10},{10,1... | collective-permute-start | bytes 1572872 | tf_op jit(solution)/shard_map/ppermute | solution.py:531
  209.2 6.3 %all-to-all-done.3.rows_ref = f32[8,2,8,64,128]{4,3,2,1,0:T(8,128)} async-done(((f32[8,2,8,64,128]{4,3,2,1,0:T(8,128)}), f32[8,2,8,64,128]{4,3,2,1,0:T(8,128)}, u32[]{:S(2)}, u32[]{:S(2)}) %all-to-all-start.3) | async-done | bytes 4194336 | tf_op jit(solution)/shard_map/all_to_all | solution.py:535
  215.5 7.1 %x_forward.7 = (f32[8,128,128]{2,1,0:T(8,128)}, f32[8,128,128]{2,1,0:T(8,128)}, f32[8,128,128]{2,1,0:T(8,128)}, f32[8,128,128]{2,1,0:T(8,128)}) custom-call(s32[1]{0:T(128)} %bitcast.me_ref.group_ref, f32[8,2,8,64,128]{4,3,2,1,0:T(8,128)} %all-to-all-done.3.rows_ref, bf16[2,4,128,1024]{3,2,1,0:T(8,128)(2,1)} %constant.30.clone.table_ref, ...), custom_call_target="tpu_custom_call" | custom-call | flops 322122547200 | bytes 838860800 | tf_op jit(solution)/shard_map/x_forward/pallas_call | solution.py:320
  222.6 19.9 %collective-permute-done.14.refs_5_.refs_2_ = f32[8,128,128]{2,1,0:T(8,128)} collective-permute-done((f32[8,128,128]{2,1,0:T(8,128)}, f32[8,128,128]{2,1,0:T(8,128)}, u32[]{:S(2)}, u32[]{:S(2)}) %collective-permute-start.14) | collective-permute-done | bytes 524320 | tf_op jit(solution)/shard_map/ppermute | solution.py:531
  242.5 11.7 %collective-permute-start.16 = (f32[8,128,128]{2,1,0:T(8,128)}, f32[8,128,128]{2,1,0:T(8,128)}, u32[]{:S(2)}, u32[]{:S(2)}) collective-permute-start(f32[8,128,128]{2,1,0:T(8,128)} %get-tuple-element.106), channel_id=1, source_target_pairs={{0,1},{1,2},{2,3},{3,0},{4,5},{5,6},{6,7},{7,4},{8,9},{9,10},{10,1... | collective-permute-start | bytes 1572872 | tf_op jit(solution)/shard_map/ppermute | solution.py:531
  256.6 11.3 %x_inverse.4.refs_7_ = f32[8,2,64,8,128]{4,3,2,1,0:T(8,128)} custom-call(s32[1]{0:T(128)} %bitcast.me_ref.group_ref, f32[8,128,128]{2,1,0:T(8,128)} %get-tuple-element.95.refs_0_._.refs_3_, f32[8,128,128]{2,1,0:T(8,128)} %get-tuple-element.99.refs_3_.refs_0_, f32[8,128,128]{2,1,0:T(8,128)} %collective-permute-done.13.refs_4_.refs_1_, ...), custom_call_target="tpu_custom_call" | custom-call | flops 322122547200 | bytes 838860800 | tf_op jit(solution)/shard_map/x_inverse/pallas_call | solution.py:429
  267.9 4.5 all-to-all-start.4
  272.5 17.4 %collective-permute-done.17.refs_2_.refs_5_ = f32[8,128,128]{2,1,0:T(8,128)} collective-permute-done((f32[8,128,128]{2,1,0:T(8,128)}, f32[8,128,128]{2,1,0:T(8,128)}, u32[]{:S(2)}, u32[]{:S(2)}) %collective-permute-start.17) | collective-permute-done | bytes 524320 | tf_op jit(solution)/shard_map/ppermute | solution.py:531
  289.9 11.7 %collective-permute-start.19 = (f32[8,128,128]{2,1,0:T(8,128)}, f32[8,128,128]{2,1,0:T(8,128)}, u32[]{:S(2)}, u32[]{:S(2)}) collective-permute-start(f32[8,128,128]{2,1,0:T(8,128)} %get-tuple-element.113), channel_id=1, source_target_pairs={{0,1},{1,2},{2,3},{3,0},{4,5},{5,6},{6,7},{7,4},{8,9},{9,10},{10,1... | collective-permute-start | bytes 1572872 | tf_op jit(solution)/shard_map/ppermute | solution.py:531
  303.9 14.6 %y_solve.3 = (f32[8,128,128]{2,1,0:T(8,128)}, f32[8,128,128]{2,1,0:T(8,128)}, f32[8,128,128]{2,1,0:T(8,128)}, f32[8,128,128]{2,1,0:T(8,128)}, f32[8,128,128]{2,1...) custom-call(s32[1]{0:T(128)} %bitcast.me_ref.group_ref, ...), custom_call_target="tpu_custom_call" | custom-call | flops 644245094400 | bytes 1258291200 | tf_op jit(solution)/shard_map/y_solve/pallas_call | solution.py:380
  318.6 18.6 %collective-permute-done.20.refs_2_.refs_5_ = f32[8,128,128]{2,1,0:T(8,128)} collective-permute-done((f32[8,128,128]{2,1,0:T(8,128)}, f32[8,128,128]{2,1,0:T(8,128)}, u32[]{:S(2)}, u32[]{:S(2)}) %collective-permute-start.20) | collective-permute-done | bytes 524320 | tf_op jit(solution)/shard_map/ppermute | solution.py:531
  337.2 11.7 %collective-permute-start.22 = (f32[8,128,128]{2,1,0:T(8,128)}, f32[8,128,128]{2,1,0:T(8,128)}, u32[]{:S(2)}, u32[]{:S(2)}) collective-permute-start(f32[8,128,128]{2,1,0:T(8,128)} %get-tuple-element.119), channel_id=1, source_target_pairs={{0,1},{1,2},{2,3},{3,0},{4,5},{5,6},{6,7},{7,4},{8,9},{9,10},{10,1... | collective-permute-start | bytes 1572872 | tf_op jit(solution)/shard_map/ppermute | solution.py:531
  351.3 7.3 %x_inverse.5.refs_0_ = f32[8,1,64,8,128]{4,3,2,1,0:T(8,128)} custom-call(s32[1]{0:T(128)} %bitcast.me_ref.group_ref, f32[8,128,128]{2,1,0:T(8,128)} %get-tuple-element.109._.refs_0_.refs_3_, f32[8,128,128]{2,1,0:T(8,128)} %get-tuple-element.88._.refs_0_.refs_3_, f32[8,128,128]{2,1,0:T(8,128)} %collective-permute-done.19.refs_1_.refs_4_, ...), custom_call_target="tpu_custom_call" | custom-call | flops 161061273600 | bytes 524288000 | tf_op jit(solution)/shard_map/x_inverse/pallas_call | solution.py:429
  358.5 3.8 all-to-all-start.5
  362.4 8.4 %from_levels.3.refs_7_.done_ref = f32[3,64,64,128]{3,2,1,0:T(8,128)} custom-call(f32[8,2,64,8,128]{4,3,2,1,0:T(8,128)} %all-to-all-done.4.refs_1_.rows_ref, bf16[2,64,192]{2,1,0:T(8,128)(2,1)} %pad_maximum_fusion.5.matrix_ref, f32[3,64,64,128]{3,2,1,0:T(8,128)} %base_ref.3), custom_call_target="tpu_custom_call" | custom-call | flops 40265318400 | bytes 1258291200 | tf_op jit(solution)/shard_map/from_levels/pallas_call | solution.py:467
  370.7 13.8 %collective-permute-done.23.refs_2_.refs_5_ = f32[8,128,128]{2,1,0:T(8,128)} collective-permute-done((f32[8,128,128]{2,1,0:T(8,128)}, f32[8,128,128]{2,1,0:T(8,128)}, u32[]{:S(2)}, u32[]{:S(2)}) %collective-permute-start.23) | collective-permute-done | bytes 524320 | tf_op jit(solution)/shard_map/ppermute | solution.py:531
  384.6 11.7 %collective-permute-start.25 = (f32[8,128,128]{2,1,0:T(8,128)}, f32[8,128,128]{2,1,0:T(8,128)}, u32[]{:S(2)}, u32[]{:S(2)}) collective-permute-start(f32[8,128,128]{2,1,0:T(8,128)} %get-tuple-element.126), channel_id=1, source_target_pairs={{0,1},{1,2},{2,3},{3,0},{4,5},{5,6},{6,7},{7,4},{8,9},{9,10},{10,1... | collective-permute-start | bytes 1572872 | tf_op jit(solution)/shard_map/ppermute | solution.py:531
  400.0 11.4 %x_inverse.6._ = f32[8,2,64,8,128]{4,3,2,1,0:T(8,128)} custom-call(s32[1]{0:T(128)} %bitcast.me_ref.group_ref, f32[8,1,64,8,128]{4,3,2,1,0:T(8,128)} %copy-done.2, f32[8,128,128]{2,1,0:T(8,128)} %get-tuple-element.109._.refs_0_.refs_3_, f32[8,128,128]{2,1,0:T(8,128)} %collective-permute-done.22.refs_1_.refs_4_, ...), custom_call_target="tpu_custom_call" | custom-call | flops 322122547200 | bytes 838860800 | tf_op jit(solution)/shard_map/x_inverse/pallas_call | solution.py:429
  411.3 4.6 all-to-all-start.6
  415.9 16.0 %collective-permute-done.26.refs_2_ = f32[8,128,128]{2,1,0:T(8,128)} collective-permute-done((f32[8,128,128]{2,1,0:T(8,128)}, f32[8,128,128]{2,1,0:T(8,128)}, u32[]{:S(2)}, u32[]{:S(2)}) %collective-permute-start.26) | collective-permute-done | bytes 524320 | tf_op jit(solution)/shard_map/ppermute | solution.py:531
  431.9 7.3 %x_inverse.7.refs_0_ = f32[8,1,64,8,128]{4,3,2,1,0:T(8,128)} custom-call(s32[1]{0:T(128)} %bitcast.me_ref.group_ref, f32[8,2,64,8,128]{4,3,2,1,0:T(8,128)} %x_inverse.6._, f32[8,128,128]{2,1,0:T(8,128)} %get-tuple-element.122.refs_0_, f32[8,128,128]{2,1,0:T(8,128)} %collective-permute-done.25.refs_1_._, f32[8,128,128]{2,1,0:T(8,128)} %collective-permute-done.26.refs_2_, ...), custom_call_target="tpu_custom_call" | custom-call | flops 161061273600 | bytes 524288000 | tf_op jit(solution)/shard_map/x_inverse/pallas_call | solution.py:429
  439.2 9.3 %gradient_of.1 = (f32[3,64,64,128]{3,2,1,0:T(8,128)}, f32[64,64,128]{2,1,0:T(8,128)}) custom-call(f32[8,1,64,8,128]{4,3,2,1,0:T(8,128)} %copy-done.2, bf16[1,64,192]{2,1,0:T(8,128)(2,1)} %pad_maximum_fusion.12.matrix_ref, f32[3,64,64,128]{3,2,1,0:T(8,128)} %base_ref.3, ...), custom_call_target="tpu_custom_call", output_to_operand_aliasing={{0}: (3, {})} | custom-call | flops 20132659200 | bytes 1887436800 | tf_op jit(solution)/shard_map/gradient_of/pallas_call | solution.py:506
  448.5 16.5 %all-to-all-done.6.refs_1_.rows_ref = f32[8,2,64,8,128]{4,3,2,1,0:T(8,128)} async-done(((f32[8,2,64,8,128]{4,3,2,1,0:T(8,128)}), f32[8,2,64,8,128]{4,3,2,1,0:T(8,128)}, u32[]{:S(2)}, u32[]{:S(2)}) %all-to-all-start.6) | async-done | bytes 4194336 | tf_op jit(solution)/shard_map/all_to_all | solution.py:535
  465.0 3.6 all-to-all-start.7
  468.6 8.4 %from_levels.4.base_ref = f32[3,64,64,128]{3,2,1,0:T(8,128)} custom-call(f32[8,2,64,8,128]{4,3,2,1,0:T(8,128)} %all-to-all-done.6.refs_1_.rows_ref, bf16[2,64,192]{2,1,0:T(8,128)(2,1)} %pad_maximum_fusion.7.matrix_ref, f32[3,64,64,128]{3,2,1,0:T(8,128)} %get-tuple-element.129.base_ref), custom_call_target="tpu_custom_call", output_to_operand_aliasing={{}: (2, {})} | custom-call | flops 40265318400 | bytes 1258291200 | tf_op jit(solution)/shard_map/from_levels/pallas_call | solution.py:467
  477.0 18.2 %all-to-all-done.7.rows_ref = f32[8,1,64,8,128]{4,3,2,1,0:T(8,128)S(1)} async-done(((f32[8,1,64,8,128]{4,3,2,1,0:T(8,128)}), f32[8,1,64,8,128]{4,3,2,1,0:T(8,128)S(1)}, u32[]{:S(2)}, u32[]{:S(2)}) %all-to-all-start.7) | async-done | bytes 2097184 | tf_op jit(solution)/shard_map/all_to_all | solution.py:535
  496.5 4.6 from_levels.5
  (118 shorter events, 42.1 us)
Async XLA Ops:
  6.5 32.3 %all-to-all-start = ((f32[8,1,8,64,128]{4,3,2,1,0:T(8,128)}), f32[8,1,8,64,128]{4,3,2,1,0:T(8,128)S(1)}, u32[]{:S(2)}, u32[]{:S(2)}) async-start(f32[8,1,8,64,128]{4,3,2,1,0:T(8,128)} %into_levels.2._.refs_0_), calls=%async_computation | async-start | bytes 4194304 | tf_op jit(solution)/shard_map/all_to_all | solution.py:535
  11.7 13.3 %copy-start.8 = (f32[64,64]{1,0:T(8,128)S(1)}, f32[64,64]{1,0:T(8,128)}, u32[]{:S(2)}) copy-start(f32[64,64]{1,0:T(8,128)} %param.19) | copy-start | bytes 49156
  11.7 13.9 %copy-start.4 = (f32[64,64]{1,0:T(8,128)S(1)}, f32[64,64]{1,0:T(8,128)}, u32[]{:S(2)}) copy-start(f32[64,64]{1,0:T(8,128)} %param.18) | copy-start | bytes 49156
  18.5 18.1 %collective-permute-start.2 = (f32[3,64,64]{2,1,0:T(8,128)}, f32[3,64,64]{2,1,0:T(8,128)S(1)}, u32[]{:S(2)}, u32[]{:S(2)}) collective-permute-start(f32[3,64,64]{2,1,0:T(8,128)} %get-tuple-element.70), channel_id=1, source_target_pairs={{0,1},{1,2},{2,3},{3,0},{4,5},{5,6},{6,7},{7,4},{8,9},{9,10},{10,1... | collective-permute-start | bytes 147464 | tf_op jit(solution)/shard_map/ppermute | solution.py:531
  20.1 17.1 %collective-permute-start.3 = (f32[3,64,64]{2,1,0:T(8,128)}, f32[3,64,64]{2,1,0:T(8,128)S(1)}, u32[]{:S(2)}, u32[]{:S(2)}) collective-permute-start(f32[3,64,64]{2,1,0:T(8,128)} %get-tuple-element.71), channel_id=1, source_target_pairs={{0,3},{1,0},{2,1},{3,2},{4,7},{5,4},{6,5},{7,6},{8,11},{9,8},{10,9... | collective-permute-start | bytes 147464 | tf_op jit(solution)/shard_map/ppermute | solution.py:531
  22.4 22.4 %collective-permute-start = (f32[3,1,64,128]{3,2,1,0:T(8,128)}, f32[3,1,64,128]{3,2,1,0:T(8,128)S(1)}, u32[]{:S(2)}, u32[]{:S(2)}) collective-permute-start(f32[3,1,64,128]{3,2,1,0:T(8,128)} %get-tuple-element.68), channel_id=1, source_target_pairs={{0,4},{4,8},{8,12},{12,16},{16,20},{20,24},{24,28},{28,0},{1,5},{5... | collective-permute-start | bytes 294920 | tf_op jit(solution)/shard_map/ppermute | solution.py:531
  22.4 22.4 %collective-permute-start.1 = (f32[3,1,64,128]{3,2,1,0:T(8,128)}, f32[3,1,64,128]{3,2,1,0:T(8,128)S(1)}, u32[]{:S(2)}, u32[]{:S(2)}) collective-permute-start(f32[3,1,64,128]{3,2,1,0:T(8,128)} %get-tuple-element.69), channel_id=1, source_target_pairs={{0,28},{4,0},{8,4},{12,8},{16,12},{20,16},{24,20},{28,24},{1,29},{... | collective-permute-start | bytes 294920 | tf_op jit(solution)/shard_map/ppermute | solution.py:531
  26.6 8.4 %copy-start.6 = (f32[64,64]{1,0:T(8,128)S(1)}, f32[64,64]{1,0:T(8,128)}, u32[]{:S(2)}) copy-start(f32[64,64]{1,0:T(8,128)} %param.20) | copy-start | bytes 49156
  40.1 53.7 %all-to-all-start.1 = ((f32[8,2,8,64,128]{4,3,2,1,0:T(8,128)}), f32[8,2,8,64,128]{4,3,2,1,0:T(8,128)}, u32[]{:S(2)}, u32[]{:S(2)}) async-start(f32[8,2,8,64,128]{4,3,2,1,0:T(8,128)} %gate.12), calls=%async_computation.1 | async-start | bytes 8388608 | tf_op jit(solution)/shard_map/all_to_all | solution.py:535
  45.4 10.6 %copy-start.13 = (f32[64]{0:T(128)S(1)}, f32[64]{0:T(128)}, u32[]{:S(2)}) copy-start(f32[64]{0:T(128)} %param.17) | copy-start | bytes 772
  50.5 50.4 %collective-permute-start.4 = (f32[8,128,128]{2,1,0:T(8,128)}, f32[8,128,128]{2,1,0:T(8,128)}, u32[]{:S(2)}, u32[]{:S(2)}) collective-permute-start(f32[8,128,128]{2,1,0:T(8,128)} %get-tuple-element.78), channel_id=1, source_target_pairs={{0,1},{1,2},{2,3},{3,0},{4,5},{5,6},{6,7},{7,4},{8,9},{9,10},{10,1... | collective-permute-start | bytes 1572872 | tf_op jit(solution)/shard_map/ppermute | solution.py:531
  52.1 48.8 %collective-permute-start.5 = (f32[8,128,128]{2,1,0:T(8,128)}, f32[8,128,128]{2,1,0:T(8,128)}, u32[]{:S(2)}, u32[]{:S(2)}) collective-permute-start(f32[8,128,128]{2,1,0:T(8,128)} %get-tuple-element.79), channel_id=1, source_target_pairs={{0,2},{1,3},{2,0},{3,1},{4,6},{5,7},{6,4},{7,5},{8,10},{9,11},{10,... | collective-permute-start | bytes 1572872 | tf_op jit(solution)/shard_map/ppermute | solution.py:531
  54.7 46.2 %collective-permute-start.6 = (f32[8,128,128]{2,1,0:T(8,128)}, f32[8,128,128]{2,1,0:T(8,128)}, u32[]{:S(2)}, u32[]{:S(2)}) collective-permute-start(f32[8,128,128]{2,1,0:T(8,128)} %get-tuple-element.80), channel_id=1, source_target_pairs={{0,3},{1,0},{2,1},{3,2},{4,7},{5,4},{6,5},{7,6},{8,11},{9,8},{10,9... | collective-permute-start | bytes 1572872 | tf_op jit(solution)/shard_map/ppermute | solution.py:531
  100.9 3.9 copy-start.7
  100.9 3.9 copy-start.16
  100.9 5.2 %copy-start.11 = (bf16[1,64,64]{2,1,0:T(8,128)(2,1)S(1)}, bf16[1,64,64]{2,1,0:T(8,128)(2,1)}, u32[]{:S(2)}) copy-start(bf16[1,64,64]{2,1,0:T(8,128)(2,1)} %get-tuple-element.144) | copy-start | bytes 24580
  100.9 5.2 %copy-start.12 = (bf16[1,64,64]{2,1,0:T(8,128)(2,1)S(1)}, bf16[1,64,64]{2,1,0:T(8,128)(2,1)}, u32[]{:S(2)}) copy-start(bf16[1,64,64]{2,1,0:T(8,128)(2,1)} %get-tuple-element.145) | copy-start | bytes 24580
  100.9 5.9 %copy-start.5 = (f32[64,64]{1,0:T(8,128)S(1)}, f32[64,64]{1,0:T(8,128)}, u32[]{:S(2)}) copy-start(f32[64,64]{1,0:T(8,128)} %param.18) | copy-start | bytes 49156
  101.0 6.9 %copy-start.9 = (f32[64,64]{1,0:T(8,128)S(1)}, f32[64,64]{1,0:T(8,128)}, u32[]{:S(2)}) copy-start(f32[64,64]{1,0:T(8,128)} %param.19) | copy-start | bytes 49156
  101.0 7.0 %copy-start.10 = (f32[1,64,64]{2,1,0:T(8,128)S(1)}, f32[1,64,64]{2,1,0:T(8,128)}, u32[]{:S(2)}) copy-start(f32[1,64,64]{2,1,0:T(8,128)} %get-tuple-element.143) | copy-start | bytes 49156
  101.0 30.3 %all-to-all-start.2 = ((f32[8,1,8,64,128]{4,3,2,1,0:T(8,128)}), f32[8,1,8,64,128]{4,3,2,1,0:T(8,128)S(1)}, u32[]{:S(2)}, u32[]{:S(2)}) async-start(f32[8,1,8,64,128]{4,3,2,1,0:T(8,128)} %gate.13), calls=%async_computation.2 | async-start | bytes 4194304 | tf_op jit(solution)/shard_map/all_to_all | solution.py:535
  108.8 28.9 %collective-permute-start.7 = (f32[8,128,128]{2,1,0:T(8,128)}, f32[8,128,128]{2,1,0:T(8,128)}, u32[]{:S(2)}, u32[]{:S(2)}) collective-permute-start(f32[8,128,128]{2,1,0:T(8,128)} %get-tuple-element.85), channel_id=1, source_target_pairs={{0,1},{1,2},{2,3},{3,0},{4,5},{5,6},{6,7},{7,4},{8,9},{9,10},{10,1... | collective-permute-start | bytes 1572872 | tf_op jit(solution)/shard_map/ppermute | solution.py:531
  110.3 37.4 %collective-permute-start.8 = (f32[8,128,128]{2,1,0:T(8,128)}, f32[8,128,128]{2,1,0:T(8,128)}, u32[]{:S(2)}, u32[]{:S(2)}) collective-permute-start(f32[8,128,128]{2,1,0:T(8,128)} %get-tuple-element.86), channel_id=1, source_target_pairs={{0,2},{1,3},{2,0},{3,1},{4,6},{5,7},{6,4},{7,5},{8,10},{9,11},{10,... | collective-permute-start | bytes 1572872 | tf_op jit(solution)/shard_map/ppermute | solution.py:531
  112.9 34.8 %collective-permute-start.9 = (f32[8,128,128]{2,1,0:T(8,128)}, f32[8,128,128]{2,1,0:T(8,128)}, u32[]{:S(2)}, u32[]{:S(2)}) collective-permute-start(f32[8,128,128]{2,1,0:T(8,128)} %get-tuple-element.87), channel_id=1, source_target_pairs={{0,3},{1,0},{2,1},{3,2},{4,7},{5,4},{6,5},{7,6},{8,11},{9,8},{10,9... | collective-permute-start | bytes 1572872 | tf_op jit(solution)/shard_map/ppermute | solution.py:531
  147.7 33.3 %collective-permute-start.10 = (f32[8,128,128]{2,1,0:T(8,128)}, f32[8,128,128]{2,1,0:T(8,128)}, u32[]{:S(2)}, u32[]{:S(2)}) collective-permute-start(f32[8,128,128]{2,1,0:T(8,128)} %get-tuple-element.92), channel_id=1, source_target_pairs={{0,1},{1,2},{2,3},{3,0},{4,5},{5,6},{6,7},{7,4},{8,9},{9,10},{10,1... | collective-permute-start | bytes 1572872 | tf_op jit(solution)/shard_map/ppermute | solution.py:531
  159.5 35.7 %collective-permute-start.11 = (f32[8,128,128]{2,1,0:T(8,128)}, f32[8,128,128]{2,1,0:T(8,128)}, u32[]{:S(2)}, u32[]{:S(2)}) collective-permute-start(f32[8,128,128]{2,1,0:T(8,128)} %get-tuple-element.93), channel_id=1, source_target_pairs={{0,2},{1,3},{2,0},{3,1},{4,6},{5,7},{6,4},{7,5},{8,10},{9,11},{10,... | collective-permute-start | bytes 1572872 | tf_op jit(solution)/shard_map/ppermute | solution.py:531
  161.1 34.1 %collective-permute-start.12 = (f32[8,128,128]{2,1,0:T(8,128)}, f32[8,128,128]{2,1,0:T(8,128)}, u32[]{:S(2)}, u32[]{:S(2)}) collective-permute-start(f32[8,128,128]{2,1,0:T(8,128)} %get-tuple-element.94), channel_id=1, source_target_pairs={{0,3},{1,0},{2,1},{3,2},{4,7},{5,4},{6,5},{7,6},{8,11},{9,8},{10,9... | collective-permute-start | bytes 1572872 | tf_op jit(solution)/shard_map/ppermute | solution.py:531
  161.8 53.7 %all-to-all-start.3 = ((f32[8,2,8,64,128]{4,3,2,1,0:T(8,128)}), f32[8,2,8,64,128]{4,3,2,1,0:T(8,128)}, u32[]{:S(2)}, u32[]{:S(2)}) async-start(f32[8,2,8,64,128]{4,3,2,1,0:T(8,128)} %gate.15), calls=%async_computation.3 | async-start | bytes 8388608 | tf_op jit(solution)/shard_map/all_to_all | solution.py:535
  195.2 27.4 %collective-permute-start.13 = (f32[8,128,128]{2,1,0:T(8,128)}, f32[8,128,128]{2,1,0:T(8,128)}, u32[]{:S(2)}, u32[]{:S(2)}) collective-permute-start(f32[8,128,128]{2,1,0:T(8,128)} %get-tuple-element.103), channel_id=1, source_target_pairs={{0,1},{1,2},{2,3},{3,0},{4,5},{5,6},{6,7},{7,4},{8,9},{9,10},{10,1... | collective-permute-start | bytes 1572872 | tf_op jit(solution)/shard_map/ppermute | solution.py:531
  206.9 35.6 %collective-permute-start.14 = (f32[8,128,128]{2,1,0:T(8,128)}, f32[8,128,128]{2,1,0:T(8,128)}, u32[]{:S(2)}, u32[]{:S(2)}) collective-permute-start(f32[8,128,128]{2,1,0:T(8,128)} %get-tuple-element.104), channel_id=1, source_target_pairs={{0,2},{1,3},{2,0},{3,1},{4,6},{5,7},{6,4},{7,5},{8,10},{9,11},{10,... | collective-permute-start | bytes 1572872 | tf_op jit(solution)/shard_map/ppermute | solution.py:531
  208.5 34.0 %collective-permute-start.15 = (f32[8,128,128]{2,1,0:T(8,128)}, f32[8,128,128]{2,1,0:T(8,128)}, u32[]{:S(2)}, u32[]{:S(2)}) collective-permute-start(f32[8,128,128]{2,1,0:T(8,128)} %get-tuple-element.105), channel_id=1, source_target_pairs={{0,3},{1,0},{2,1},{3,2},{4,7},{5,4},{6,5},{7,6},{8,11},{9,8},{10,9... | collective-permute-start | bytes 1572872 | tf_op jit(solution)/shard_map/ppermute | solution.py:531
  242.5 30.0 %collective-permute-start.16 = (f32[8,128,128]{2,1,0:T(8,128)}, f32[8,128,128]{2,1,0:T(8,128)}, u32[]{:S(2)}, u32[]{:S(2)}) collective-permute-start(f32[8,128,128]{2,1,0:T(8,128)} %get-tuple-element.106), channel_id=1, source_target_pairs={{0,1},{1,2},{2,3},{3,0},{4,5},{5,6},{6,7},{7,4},{8,9},{9,10},{10,1... | collective-permute-start | bytes 1572872 | tf_op jit(solution)/shard_map/ppermute | solution.py:531
  254.2 35.7 %collective-permute-start.17 = (f32[8,128,128]{2,1,0:T(8,128)}, f32[8,128,128]{2,1,0:T(8,128)}, u32[]{:S(2)}, u32[]{:S(2)}) collective-permute-start(f32[8,128,128]{2,1,0:T(8,128)} %get-tuple-element.107), channel_id=1, source_target_pairs={{0,2},{1,3},{2,0},{3,1},{4,6},{5,7},{6,4},{7,5},{8,10},{9,11},{10,... | collective-permute-start | bytes 1572872 | tf_op jit(solution)/shard_map/ppermute | solution.py:531
  255.9 33.9 %collective-permute-start.18 = (f32[8,128,128]{2,1,0:T(8,128)}, f32[8,128,128]{2,1,0:T(8,128)}, u32[]{:S(2)}, u32[]{:S(2)}) collective-permute-start(f32[8,128,128]{2,1,0:T(8,128)} %get-tuple-element.108), channel_id=1, source_target_pairs={{0,3},{1,0},{2,1},{3,2},{4,7},{5,4},{6,5},{7,6},{8,11},{9,8},{10,9... | collective-permute-start | bytes 1572872 | tf_op jit(solution)/shard_map/ppermute | solution.py:531
  267.9 90.6 %all-to-all-start.4 = ((f32[8,2,64,8,128]{4,3,2,1,0:T(8,128)}), f32[8,2,64,8,128]{4,3,2,1,0:T(8,128)}, u32[]{:S(2)}, u32[]{:S(2)}) async-start(f32[8,2,64,8,128]{4,3,2,1,0:T(8,128)} %x_inverse.4.refs_7_), calls=%async_computation.4 | async-start | bytes 8388608 | tf_op jit(solution)/shard_map/all_to_all | solution.py:535
  289.9 28.7 %collective-permute-start.19 = (f32[8,128,128]{2,1,0:T(8,128)}, f32[8,128,128]{2,1,0:T(8,128)}, u32[]{:S(2)}, u32[]{:S(2)}) collective-permute-start(f32[8,128,128]{2,1,0:T(8,128)} %get-tuple-element.113), channel_id=1, source_target_pairs={{0,1},{1,2},{2,3},{3,0},{4,5},{5,6},{6,7},{7,4},{8,9},{9,10},{10,1... | collective-permute-start | bytes 1572872 | tf_op jit(solution)/shard_map/ppermute | solution.py:531
  301.6 35.6 %collective-permute-start.20 = (f32[8,128,128]{2,1,0:T(8,128)}, f32[8,128,128]{2,1,0:T(8,128)}, u32[]{:S(2)}, u32[]{:S(2)}) collective-permute-start(f32[8,128,128]{2,1,0:T(8,128)} %get-tuple-element.114), channel_id=1, source_target_pairs={{0,2},{1,3},{2,0},{3,1},{4,6},{5,7},{6,4},{7,5},{8,10},{9,11},{10,... | collective-permute-start | bytes 1572872 | tf_op jit(solution)/shard_map/ppermute | solution.py:531
  303.3 33.9 %collective-permute-start.21 = (f32[8,128,128]{2,1,0:T(8,128)}, f32[8,128,128]{2,1,0:T(8,128)}, u32[]{:S(2)}, u32[]{:S(2)}) collective-permute-start(f32[8,128,128]{2,1,0:T(8,128)} %get-tuple-element.115), channel_id=1, source_target_pairs={{0,3},{1,0},{2,1},{3,2},{4,7},{5,4},{6,5},{7,6},{8,11},{9,8},{10,9... | collective-permute-start | bytes 1572872 | tf_op jit(solution)/shard_map/ppermute | solution.py:531
  337.2 33.5 %collective-permute-start.22 = (f32[8,128,128]{2,1,0:T(8,128)}, f32[8,128,128]{2,1,0:T(8,128)}, u32[]{:S(2)}, u32[]{:S(2)}) collective-permute-start(f32[8,128,128]{2,1,0:T(8,128)} %get-tuple-element.119), channel_id=1, source_target_pairs={{0,1},{1,2},{2,3},{3,0},{4,5},{5,6},{6,7},{7,4},{8,9},{9,10},{10,1... | collective-permute-start | bytes 1572872 | tf_op jit(solution)/shard_map/ppermute | solution.py:531
  348.9 35.7 %collective-permute-start.23 = (f32[8,128,128]{2,1,0:T(8,128)}, f32[8,128,128]{2,1,0:T(8,128)}, u32[]{:S(2)}, u32[]{:S(2)}) collective-permute-start(f32[8,128,128]{2,1,0:T(8,128)} %get-tuple-element.120), channel_id=1, source_target_pairs={{0,2},{1,3},{2,0},{3,1},{4,6},{5,7},{6,4},{7,5},{8,10},{9,11},{10,... | collective-permute-start | bytes 1572872 | tf_op jit(solution)/shard_map/ppermute | solution.py:531
  350.6 33.9 %collective-permute-start.24 = (f32[8,128,128]{2,1,0:T(8,128)}, f32[8,128,128]{2,1,0:T(8,128)}, u32[]{:S(2)}, u32[]{:S(2)}) collective-permute-start(f32[8,128,128]{2,1,0:T(8,128)} %get-tuple-element.121), channel_id=1, source_target_pairs={{0,3},{1,0},{2,1},{3,2},{4,7},{5,4},{6,5},{7,6},{8,11},{9,8},{10,9... | collective-permute-start | bytes 1572872 | tf_op jit(solution)/shard_map/ppermute | solution.py:531
  358.5 40.1 %all-to-all-start.5 = ((f32[8,1,64,8,128]{4,3,2,1,0:T(8,128)}), f32[8,1,64,8,128]{4,3,2,1,0:T(8,128)S(1)}, u32[]{:S(2)}, u32[]{:S(2)}) async-start(f32[8,1,64,8,128]{4,3,2,1,0:T(8,128)} %gate.20), calls=%async_computation.5 | async-start | bytes 4194304 | tf_op jit(solution)/shard_map/all_to_all | solution.py:535
  384.6 31.3 %collective-permute-start.25 = (f32[8,128,128]{2,1,0:T(8,128)}, f32[8,128,128]{2,1,0:T(8,128)}, u32[]{:S(2)}, u32[]{:S(2)}) collective-permute-start(f32[8,128,128]{2,1,0:T(8,128)} %get-tuple-element.126), channel_id=1, source_target_pairs={{0,1},{1,2},{2,3},{3,0},{4,5},{5,6},{6,7},{7,4},{8,9},{9,10},{10,1... | collective-permute-start | bytes 1572872 | tf_op jit(solution)/shard_map/ppermute | solution.py:531
  396.3 35.6 %collective-permute-start.26 = (f32[8,128,128]{2,1,0:T(8,128)}, f32[8,128,128]{2,1,0:T(8,128)}, u32[]{:S(2)}, u32[]{:S(2)}) collective-permute-start(f32[8,128,128]{2,1,0:T(8,128)} %get-tuple-element.127), channel_id=1, source_target_pairs={{0,2},{1,3},{2,0},{3,1},{4,6},{5,7},{6,4},{7,5},{8,10},{9,11},{10,... | collective-permute-start | bytes 1572872 | tf_op jit(solution)/shard_map/ppermute | solution.py:531
  398.0 33.9 %collective-permute-start.27 = (f32[8,128,128]{2,1,0:T(8,128)}, f32[8,128,128]{2,1,0:T(8,128)}, u32[]{:S(2)}, u32[]{:S(2)}) collective-permute-start(f32[8,128,128]{2,1,0:T(8,128)} %get-tuple-element.128), channel_id=1, source_target_pairs={{0,3},{1,0},{2,1},{3,2},{4,7},{5,4},{6,5},{7,6},{8,11},{9,8},{10,9... | collective-permute-start | bytes 1572872 | tf_op jit(solution)/shard_map/ppermute | solution.py:531
  398.6 1.3 copy-start.2
  411.3 53.7 %all-to-all-start.6 = ((f32[8,2,64,8,128]{4,3,2,1,0:T(8,128)}), f32[8,2,64,8,128]{4,3,2,1,0:T(8,128)}, u32[]{:S(2)}, u32[]{:S(2)}) async-start(f32[8,2,64,8,128]{4,3,2,1,0:T(8,128)} %x_inverse.6._), calls=%async_computation.6 | async-start | bytes 8388608 | tf_op jit(solution)/shard_map/all_to_all | solution.py:535
  465.0 30.2 %all-to-all-start.7 = ((f32[8,1,64,8,128]{4,3,2,1,0:T(8,128)}), f32[8,1,64,8,128]{4,3,2,1,0:T(8,128)S(1)}, u32[]{:S(2)}, u32[]{:S(2)}) async-start(f32[8,1,64,8,128]{4,3,2,1,0:T(8,128)} %gate.23), calls=%async_computation.7 | async-start | bytes 4194304 | tf_op jit(solution)/shard_map/all_to_all | solution.py:535
  (5 other events, 5.2 us)

commit v2 on v1

--- a/solution.py
+++ b/solution.py
@@ -58,11 +58,11 @@
     return dot(left[0], right[0]) + (dot(left[0], right[1]) + dot(left[1], right[0]))
 
 
-def parameters(flops, read, written):
+def parameters(flops, read, written, weight=100):
     return dict(
         compiler_params=pltpu.CompilerParams(vmem_limit_bytes=vmem_bytes),
         cost_estimate=pl.CostEstimate(
-            flops=100 * flops, bytes_accessed=400 * (read + written), transcendentals=0
+            flops=weight * flops, bytes_accessed=4 * weight * (read + written), transcendentals=0
         ),
     )
 
@@ -124,7 +124,7 @@
         scratch_shapes=[pltpu.VMEM((levels * sublanes, part_y), jnp.float32)],
         name="into_levels",
         **parameters(6 * size * levels, size, size),
-    )(fields, wide(matrices), *follow)
+    )(fields, matrices, *follow)
 
 
 def edges_kernel(field_ref, _, low_ref, high_ref, first_ref, last_ref):
@@ -285,8 +285,8 @@
         *edges,
         coefficient,
         profile,
-        wide(deriv),
-        wide(matrices),
+        deriv,
+        matrices,
         *done,
         *follow,
     )
@@ -301,11 +301,16 @@
         lines = [rows_ref[:, f, m].reshape(groups * part_x, part_y) for f in range(count)]
         columns.append(jnp.concatenate(lines, axis=0))
     data = split(jnp.concatenate(columns, axis=1))
+    order = [lax.rem(me_ref[0] + s, targets) for s in range(targets)]
+    spectrum = product(
+        [jnp.concatenate([table_ref[h, o] for o in order], axis=0) for h in range(2)], data
+    )
+    lines = table_ref.shape[2]
     for s, out_ref in enumerate(out_refs):
-        target = lax.rem(me_ref[0] + s, targets)
-        spectrum = product((table_ref[0, target], table_ref[1, target]), data)
         for m in range(block):
-            out_ref[m] = spectrum[:, m * part_y : (m + 1) * part_y]
+            out_ref[m] = spectrum[
+                s * lines : (s + 1) * lines, m * part_y : (m + 1) * part_y
+            ]
 
 
 def block_of(levels):
@@ -410,15 +415,18 @@
         jnp.concatenate([table_ref[h, 0, o] for o in origins], axis=1) for h in range(2)
     ]
     lines = table[0].shape[0]
-    for m in range(levels):
-        cut = slice(m * part_y, (m + 1) * part_y)
-        rows_ref[pl.ds(m, lines, stride=levels), :] = product(
-            table, (high_ref[:, cut], low_ref[:, cut])
-        )
+    block = block_of(levels)
+    for start in range(0, levels, block):
+        cut = slice(start * part_y, (start + block) * part_y)
+        result = product(table, (high_ref[:, cut], low_ref[:, cut]))
+        for m in range(block):
+            rows_ref[pl.ds(start + m, lines, stride=levels), :] = result[
+                :, m * part_y : (m + 1) * part_y
+            ]
     out_ref[...] = rows_ref[...].reshape(out_ref.shape)
 
 
-def x_inverse(me, pieces, table, groups, follow):
+def x_inverse(me, pieces, table, groups, follow, weight=100):
     sources = len(pieces)
     levels, lines, part_y = pieces[0].shape
     count, full_x = table.shape[1], table.shape[3]
@@ -439,7 +447,9 @@
         scratch_shapes=[pltpu.VMEM((full_x, levels * part_y), half)] * 2
         + [pltpu.VMEM((rows * levels, part_y), jnp.float32)],
         name="x_inverse",
-        **parameters(6 * size * full_x * count, size + table.size // 2, size * count),
+        **parameters(
+            6 * size * full_x * count, size + table.size // 2, size * count, weight
+        ),
     )(me, follow, *pieces, table)
 
 
@@ -448,7 +458,8 @@
     return jnp.concatenate([rows_ref[g, component, x] for g in range(groups)], axis=0)
 
 
-def from_kernel(rows_ref, matrix_ref, base_ref, out_ref):
+def from_kernel(rows_ref, matrix_ref, base_ref, *refs):
+    out_ref = refs[-1]
     part_y = base_ref.shape[3]
     for pair in range(0, base_ref.shape[1], 2):
         fields = [column(rows_ref, 0, x) for x in (pair, pair + 1)]
@@ -457,7 +468,7 @@
         out_ref[0, pair + 1] = base_ref[0, pair + 1] + turned[:, part_y:]
 
 
-def from_levels(rows, matrices, base, components, in_place):
+def from_levels(rows, matrices, base, components, in_place, *follow):
     groups, count, part_x, per, part_y = rows.shape
     levels = groups * per
     sublanes = block_x(part_x)
@@ -471,13 +482,14 @@
             pl.BlockSpec((groups, 1, sublanes, per, part_y), lambda f, i: (0, f, i, 0, 0)),
             pl.BlockSpec((1, levels, 3 * levels), lambda f, i: (f, 0, 0)),
             spec,
-        ],
+        ]
+        + [anywhere] * len(follow),
         out_specs=spec,
         out_shape=jax.ShapeDtypeStruct(base.shape, jnp.float32),
         input_output_aliases={2: 0} if in_place else {},
         name="from_levels",
         **parameters(6 * size * levels, 2 * size, size),
-    )(rows, wide(matrices), base)
+    )(rows, matrices, base, *follow)
 
 
 def gradient_kernel(
@@ -523,7 +535,7 @@
         input_output_aliases={3: 0},
         name="gradient_of",
         **parameters(6 * size * levels, 7 * size, 2 * size),
-    )(rows, wide(matrix[None]), base, done, laplace, profile, follow)
+    )(rows, matrix, base, done, laplace, profile, follow)
 
 
 def shifted(cells, axis, shift):
@@ -607,12 +619,26 @@
     vectors_t = eigen_vectors.T
     inverse_t = eigen_inverse.T
     deriv_t = vert_deriv.T
-
     profile = jnp.broadcast_to(level_profile[:, None], velocity.shape[2:])
-
-    a_one = into_levels(cotangent, -vectors_t[None], (1,), count_x)
-    last = matmul(vectors_t, deriv_t)
-    a_two = into_levels(cotangent, jnp.stack([-vectors_t, last]), (0, 2), count_x, a_one)
+    enter_adjoint = wide(jnp.stack([-vectors_t, matmul(vectors_t, deriv_t)]))
+    enter_forward = wide(jnp.stack([eigen_inverse, matmul(eigen_inverse, vert_deriv)]))
+    leave_adjoint = wide(jnp.stack([inverse_t, -matmul(deriv_t, inverse_t)]))
+    leave_forward = wide(-jnp.stack([eigen_vectors, matmul(vert_deriv, eigen_vectors)]))
+    slope = wide(vert_deriv)
+
+    a_one = into_levels(cotangent, wide(-vectors_t[None]), (1,), count_x)
+    a_two = into_levels(
+        cotangent,
+        enter_adjoint,
+        (0, 2),
+        count_x,
+        a_one,
+        enter_forward,
+        leave_adjoint,
+        leave_forward,
+        slope,
+        profile,
+    )
     low, high, first, final = edges_of(velocity, a_one)
     sides = (shifted(final, "gx", 1), shifted(first, "gx", -1))
     lanes = -(-velocity.shape[1] // 128) * 128
@@ -623,52 +649,49 @@
     a_one = swap_x(a_one)
     a_sloped = x_forward(me, a_one, table_plain, *sides, *edges)
     a_two = swap_x(*gate([a_two], [a_one]))
-    last = matmul(eigen_inverse, vert_deriv)
-    common = (velocity, sides, edges, coefficient, profile, vert_deriv)
+    common = (velocity, sides, edges, coefficient, profile, slope)
     section, laplace, f_one = make_section(
-        *common, eigen_inverse[None], count_x, (1,), (), (a_sloped[0],)
+        *common, enter_forward, count_x, (1,), (), (a_sloped[0],)
     )
     section, laplace, f_two = make_section(
-        *common, jnp.stack([eigen_inverse, last]), count_x, (0, 2), (section, laplace), ()
+        *common, enter_forward, count_x, (0, 2), (section, laplace), ()
     )
     a_sloped = swap_y(a_sloped, ())
     a_plain = x_forward(me, a_two, table_joint, f_two)
     f_one = swap_x(*gate([f_one], [a_plain[0], *a_sloped]))
     a_plain = swap_y(a_plain, a_sloped)
     f_sloped = x_forward(me, f_one, table_plain, *a_sloped)
-    f_two = swap_x(*gate([f_two], [f_sloped[0]]))
+    f_two = swap_x(*gate([f_two], [f_one]))
     f_sloped = swap_y(f_sloped, a_plain)
+    f_plain = x_forward(me, f_two, table_joint, *a_plain)
+
     def solve(plain, sloped, follow):
         full = (full_x, full_y)
         return y_solve(plain, sloped, rates, me, y_forward, y_inverse, full, follow)
 
-    a_flat, a_bent = solve(a_plain, a_sloped, f_sloped[0])
-    a_flat = swap_y(a_flat, f_sloped)
-    f_plain = x_forward(me, f_two, table_joint, *f_sloped)
-    f_plain = swap_y(f_plain, a_flat)
-    a_two = x_inverse(me, a_flat, back_joint, count_x, f_plain[0])
-    a_bent = swap_y(a_bent, (*f_plain, a_two))
+    a_flat, a_bent = solve(a_plain, a_sloped, f_plain[0])
+    f_plain = swap_y(f_plain, f_sloped)
+    a_flat = swap_y(a_flat, f_plain)
+    f_flat, f_bent = solve(f_plain, f_sloped, a_bent[0])
+    f_flat = swap_y(f_flat, a_flat)
+    a_two = x_inverse(me, a_flat, back_joint, count_x, f_flat[0])
+    a_bent = swap_y(a_bent, (*f_flat, a_two))
     a_two = swap_x(a_two)
-    f_flat, f_bent = solve(f_plain, f_sloped, a_bent[0])
-    f_flat = swap_y(f_flat, a_bent)
-    a_one = x_inverse(me, a_bent, back_plain, count_x, f_flat[0])
-    last = -matmul(deriv_t, inverse_t)
-    adjoint = from_levels(a_two, jnp.stack([inverse_t, last]), cotangent, (0, 2), False)
-    f_bent = swap_y(f_bent, (*f_flat, adjoint))
-    a_one = swap_x(*gate([a_one], [a_two]))
-    f_two = x_inverse(me, f_flat, back_joint, count_x, a_one)
-    f_one = x_inverse(me, f_bent, back_plain, count_x, f_two)
-    f_two = swap_x(f_two)
-    f_one = swap_x(*gate([f_one], [f_two]))
+    f_two = x_inverse(me, f_flat, back_joint, count_x, a_bent[0])
+    adjoint = from_levels(a_two, leave_adjoint, cotangent, (0, 2), False)
+    f_bent = swap_y(f_bent, (*a_bent, adjoint))
+    f_two = swap_x(*gate([f_two], [a_two]))
+    a_one = x_inverse(me, a_bent, back_plain, count_x, f_bent[0], 10)
+    (a_one,) = gate([a_one], [f_two])
+    f_one = x_inverse(me, f_bent, back_plain, count_x, a_one)
+    a_one = swap_x(a_one)
+    f_one = swap_x(*gate([f_one], [a_one]))
 
     adjoint_velocity, gradient = gradient_of(
-        a_one, inverse_t, cotangent, adjoint, laplace, profile, f_bent[1]
-    )
-    last = -matmul(vert_deriv, eigen_vectors)
-    new_velocity = from_levels(
-        f_two, jnp.stack([-eigen_vectors, last]), section, (0, 2), True
-    )
-    new_velocity = from_levels(f_one, -eigen_vectors[None], new_velocity, (1,), True)
+        a_one, leave_adjoint, cotangent, adjoint, laplace, profile, f_bent[1]
+    )
+    new_velocity = from_levels(f_two, leave_forward, section, (0, 2), True, a_one)
+    new_velocity = from_levels(f_one, leave_forward, new_velocity, (1,), True)
     return (new_velocity, adjoint_velocity, gradient)
 
 

time: 503 us -> 485 us (0.964)
  Pallas kernels: 166 us -> 156 us
    ppermute x28, waiting for transfers between devices: 110 us -> 74.2 us  [shifted(): lax.ppermute(cells, axis, [(i, (i + shift) % count) for i in range(count)])]
    all_to_all x8, waiting for transfers between devices: 70.7 us -> 103 us  [swap_x(): return lax.all_to_all(rows, 'gx', split_axis=0, concat_axis=0, tiled=True)]
    pallas_call x4, Pallas kernels: 37.3 us -> 27.2 us  [x_inverse(): pl.pallas_call(functools.partial(x_inverse_kernel, sources), grid=(count,...]
  transfers between devices with their start and end apart: 36 -> 36, of which waited for: 13 -> 13; matrix products, arithmetic and copies ran while one was open for 2% -> 1% of each run, Pallas kernels for 31% -> 30%
where the time goes in v2:
time: 485 us; the launch traced here: 483 us
  waiting for transfers between devices  178 us (37%)
  Pallas kernels  156 us (32%)
  starting transfers between devices  134 us (28%)
  local copies, waits for them, and re-layouts  9.75 us (2%)
    all_to_all x8, waiting for transfers between devices, swap_x(): return lax.all_to_all(rows, 'gx', split_axis=0, concat_axis=0, tiled=True)  103 us
    ppermute x28, starting transfers between devices, shifted(): lax.ppermute(cells, axis, [(i, (i + shift) % count) for i in range(count)])  98.6 us
    ppermute x28, waiting for transfers between devices, shifted(): lax.ppermute(cells, axis, [(i, (i + shift) % count) for i in range(count)])  74.2 us
    all_to_all x8, starting transfers between devices, swap_x(): return lax.all_to_all(rows, 'gx', split_axis=0, concat_axis=0, tiled=True)  34.9 us
    pallas_call x2, Pallas kernels, y_solve(): pl.pallas_call(functools.partial(solve_kernel, sources, full), grid=(leve...  29.2 us
    pallas_call x4, Pallas kernels, x_inverse(): pl.pallas_call(functools.partial(x_inverse_kernel, sources), grid=(count,...  27.2 us
    pallas_call x2, Pallas kernels, make_section(): pl.pallas_call(section_kernel, grid=(count, part_x // sublanes), in_specs...  25.4 us
    pallas_call x4, Pallas kernels, x_forward(): pl.pallas_call(x_kernel, grid=(levels // block,), in_specs=[scalars, pl.B...  24.4 us
  transfers between devices with their start and end apart: 36, of which 13 were waited for; matrix products, arithmetic and copies ran while one was open for 1% of the time, Pallas kernels for 30%

profile of v2, /device:TPU:0, one launch (start us, length us, event | category | flops | bytes accessed | tf_op | source)
XLA Modules:
  0.0 482.9 jit_solution(5363350322614418013)
XLA Ops:
  2.2 4.4 into_levels.2._.refs_0_
  6.6 5.2 %all-to-all-start = ((f32[8,1,8,64,128]{4,3,2,1,0:T(8,128)}), f32[8,1,8,64,128]{4,3,2,1,0:T(8,128)S(1)}, u32[]{:S(2)}, u32[]{:S(2)}) async-start(f32[8,1,8,64,128]{4,3,2,1,0:T(8,128)} %into_levels.2._.refs_0_), calls=%async_computation | async-start | bytes 4194304 | tf_op jit(solution)/shard_map/all_to_all | solution.py:547
  11.8 6.8 %edges_of.1 = (f32[3,64,64]{2,1,0:T(8,128)}, f32[3,64,64]{2,1,0:T(8,128)}, f32[3,1,64,128]{3,2,1,0:T(8,128)}, f32[3,1,64,128]{3,2,1,0:T(8,128)}) custom-call(f32[3,64,64,128]{3,2,1,0:T(8,128)} %refs_3_.3, f32[8,1,8,64,128]{4,3,2,1,0:T(8,128)} %into_levels.2._.refs_0_), custom_call_target="tpu_custom_call" | custom-call | bytes 629145600 | tf_op jit(solution)/shard_map/edges_of/pallas_call | solution.py:158
  22.4 2.6 collective-permute-start.1
  30.3 7.7 %into_levels.3.refs_0_ = f32[8,2,8,64,128]{4,3,2,1,0:T(8,128)} custom-call(f32[3,64,64,128]{3,2,1,0:T(8,128)} %base_ref.3, bf16[2,64,192]{2,1,0:T(8,128)(2,1)} %pad_maximum_fusion.3.matrix_ref, f32[8,1,8,64,128]{4,3,2,1,0:T(8,128)} %into_levels.2._.refs_0_, bf16[2,64,192]{2,1,0:T(8,128)(2,1)} %pad_maximum_fusion.1.refs_11_.refs_1_, ...), custom_call_target="tpu_custom_call" | custom-call | flops 40265318400 | bytes 838860800 | tf_op jit(solution)/shard_map/into_levels/pallas_call | solution.py:112
  40.7 4.6 all-to-all-start.1
  46.0 5.1 %x_forward.4 = (f32[8,128,128]{2,1,0:T(8,128)}, f32[8,128,128]{2,1,0:T(8,128)}, f32[8,128,128]{2,1,0:T(8,128)}, f32[8,128,128]{2,1,0:T(8,128)}) custom-call(s32[1]{0:T(128)} %bitcast.me_ref.group_ref, f32[8,1,8,64,128]{4,3,2,1,0:T(8,128)} %copy-done, bf16[2,4,128,512]{3,2,1,0:T(8,128)(2,1)} %constant.29.clone.table_ref, f32[3,1,64,128]{3,2,1,0:T(8,128)} %copy-done.10, ...), custom_call_target="tpu_custom_call" | custom-call | flops 161061273600 | bytes 524288000 | tf_op jit(solution)/shard_map/x_forward/pallas_call | solution.py:325
  52.1 2.6 collective-permute-start.5
  56.1 9.1 %make_section.2 = (f32[3,64,64,128]{3,2,1,0:T(8,128)}, f32[3,64,64,128]{3,2,1,0:T(8,128)}, f32[8,1,8,64,128]{4,3,2,1,0:T(8,128)}) custom-call(f32[3,64,64,128]{3,2,1,0:T(8,128)} %refs_3_.3, f32[3,64,64,128]{3,2,1,0:T(8,128)} %refs_3_.3, f32[3,64,64,128]{3,2,1,0:T(8,128)} %refs_3_.3, f32[3,64,64,128]{3,2,1,0:T(8,128)} %refs_3_.3, ...), custom_call_target="tpu_custom_call" | custom-call | flops 40265318400 | bytes 1887436800 | tf_op jit(solution)/shard_map/make_section/pallas_call | solution.py:237
  65.2 16.3 %make_section.3 = (f32[3,64,64,128]{3,2,1,0:T(8,128)}, f32[3,64,64,128]{3,2,1,0:T(8,128)}, f32[8,2,8,64,128]{4,3,2,1,0:T(8,128)}) custom-call(f32[3,64,64,128]{3,2,1,0:T(8,128)} %refs_3_.3, f32[3,64,64,128]{3,2,1,0:T(8,128)} %refs_3_.3, f32[3,64,64,128]{3,2,1,0:T(8,128)} %refs_3_.3, ...), custom_call_target="tpu_custom_call", output_to_operand_aliasing={{0}: (12, {}), {1}: (13, {})} | custom-call | flops 80530636800 | bytes 3774873600 | tf_op jit(solution)/shard_map/make_section/pallas_call | solution.py:237
  81.4 12.9 %all-to-all-done.1.rows_ref = f32[8,2,8,64,128]{4,3,2,1,0:T(8,128)} async-done(((f32[8,2,8,64,128]{4,3,2,1,0:T(8,128)}), f32[8,2,8,64,128]{4,3,2,1,0:T(8,128)}, u32[]{:S(2)}, u32[]{:S(2)}) %all-to-all-start.1) | async-done | bytes 4194336 | tf_op jit(solution)/shard_map/all_to_all | solution.py:547
  94.4 7.1 %x_forward.5 = (f32[8,128,128]{2,1,0:T(8,128)}, f32[8,128,128]{2,1,0:T(8,128)}, f32[8,128,128]{2,1,0:T(8,128)}, f32[8,128,128]{2,1,0:T(8,128)}) custom-call(s32[1]{0:T(128)} %bitcast.me_ref.group_ref, f32[8,2,8,64,128]{4,3,2,1,0:T(8,128)} %all-to-all-done.1.rows_ref, bf16[2,4,128,1024]{3,2,1,0:T(8,128)(2,1)} %constant.30.clone.table_ref, ...), custom_call_target="tpu_custom_call" | custom-call | flops 322122547200 | bytes 838860800 | tf_op jit(solution)/shard_map/x_forward/pallas_call | solution.py:325
  101.5 3.6 all-to-all-start.2
  106.9 2.6 collective-permute-start.8
  110.8 20.9 %all-to-all-done.2.refs_1_.rows_ref = f32[8,1,8,64,128]{4,3,2,1,0:T(8,128)S(1)} async-done(((f32[8,1,8,64,128]{4,3,2,1,0:T(8,128)}), f32[8,1,8,64,128]{4,3,2,1,0:T(8,128)S(1)}, u32[]{:S(2)}, u32[]{:S(2)}) %all-to-all-start.2) | async-done | bytes 2097184 | tf_op jit(solution)/shard_map/all_to_all | solution.py:547
  133.0 4.6 all-to-all-start.3
  137.6 5.1 %x_forward.7 = (f32[8,128,128]{2,1,0:T(8,128)}, f32[8,128,128]{2,1,0:T(8,128)}, f32[8,128,128]{2,1,0:T(8,128)}, f32[8,128,128]{2,1,0:T(8,128)}) custom-call(s32[1]{0:T(128)} %bitcast.me_ref.group_ref, f32[8,1,8,64,128]{4,3,2,1,0:T(8,128)} %copy-done.1, bf16[2,4,128,512]{3,2,1,0:T(8,128)(2,1)} %constant.29.clone.table_ref, ...), custom_call_target="tpu_custom_call" | custom-call | flops 161061273600 | bytes 524288000 | tf_op jit(solution)/shard_map/x_forward/pallas_call | solution.py:325
  144.7 11.6 %collective-permute-start.10 = (f32[8,128,128]{2,1,0:T(8,128)}, f32[8,128,128]{2,1,0:T(8,128)}, u32[]{:S(2)}, u32[]{:S(2)}) collective-permute-start(f32[8,128,128]{2,1,0:T(8,128)} %get-tuple-element.96), channel_id=1, source_target_pairs={{0,1},{1,2},{2,3},{3,0},{4,5},{5,6},{6,7},{7,4},{8,9},{9,10},{10,1... | collective-permute-start | bytes 1572872 | tf_op jit(solution)/shard_map/ppermute | solution.py:543
  158.7 28.0 %all-to-all-done.3.rows_ref = f32[8,2,8,64,128]{4,3,2,1,0:T(8,128)} async-done(((f32[8,2,8,64,128]{4,3,2,1,0:T(8,128)}), f32[8,2,8,64,128]{4,3,2,1,0:T(8,128)}, u32[]{:S(2)}, u32[]{:S(2)}) %all-to-all-start.3) | async-done | bytes 4194336 | tf_op jit(solution)/shard_map/all_to_all | solution.py:547
  186.7 7.1 %x_forward.6 = (f32[8,128,128]{2,1,0:T(8,128)}, f32[8,128,128]{2,1,0:T(8,128)}, f32[8,128,128]{2,1,0:T(8,128)}, f32[8,128,128]{2,1,0:T(8,128)}) custom-call(s32[1]{0:T(128)} %bitcast.me_ref.group_ref, f32[8,2,8,64,128]{4,3,2,1,0:T(8,128)} %all-to-all-done.3.rows_ref, bf16[2,4,128,1024]{3,2,1,0:T(8,128)(2,1)} %constant.30.clone.table_ref, ...), custom_call_target="tpu_custom_call" | custom-call | flops 322122547200 | bytes 838860800 | tf_op jit(solution)/shard_map/x_forward/pallas_call | solution.py:325
  193.8 9.5 %collective-permute-start.13 = (f32[8,128,128]{2,1,0:T(8,128)}, f32[8,128,128]{2,1,0:T(8,128)}, u32[]{:S(2)}, u32[]{:S(2)}) collective-permute-start(f32[8,128,128]{2,1,0:T(8,128)} %get-tuple-element.99), channel_id=1, source_target_pairs={{0,1},{1,2},{2,3},{3,0},{4,5},{5,6},{6,7},{7,4},{8,9},{9,10},{10,1... | collective-permute-start | bytes 1572872 | tf_op jit(solution)/shard_map/ppermute | solution.py:543
  205.6 14.6 %y_solve.2 = (f32[8,128,128]{2,1,0:T(8,128)}, f32[8,128,128]{2,1,0:T(8,128)}, f32[8,128,128]{2,1,0:T(8,128)}, f32[8,128,128]{2,1,0:T(8,128)}, f32[8,128,128]{2,1...) custom-call(s32[1]{0:T(128)} %bitcast.me_ref.group_ref, ...), custom_call_target="tpu_custom_call" | custom-call | flops 644245094400 | bytes 1258291200 | tf_op jit(solution)/shard_map/y_solve/pallas_call | solution.py:385
  220.3 18.8 %collective-permute-done.14.refs_2_.refs_5_ = f32[8,128,128]{2,1,0:T(8,128)} collective-permute-done((f32[8,128,128]{2,1,0:T(8,128)}, f32[8,128,128]{2,1,0:T(8,128)}, u32[]{:S(2)}, u32[]{:S(2)}) %collective-permute-start.14) | collective-permute-done | bytes 524320 | tf_op jit(solution)/shard_map/ppermute | solution.py:543
  239.1 11.7 %collective-permute-start.16 = (f32[8,128,128]{2,1,0:T(8,128)}, f32[8,128,128]{2,1,0:T(8,128)}, u32[]{:S(2)}, u32[]{:S(2)}) collective-permute-start(f32[8,128,128]{2,1,0:T(8,128)} %get-tuple-element.114), channel_id=1, source_target_pairs={{0,1},{1,2},{2,3},{3,0},{4,5},{5,6},{6,7},{7,4},{8,9},{9,10},{10,1... | collective-permute-start | bytes 1572872 | tf_op jit(solution)/shard_map/ppermute | solution.py:543
  253.2 14.6 %y_solve.3 = (f32[8,128,128]{2,1,0:T(8,128)}, f32[8,128,128]{2,1,0:T(8,128)}, f32[8,128,128]{2,1,0:T(8,128)}, f32[8,128,128]{2,1,0:T(8,128)}, f32[8,128,128]{2,1...) custom-call(s32[1]{0:T(128)} %bitcast.me_ref.group_ref, ...), custom_call_target="tpu_custom_call" | custom-call | flops 644245094400 | bytes 1258291200 | tf_op jit(solution)/shard_map/y_solve/pallas_call | solution.py:385
  267.8 18.5 %collective-permute-done.17.refs_5_.refs_2_ = f32[8,128,128]{2,1,0:T(8,128)} collective-permute-done((f32[8,128,128]{2,1,0:T(8,128)}, f32[8,128,128]{2,1,0:T(8,128)}, u32[]{:S(2)}, u32[]{:S(2)}) %collective-permute-start.17) | collective-permute-done | bytes 524320 | tf_op jit(solution)/shard_map/ppermute | solution.py:543
  286.3 11.7 %collective-permute-start.19 = (f32[8,128,128]{2,1,0:T(8,128)}, f32[8,128,128]{2,1,0:T(8,128)}, u32[]{:S(2)}, u32[]{:S(2)}) collective-permute-start(f32[8,128,128]{2,1,0:T(8,128)} %get-tuple-element.117), channel_id=1, source_target_pairs={{0,1},{1,2},{2,3},{3,0},{4,5},{5,6},{6,7},{7,4},{8,9},{9,10},{10,1... | collective-permute-start | bytes 1572872 | tf_op jit(solution)/shard_map/ppermute | solution.py:543
  300.3 8.1 %x_inverse.4.refs_7_ = f32[8,2,64,8,128]{4,3,2,1,0:T(8,128)} custom-call(s32[1]{0:T(128)} %bitcast.me_ref.group_ref, f32[8,128,128]{2,1,0:T(8,128)} %get-tuple-element.106._.refs_3_.refs_0_, f32[8,128,128]{2,1,0:T(8,128)} %get-tuple-element.110.refs_3_.refs_0_, f32[8,128,128]{2,1,0:T(8,128)} %collective-permute-done.16.refs_4_.refs_1_, ...), custom_call_target="tpu_custom_call" | custom-call | flops 322122547200 | bytes 838860800 | tf_op jit(solution)/shard_map/x_inverse/pallas_call | solution.py:437
  308.4 4.6 all-to-all-start.4
  313.0 20.8 %collective-permute-done.20.refs_5_.refs_2_ = f32[8,128,128]{2,1,0:T(8,128)} collective-permute-done((f32[8,128,128]{2,1,0:T(8,128)}, f32[8,128,128]{2,1,0:T(8,128)}, u32[]{:S(2)}, u32[]{:S(2)}) %collective-permute-start.20) | collective-permute-done | bytes 524320 | tf_op jit(solution)/shard_map/ppermute | solution.py:543
  333.8 11.7 %collective-permute-start.22 = (f32[8,128,128]{2,1,0:T(8,128)}, f32[8,128,128]{2,1,0:T(8,128)}, u32[]{:S(2)}, u32[]{:S(2)}) collective-permute-start(f32[8,128,128]{2,1,0:T(8,128)} %get-tuple-element.120), channel_id=1, source_target_pairs={{0,1},{1,2},{2,3},{3,0},{4,5},{5,6},{6,7},{7,4},{8,9},{9,10},{10,1... | collective-permute-start | bytes 1572872 | tf_op jit(solution)/shard_map/ppermute | solution.py:543
  347.9 8.1 %x_inverse.6.refs_0_ = f32[8,2,64,8,128]{4,3,2,1,0:T(8,128)} custom-call(s32[1]{0:T(128)} %bitcast.me_ref.group_ref, f32[8,128,128]{2,1,0:T(8,128)} %get-tuple-element.88._.refs_0_.refs_3_, f32[8,128,128]{2,1,0:T(8,128)} %get-tuple-element.106._.refs_3_.refs_0_, f32[8,128,128]{2,1,0:T(8,128)} %collective-permute-done.19.refs_4_.refs_1_, ...), custom_call_target="tpu_custom_call" | custom-call | flops 322122547200 | bytes 838860800 | tf_op jit(solution)/shard_map/x_inverse/pallas_call | solution.py:437
  356.0 6.2 %all-to-all-done.4.refs_1_.rows_ref = f32[8,2,64,8,128]{4,3,2,1,0:T(8,128)} async-done(((f32[8,2,64,8,128]{4,3,2,1,0:T(8,128)}), f32[8,2,64,8,128]{4,3,2,1,0:T(8,128)}, u32[]{:S(2)}, u32[]{:S(2)}) %all-to-all-start.4) | async-done | bytes 4194336 | tf_op jit(solution)/shard_map/all_to_all | solution.py:547
  362.1 4.6 all-to-all-start.5
  366.7 8.4 %from_levels.3.refs_7_.done_ref = f32[3,64,64,128]{3,2,1,0:T(8,128)} custom-call(f32[8,2,64,8,128]{4,3,2,1,0:T(8,128)} %all-to-all-done.4.refs_1_.rows_ref, bf16[2,64,192]{2,1,0:T(8,128)(2,1)} %pad_maximum_fusion.5.refs_2_.matrix_ref, f32[3,64,64,128]{3,2,1,0:T(8,128)} %base_ref.3), custom_call_target="tpu_custom_call" | custom-call | flops 40265318400 | bytes 1258291200 | tf_op jit(solution)/shard_map/from_levels/pallas_call | solution.py:478
  375.1 5.9 %collective-permute-done.23.refs_2_.refs_5_ = f32[8,128,128]{2,1,0:T(8,128)} collective-permute-done((f32[8,128,128]{2,1,0:T(8,128)}, f32[8,128,128]{2,1,0:T(8,128)}, u32[]{:S(2)}, u32[]{:S(2)}) %collective-permute-start.23) | collective-permute-done | bytes 524320 | tf_op jit(solution)/shard_map/ppermute | solution.py:543
  381.0 11.7 %collective-permute-start.25 = (f32[8,128,128]{2,1,0:T(8,128)}, f32[8,128,128]{2,1,0:T(8,128)S(1)}, u32[]{:S(2)}, u32[]{:S(2)}) collective-permute-start(f32[8,128,128]{2,1,0:T(8,128)} %get-tuple-element.126), channel_id=1, source_target_pairs={{0,1},{1,2},{2,3},{3,0},{4,5},{5,6},{6,7},{7,4},{8,9},{9,10},{10,1... | collective-permute-start | bytes 1572872 | tf_op jit(solution)/shard_map/ppermute | solution.py:543
  395.0 5.5 %x_inverse.5.refs_0_ = f32[8,1,64,8,128]{4,3,2,1,0:T(8,128)} custom-call(s32[1]{0:T(128)} %bitcast.me_ref.group_ref, f32[8,128,128]{2,1,0:T(8,128)} %get-tuple-element.102._.refs_0_, f32[8,128,128]{2,1,0:T(8,128)} %get-tuple-element.88._.refs_0_.refs_3_, f32[8,128,128]{2,1,0:T(8,128)} %collective-permute-done.22.refs_1_.refs_4_, ...), custom_call_target="tpu_custom_call" | custom-call | flops 16106127360 | bytes 52428800 | tf_op jit(solution)/shard_map/x_inverse/pallas_call | solution.py:437
  400.5 15.3 %all-to-all-done.5.refs_1_.rows_ref = f32[8,2,64,8,128]{4,3,2,1,0:T(8,128)} async-done(((f32[8,2,64,8,128]{4,3,2,1,0:T(8,128)}), f32[8,2,64,8,128]{4,3,2,1,0:T(8,128)}, u32[]{:S(2)}, u32[]{:S(2)}) %all-to-all-start.5) | async-done | bytes 4194336 | tf_op jit(solution)/shard_map/all_to_all | solution.py:547
  415.8 4.3 all-to-all-start.6
  420.2 8.2 %collective-permute-done.26.refs_2_ = f32[8,128,128]{2,1,0:T(8,128)S(1)} collective-permute-done((f32[8,128,128]{2,1,0:T(8,128)}, f32[8,128,128]{2,1,0:T(8,128)S(1)}, u32[]{:S(2)}, u32[]{:S(2)}) %collective-permute-start.26) | collective-permute-done | bytes 524320 | tf_op jit(solution)/shard_map/ppermute | solution.py:543
  430.0 5.5 %x_inverse.7.refs_0_ = f32[8,1,64,8,128]{4,3,2,1,0:T(8,128)} custom-call(s32[1]{0:T(128)} %bitcast.me_ref.group_ref, f32[8,1,64,8,128]{4,3,2,1,0:T(8,128)} %gate.23._, f32[8,128,128]{2,1,0:T(8,128)} %get-tuple-element.102._.refs_0_, f32[8,128,128]{2,1,0:T(8,128)} %copy-done.7, f32[8,128,128]{2,1,0:T(8,128)} %copy-done.8, f32[8,128,128]{2,1,0:T(8,128)} %copy-done.9, ...), custom_call_target="tpu_custom_call" | custom-call | flops 161061273600 | bytes 524288000 | tf_op jit(solution)/shard_map/x_inverse/pallas_call | solution.py:437
  435.5 11.3 %all-to-all-done.6.refs_1_.refs_0_.rows_ref = f32[8,1,64,8,128]{4,3,2,1,0:T(8,128)} async-done(((f32[8,1,64,8,128]{4,3,2,1,0:T(8,128)}), f32[8,1,64,8,128]{4,3,2,1,0:T(8,128)}, u32[]{:S(2)}, u32[]{:S(2)}) %all-to-all-start.6) | async-done | bytes 2097184 | tf_op jit(solution)/shard_map/all_to_all | solution.py:547
  446.8 3.6 all-to-all-start.7
  450.4 8.4 %from_levels.4.base_ref = f32[3,64,64,128]{3,2,1,0:T(8,128)} custom-call(f32[8,2,64,8,128]{4,3,2,1,0:T(8,128)} %all-to-all-done.5.refs_1_.rows_ref, bf16[2,64,192]{2,1,0:T(8,128)(2,1)} %pad_maximum_fusion.6.refs_3_.matrix_ref, f32[3,64,64,128]{3,2,1,0:T(8,128)} %get-tuple-element.129.base_ref, ...), custom_call_target="tpu_custom_call", output_to_operand_aliasing={{}: (2, {})} | custom-call | flops 40265318400 | bytes 1258291200 | tf_op jit(solution)/shard_map/from_levels/pallas_call | solution.py:478
  458.8 9.3 %gradient_of.1 = (f32[3,64,64,128]{3,2,1,0:T(8,128)}, f32[64,64,128]{2,1,0:T(8,128)}) custom-call(f32[8,1,64,8,128]{4,3,2,1,0:T(8,128)} %all-to-all-done.6.refs_1_.refs_0_.rows_ref, bf16[2,64,192]{2,1,0:T(8,128)(2,1)} %pad_maximum_fusion.5.refs_2_.matrix_ref, f32[3,64,64,128]{3,2,1,0:T(8,128)} %base_ref.3, ...), custom_call_target="tpu_custom_call", output_to_operand_aliasing={{0}: (3, {})} | custom-call | flops 20132659200 | bytes 1887436800 | tf_op jit(solution)/shard_map/gradient_of/pallas_call | solution.py:518
  468.1 8.9 %all-to-all-done.7.rows_ref = f32[8,1,64,8,128]{4,3,2,1,0:T(8,128)S(1)} async-done(((f32[8,1,64,8,128]{4,3,2,1,0:T(8,128)}), f32[8,1,64,8,128]{4,3,2,1,0:T(8,128)S(1)}, u32[]{:S(2)}, u32[]{:S(2)}) %all-to-all-start.7) | async-done | bytes 2097184 | tf_op jit(solution)/shard_map/all_to_all | solution.py:547
  478.3 4.6 from_levels.5
  (105 shorter events, 39.8 us)
Async XLA Ops:
  6.6 32.8 %all-to-all-start = ((f32[8,1,8,64,128]{4,3,2,1,0:T(8,128)}), f32[8,1,8,64,128]{4,3,2,1,0:T(8,128)S(1)}, u32[]{:S(2)}, u32[]{:S(2)}) async-start(f32[8,1,8,64,128]{4,3,2,1,0:T(8,128)} %into_levels.2._.refs_0_), calls=%async_computation | async-start | bytes 4194304 | tf_op jit(solution)/shard_map/all_to_all | solution.py:547
  11.8 13.3 %copy-start.3 = (f32[64,64]{1,0:T(8,128)S(1)}, f32[64,64]{1,0:T(8,128)}, u32[]{:S(2)}) copy-start(f32[64,64]{1,0:T(8,128)} %param.18) | copy-start | bytes 49156
  11.8 13.3 %copy-start.5 = (f32[64,64]{1,0:T(8,128)S(1)}, f32[64,64]{1,0:T(8,128)}, u32[]{:S(2)}) copy-start(f32[64,64]{1,0:T(8,128)} %param.19) | copy-start | bytes 49156
  11.8 13.6 %copy-start.4 = (f32[64,64]{1,0:T(8,128)S(1)}, f32[64,64]{1,0:T(8,128)}, u32[]{:S(2)}) copy-start(f32[64,64]{1,0:T(8,128)} %param.20) | copy-start | bytes 49156
  11.8 17.9 %copy-start.6 = (f32[64]{0:T(128)S(1)}, f32[64]{0:T(128)}, u32[]{:S(2)}) copy-start(f32[64]{0:T(128)} %param.17) | copy-start | bytes 772
  18.6 19.5 %collective-permute-start.2 = (f32[3,64,64]{2,1,0:T(8,128)}, f32[3,64,64]{2,1,0:T(8,128)S(1)}, u32[]{:S(2)}, u32[]{:S(2)}) collective-permute-start(f32[3,64,64]{2,1,0:T(8,128)} %get-tuple-element.70), channel_id=1, source_target_pairs={{0,1},{1,2},{2,3},{3,0},{4,5},{5,6},{6,7},{7,4},{8,9},{9,10},{10,1... | collective-permute-start | bytes 147464 | tf_op jit(solution)/shard_map/ppermute | solution.py:543
  20.2 18.5 %collective-permute-start.3 = (f32[3,64,64]{2,1,0:T(8,128)}, f32[3,64,64]{2,1,0:T(8,128)S(1)}, u32[]{:S(2)}, u32[]{:S(2)}) collective-permute-start(f32[3,64,64]{2,1,0:T(8,128)} %get-tuple-element.71), channel_id=1, source_target_pairs={{0,3},{1,0},{2,1},{3,2},{4,7},{5,4},{6,5},{7,6},{8,11},{9,8},{10,9... | collective-permute-start | bytes 147464 | tf_op jit(solution)/shard_map/ppermute | solution.py:543
  22.4 22.8 %collective-permute-start = (f32[3,1,64,128]{3,2,1,0:T(8,128)}, f32[3,1,64,128]{3,2,1,0:T(8,128)S(1)}, u32[]{:S(2)}, u32[]{:S(2)}) collective-permute-start(f32[3,1,64,128]{3,2,1,0:T(8,128)} %get-tuple-element.68), channel_id=1, source_target_pairs={{0,4},{4,8},{8,12},{12,16},{16,20},{20,24},{24,28},{28,0},{1,5},{5... | collective-permute-start | bytes 294920 | tf_op jit(solution)/shard_map/ppermute | solution.py:543
  22.4 22.8 %collective-permute-start.1 = (f32[3,1,64,128]{3,2,1,0:T(8,128)}, f32[3,1,64,128]{3,2,1,0:T(8,128)S(1)}, u32[]{:S(2)}, u32[]{:S(2)}) collective-permute-start(f32[3,1,64,128]{3,2,1,0:T(8,128)} %get-tuple-element.69), channel_id=1, source_target_pairs={{0,28},{4,0},{8,4},{12,8},{16,12},{20,16},{24,20},{28,24},{1,29},{... | collective-permute-start | bytes 294920 | tf_op jit(solution)/shard_map/ppermute | solution.py:543
  39.4 1.3 copy-start
  40.7 53.7 %all-to-all-start.1 = ((f32[8,2,8,64,128]{4,3,2,1,0:T(8,128)}), f32[8,2,8,64,128]{4,3,2,1,0:T(8,128)}, u32[]{:S(2)}, u32[]{:S(2)}) async-start(f32[8,2,8,64,128]{4,3,2,1,0:T(8,128)} %gate.13), calls=%async_computation.1 | async-start | bytes 8388608 | tf_op jit(solution)/shard_map/all_to_all | solution.py:547
  45.3 0.7 copy-start.11
  51.0 50.4 %collective-permute-start.4 = (f32[8,128,128]{2,1,0:T(8,128)}, f32[8,128,128]{2,1,0:T(8,128)}, u32[]{:S(2)}, u32[]{:S(2)}) collective-permute-start(f32[8,128,128]{2,1,0:T(8,128)} %get-tuple-element.78), channel_id=1, source_target_pairs={{0,1},{1,2},{2,3},{3,0},{4,5},{5,6},{6,7},{7,4},{8,9},{9,10},{10,1... | collective-permute-start | bytes 1572872 | tf_op jit(solution)/shard_map/ppermute | solution.py:543
  52.1 49.3 %collective-permute-start.5 = (f32[8,128,128]{2,1,0:T(8,128)}, f32[8,128,128]{2,1,0:T(8,128)}, u32[]{:S(2)}, u32[]{:S(2)}) collective-permute-start(f32[8,128,128]{2,1,0:T(8,128)} %get-tuple-element.79), channel_id=1, source_target_pairs={{0,2},{1,3},{2,0},{3,1},{4,6},{5,7},{6,4},{7,5},{8,10},{9,11},{10,... | collective-permute-start | bytes 1572872 | tf_op jit(solution)/shard_map/ppermute | solution.py:543
  54.7 46.7 %collective-permute-start.6 = (f32[8,128,128]{2,1,0:T(8,128)}, f32[8,128,128]{2,1,0:T(8,128)}, u32[]{:S(2)}, u32[]{:S(2)}) collective-permute-start(f32[8,128,128]{2,1,0:T(8,128)} %get-tuple-element.80), channel_id=1, source_target_pairs={{0,3},{1,0},{2,1},{3,2},{4,7},{5,4},{6,5},{7,6},{8,11},{9,8},{10,9... | collective-permute-start | bytes 1572872 | tf_op jit(solution)/shard_map/ppermute | solution.py:543
  101.5 3.7 copy-start.12
  101.5 30.2 %all-to-all-start.2 = ((f32[8,1,8,64,128]{4,3,2,1,0:T(8,128)}), f32[8,1,8,64,128]{4,3,2,1,0:T(8,128)S(1)}, u32[]{:S(2)}, u32[]{:S(2)}) async-start(f32[8,1,8,64,128]{4,3,2,1,0:T(8,128)} %gate.14), calls=%async_computation.2 | async-start | bytes 4194304 | tf_op jit(solution)/shard_map/all_to_all | solution.py:547
  105.8 37.0 %collective-permute-start.7 = (f32[8,128,128]{2,1,0:T(8,128)}, f32[8,128,128]{2,1,0:T(8,128)}, u32[]{:S(2)}, u32[]{:S(2)}) collective-permute-start(f32[8,128,128]{2,1,0:T(8,128)} %get-tuple-element.84), channel_id=1, source_target_pairs={{0,1},{1,2},{2,3},{3,0},{4,5},{5,6},{6,7},{7,4},{8,9},{9,10},{10,1... | collective-permute-start | bytes 1572872 | tf_op jit(solution)/shard_map/ppermute | solution.py:543
  106.9 37.8 %collective-permute-start.8 = (f32[8,128,128]{2,1,0:T(8,128)}, f32[8,128,128]{2,1,0:T(8,128)}, u32[]{:S(2)}, u32[]{:S(2)}) collective-permute-start(f32[8,128,128]{2,1,0:T(8,128)} %get-tuple-element.85), channel_id=1, source_target_pairs={{0,2},{1,3},{2,0},{3,1},{4,6},{5,7},{6,4},{7,5},{8,10},{9,11},{10,... | collective-permute-start | bytes 1572872 | tf_op jit(solution)/shard_map/ppermute | solution.py:543
  109.5 35.2 %collective-permute-start.9 = (f32[8,128,128]{2,1,0:T(8,128)}, f32[8,128,128]{2,1,0:T(8,128)}, u32[]{:S(2)}, u32[]{:S(2)}) collective-permute-start(f32[8,128,128]{2,1,0:T(8,128)} %get-tuple-element.86), channel_id=1, source_target_pairs={{0,3},{1,0},{2,1},{3,2},{4,7},{5,4},{6,5},{7,6},{8,11},{9,8},{10,9... | collective-permute-start | bytes 1572872 | tf_op jit(solution)/shard_map/ppermute | solution.py:543
  131.7 1.3 copy-start.1
  133.0 53.7 %all-to-all-start.3 = ((f32[8,2,8,64,128]{4,3,2,1,0:T(8,128)}), f32[8,2,8,64,128]{4,3,2,1,0:T(8,128)}, u32[]{:S(2)}, u32[]{:S(2)}) async-start(f32[8,2,8,64,128]{4,3,2,1,0:T(8,128)} %gate.15), calls=%async_computation.3 | async-start | bytes 8388608 | tf_op jit(solution)/shard_map/all_to_all | solution.py:547
  144.7 49.1 %collective-permute-start.10 = (f32[8,128,128]{2,1,0:T(8,128)}, f32[8,128,128]{2,1,0:T(8,128)}, u32[]{:S(2)}, u32[]{:S(2)}) collective-permute-start(f32[8,128,128]{2,1,0:T(8,128)} %get-tuple-element.96), channel_id=1, source_target_pairs={{0,1},{1,2},{2,3},{3,0},{4,5},{5,6},{6,7},{7,4},{8,9},{9,10},{10,1... | collective-permute-start | bytes 1572872 | tf_op jit(solution)/shard_map/ppermute | solution.py:543
  156.3 37.5 %collective-permute-start.11 = (f32[8,128,128]{2,1,0:T(8,128)}, f32[8,128,128]{2,1,0:T(8,128)}, u32[]{:S(2)}, u32[]{:S(2)}) collective-permute-start(f32[8,128,128]{2,1,0:T(8,128)} %get-tuple-element.97), channel_id=1, source_target_pairs={{0,2},{1,3},{2,0},{3,1},{4,6},{5,7},{6,4},{7,5},{8,10},{9,11},{10,... | collective-permute-start | bytes 1572872 | tf_op jit(solution)/shard_map/ppermute | solution.py:543
  157.6 36.2 %collective-permute-start.12 = (f32[8,128,128]{2,1,0:T(8,128)}, f32[8,128,128]{2,1,0:T(8,128)}, u32[]{:S(2)}, u32[]{:S(2)}) collective-permute-start(f32[8,128,128]{2,1,0:T(8,128)} %get-tuple-element.98), channel_id=1, source_target_pairs={{0,3},{1,0},{2,1},{3,2},{4,7},{5,4},{6,5},{7,6},{8,11},{9,8},{10,9... | collective-permute-start | bytes 1572872 | tf_op jit(solution)/shard_map/ppermute | solution.py:543
  193.8 26.5 %collective-permute-start.13 = (f32[8,128,128]{2,1,0:T(8,128)}, f32[8,128,128]{2,1,0:T(8,128)}, u32[]{:S(2)}, u32[]{:S(2)}) collective-permute-start(f32[8,128,128]{2,1,0:T(8,128)} %get-tuple-element.99), channel_id=1, source_target_pairs={{0,1},{1,2},{2,3},{3,0},{4,5},{5,6},{6,7},{7,4},{8,9},{9,10},{10,1... | collective-permute-start | bytes 1572872 | tf_op jit(solution)/shard_map/ppermute | solution.py:543
  203.3 35.8 %collective-permute-start.14 = (f32[8,128,128]{2,1,0:T(8,128)}, f32[8,128,128]{2,1,0:T(8,128)}, u32[]{:S(2)}, u32[]{:S(2)}) collective-permute-start(f32[8,128,128]{2,1,0:T(8,128)} %get-tuple-element.100), channel_id=1, source_target_pairs={{0,2},{1,3},{2,0},{3,1},{4,6},{5,7},{6,4},{7,5},{8,10},{9,11},{10,... | collective-permute-start | bytes 1572872 | tf_op jit(solution)/shard_map/ppermute | solution.py:543
  205.3 33.8 %collective-permute-start.15 = (f32[8,128,128]{2,1,0:T(8,128)}, f32[8,128,128]{2,1,0:T(8,128)}, u32[]{:S(2)}, u32[]{:S(2)}) collective-permute-start(f32[8,128,128]{2,1,0:T(8,128)} %get-tuple-element.101), channel_id=1, source_target_pairs={{0,3},{1,0},{2,1},{3,2},{4,7},{5,4},{6,5},{7,6},{8,11},{9,8},{10,9... | collective-permute-start | bytes 1572872 | tf_op jit(solution)/shard_map/ppermute | solution.py:543
  239.1 28.7 %collective-permute-start.16 = (f32[8,128,128]{2,1,0:T(8,128)}, f32[8,128,128]{2,1,0:T(8,128)}, u32[]{:S(2)}, u32[]{:S(2)}) collective-permute-start(f32[8,128,128]{2,1,0:T(8,128)} %get-tuple-element.114), channel_id=1, source_target_pairs={{0,1},{1,2},{2,3},{3,0},{4,5},{5,6},{6,7},{7,4},{8,9},{9,10},{10,1... | collective-permute-start | bytes 1572872 | tf_op jit(solution)/shard_map/ppermute | solution.py:543
  250.8 35.5 %collective-permute-start.17 = (f32[8,128,128]{2,1,0:T(8,128)}, f32[8,128,128]{2,1,0:T(8,128)}, u32[]{:S(2)}, u32[]{:S(2)}) collective-permute-start(f32[8,128,128]{2,1,0:T(8,128)} %get-tuple-element.115), channel_id=1, source_target_pairs={{0,2},{1,3},{2,0},{3,1},{4,6},{5,7},{6,4},{7,5},{8,10},{9,11},{10,... | collective-permute-start | bytes 1572872 | tf_op jit(solution)/shard_map/ppermute | solution.py:543
  252.3 33.9 %collective-permute-start.18 = (f32[8,128,128]{2,1,0:T(8,128)}, f32[8,128,128]{2,1,0:T(8,128)}, u32[]{:S(2)}, u32[]{:S(2)}) collective-permute-start(f32[8,128,128]{2,1,0:T(8,128)} %get-tuple-element.116), channel_id=1, source_target_pairs={{0,3},{1,0},{2,1},{3,2},{4,7},{5,4},{6,5},{7,6},{8,11},{9,8},{10,9... | collective-permute-start | bytes 1572872 | tf_op jit(solution)/shard_map/ppermute | solution.py:543
  286.3 26.7 %collective-permute-start.19 = (f32[8,128,128]{2,1,0:T(8,128)}, f32[8,128,128]{2,1,0:T(8,128)}, u32[]{:S(2)}, u32[]{:S(2)}) collective-permute-start(f32[8,128,128]{2,1,0:T(8,128)} %get-tuple-element.117), channel_id=1, source_target_pairs={{0,1},{1,2},{2,3},{3,0},{4,5},{5,6},{6,7},{7,4},{8,9},{9,10},{10,1... | collective-permute-start | bytes 1572872 | tf_op jit(solution)/shard_map/ppermute | solution.py:543
  298.0 35.8 %collective-permute-start.20 = (f32[8,128,128]{2,1,0:T(8,128)}, f32[8,128,128]{2,1,0:T(8,128)}, u32[]{:S(2)}, u32[]{:S(2)}) collective-permute-start(f32[8,128,128]{2,1,0:T(8,128)} %get-tuple-element.118), channel_id=1, source_target_pairs={{0,2},{1,3},{2,0},{3,1},{4,6},{5,7},{6,4},{7,5},{8,10},{9,11},{10,... | collective-permute-start | bytes 1572872 | tf_op jit(solution)/shard_map/ppermute | solution.py:543
  299.9 33.9 %collective-permute-start.21 = (f32[8,128,128]{2,1,0:T(8,128)}, f32[8,128,128]{2,1,0:T(8,128)}, u32[]{:S(2)}, u32[]{:S(2)}) collective-permute-start(f32[8,128,128]{2,1,0:T(8,128)} %get-tuple-element.119), channel_id=1, source_target_pairs={{0,3},{1,0},{2,1},{3,2},{4,7},{5,4},{6,5},{7,6},{8,11},{9,8},{10,9... | collective-permute-start | bytes 1572872 | tf_op jit(solution)/shard_map/ppermute | solution.py:543
  308.4 53.7 %all-to-all-start.4 = ((f32[8,2,64,8,128]{4,3,2,1,0:T(8,128)}), f32[8,2,64,8,128]{4,3,2,1,0:T(8,128)}, u32[]{:S(2)}, u32[]{:S(2)}) async-start(f32[8,2,64,8,128]{4,3,2,1,0:T(8,128)} %x_inverse.4.refs_7_), calls=%async_computation.4 | async-start | bytes 8388608 | tf_op jit(solution)/shard_map/all_to_all | solution.py:547
  333.8 41.3 %collective-permute-start.22 = (f32[8,128,128]{2,1,0:T(8,128)}, f32[8,128,128]{2,1,0:T(8,128)}, u32[]{:S(2)}, u32[]{:S(2)}) collective-permute-start(f32[8,128,128]{2,1,0:T(8,128)} %get-tuple-element.120), channel_id=1, source_target_pairs={{0,1},{1,2},{2,3},{3,0},{4,5},{5,6},{6,7},{7,4},{8,9},{9,10},{10,1... | collective-permute-start | bytes 1572872 | tf_op jit(solution)/shard_map/ppermute | solution.py:543
  345.5 35.5 %collective-permute-start.23 = (f32[8,128,128]{2,1,0:T(8,128)}, f32[8,128,128]{2,1,0:T(8,128)}, u32[]{:S(2)}, u32[]{:S(2)}) collective-permute-start(f32[8,128,128]{2,1,0:T(8,128)} %get-tuple-element.121), channel_id=1, source_target_pairs={{0,2},{1,3},{2,0},{3,1},{4,6},{5,7},{6,4},{7,5},{8,10},{9,11},{10,... | collective-permute-start | bytes 1572872 | tf_op jit(solution)/shard_map/ppermute | solution.py:543
  347.0 33.9 %collective-permute-start.24 = (f32[8,128,128]{2,1,0:T(8,128)}, f32[8,128,128]{2,1,0:T(8,128)}, u32[]{:S(2)}, u32[]{:S(2)}) collective-permute-start(f32[8,128,128]{2,1,0:T(8,128)} %get-tuple-element.122), channel_id=1, source_target_pairs={{0,3},{1,0},{2,1},{3,2},{4,7},{5,4},{6,5},{7,6},{8,11},{9,8},{10,9... | collective-permute-start | bytes 1572872 | tf_op jit(solution)/shard_map/ppermute | solution.py:543
  362.1 53.7 %all-to-all-start.5 = ((f32[8,2,64,8,128]{4,3,2,1,0:T(8,128)}), f32[8,2,64,8,128]{4,3,2,1,0:T(8,128)}, u32[]{:S(2)}, u32[]{:S(2)}) async-start(f32[8,2,64,8,128]{4,3,2,1,0:T(8,128)} %gate.22), calls=%async_computation.5 | async-start | bytes 8388608 | tf_op jit(solution)/shard_map/all_to_all | solution.py:547
  381.0 39.2 %collective-permute-start.25 = (f32[8,128,128]{2,1,0:T(8,128)}, f32[8,128,128]{2,1,0:T(8,128)S(1)}, u32[]{:S(2)}, u32[]{:S(2)}) collective-permute-start(f32[8,128,128]{2,1,0:T(8,128)} %get-tuple-element.126), channel_id=1, source_target_pairs={{0,1},{1,2},{2,3},{3,0},{4,5},{5,6},{6,7},{7,4},{8,9},{9,10},{10,1... | collective-permute-start | bytes 1572872 | tf_op jit(solution)/shard_map/ppermute | solution.py:543
  392.7 35.7 %collective-permute-start.26 = (f32[8,128,128]{2,1,0:T(8,128)}, f32[8,128,128]{2,1,0:T(8,128)S(1)}, u32[]{:S(2)}, u32[]{:S(2)}) collective-permute-start(f32[8,128,128]{2,1,0:T(8,128)} %get-tuple-element.127), channel_id=1, source_target_pairs={{0,2},{1,3},{2,0},{3,1},{4,6},{5,7},{6,4},{7,5},{8,10},{9,11},{10,... | collective-permute-start | bytes 1572872 | tf_op jit(solution)/shard_map/ppermute | solution.py:543
  394.6 33.8 %collective-permute-start.27 = (f32[8,128,128]{2,1,0:T(8,128)}, f32[8,128,128]{2,1,0:T(8,128)S(1)}, u32[]{:S(2)}, u32[]{:S(2)}) collective-permute-start(f32[8,128,128]{2,1,0:T(8,128)} %get-tuple-element.128), channel_id=1, source_target_pairs={{0,3},{1,0},{2,1},{3,2},{4,7},{5,4},{6,5},{7,6},{8,11},{9,8},{10,9... | collective-permute-start | bytes 1572872 | tf_op jit(solution)/shard_map/ppermute | solution.py:543
  415.8 31.0 %all-to-all-start.6 = ((f32[8,1,64,8,128]{4,3,2,1,0:T(8,128)}), f32[8,1,64,8,128]{4,3,2,1,0:T(8,128)}, u32[]{:S(2)}, u32[]{:S(2)}) async-start(f32[8,1,64,8,128]{4,3,2,1,0:T(8,128)} %gate.23._), calls=%async_computation.6 | async-start | bytes 4194304 | tf_op jit(solution)/shard_map/all_to_all | solution.py:547
  420.2 8.2 %copy-start.7 = (f32[8,128,128]{2,1,0:T(8,128)}, f32[8,128,128]{2,1,0:T(8,128)S(1)}, u32[]{:S(2)}) copy-start(f32[8,128,128]{2,1,0:T(8,128)S(1)} %collective-permute-done.25.refs_1_._) | copy-start | bytes 1572868
  428.4 0.8 copy-start.8
  429.2 0.8 copy-start.9
  446.8 30.2 %all-to-all-start.7 = ((f32[8,1,64,8,128]{4,3,2,1,0:T(8,128)}), f32[8,1,64,8,128]{4,3,2,1,0:T(8,128)S(1)}, u32[]{:S(2)}, u32[]{:S(2)}) async-start(f32[8,1,64,8,128]{4,3,2,1,0:T(8,128)} %gate.25), calls=%async_computation.7 | async-start | bytes 4194304 | tf_op jit(solution)/shard_map/all_to_all | solution.py:547
  477.0 1.3 copy-start.2
  (1 other events, 0.6 us)

commit v3 on v2

--- a/solution.py
+++ b/solution.py
@@ -566,10 +566,14 @@
     )(*pieces, *before)
 
 
-def swap_y(pieces, before, weight=0):
+def swap_y(pieces, last, before=(), early=True):
     own, *sent = pieces
-    if before:
-        sent = gate(sent, before, weight)
+    if last:
+        cut = 1 if early else len(sent)
+        sent = [
+            *gate(sent[:cut], [*last[1 : 1 + cut], *before]),
+            *(gate(sent[cut:], last[1 + cut :]) if early else ()),
+        ]
     return [own] + [shifted(piece, "gy", s) for s, piece in enumerate(sent, 1)]
 
 
@@ -673,13 +677,13 @@
     f_plain = swap_y(f_plain, f_sloped)
     a_flat = swap_y(a_flat, f_plain)
     f_flat, f_bent = solve(f_plain, f_sloped, a_bent[0])
-    f_flat = swap_y(f_flat, a_flat)
+    f_flat = swap_y(f_flat, a_flat, early=False)
     a_two = x_inverse(me, a_flat, back_joint, count_x, f_flat[0])
-    a_bent = swap_y(a_bent, (*f_flat, a_two))
+    a_bent = swap_y(a_bent, f_flat, (a_two,), False)
     a_two = swap_x(a_two)
     f_two = x_inverse(me, f_flat, back_joint, count_x, a_bent[0])
     adjoint = from_levels(a_two, leave_adjoint, cotangent, (0, 2), False)
-    f_bent = swap_y(f_bent, (*a_bent, adjoint))
+    f_bent = swap_y(f_bent, a_bent, (adjoint,), False)
     f_two = swap_x(*gate([f_two], [a_two]))
     a_one = x_inverse(me, a_bent, back_plain, count_x, f_bent[0], 10)
     (a_one,) = gate([a_one], [f_two])

time: 485 us -> 480 us (0.990)
  waiting for transfers between devices: 178 us -> 147 us
  starting transfers between devices: 134 us -> 160 us
    ppermute x28, waiting for transfers between devices: 74.2 us -> 40.5 us  [shifted(): lax.ppermute(cells, axis, [(i, (i + shift) % count) for i in range(count)])]
    ppermute x28, starting transfers between devices: 98.6 us -> 125 us  [shifted(): lax.ppermute(cells, axis, [(i, (i + shift) % count) for i in range(count)])]
  transfers between devices with their start and end apart: 36 -> 36, of which waited for: 13 -> 12; matrix products, arithmetic and copies ran while one was open for 1% -> 1% of each run, Pallas kernels for 30% -> 31%
where the time goes in v3:
time: 480 us; the launch traced here: 478 us
  starting transfers between devices  160 us (33%)
  Pallas kernels  156 us (32%)
  waiting for transfers between devices  147 us (31%)
  local copies, waits for them, and re-layouts  9.8 us (2%)
    ppermute x28, starting transfers between devices, shifted(): lax.ppermute(cells, axis, [(i, (i + shift) % count) for i in range(count)])  125 us
    all_to_all x8, waiting for transfers between devices, swap_x(): return lax.all_to_all(rows, 'gx', split_axis=0, concat_axis=0, tiled=True)  106 us
    ppermute x28, waiting for transfers between devices, shifted(): lax.ppermute(cells, axis, [(i, (i + shift) % count) for i in range(count)])  40.5 us
    all_to_all x8, starting transfers between devices, swap_x(): return lax.all_to_all(rows, 'gx', split_axis=0, concat_axis=0, tiled=True)  35 us
    pallas_call x2, Pallas kernels, y_solve(): pl.pallas_call(functools.partial(solve_kernel, sources, full), grid=(leve...  29.3 us
    pallas_call x4, Pallas kernels, x_inverse(): pl.pallas_call(functools.partial(x_inverse_kernel, sources), grid=(count,...  27.2 us
    pallas_call x2, Pallas kernels, make_section(): pl.pallas_call(section_kernel, grid=(count, part_x // sublanes), in_specs...  25.4 us
    pallas_call x4, Pallas kernels, x_forward(): pl.pallas_call(x_kernel, grid=(levels // block,), in_specs=[scalars, pl.B...  24.4 us
  transfers between devices with their start and end apart: 36, of which 12 were waited for; matrix products, arithmetic and copies ran while one was open for 1% of the time, Pallas kernels for 31%

profile of v3, /device:TPU:0, one launch (start us, length us, event | category | flops | bytes accessed | tf_op | source)
XLA Modules:
  0.0 477.7 jit_solution(14169139512342968451)
XLA Ops:
  2.2 4.4 into_levels.2._.refs_0_
  6.6 5.2 %all-to-all-start = ((f32[8,1,8,64,128]{4,3,2,1,0:T(8,128)}), f32[8,1,8,64,128]{4,3,2,1,0:T(8,128)S(1)}, u32[]{:S(2)}, u32[]{:S(2)}) async-start(f32[8,1,8,64,128]{4,3,2,1,0:T(8,128)} %into_levels.2._.refs_0_), calls=%async_computation | async-start | bytes 4194304 | tf_op jit(solution)/shard_map/all_to_all | solution.py:547
  11.8 6.8 %edges_of.1 = (f32[3,64,64]{2,1,0:T(8,128)}, f32[3,64,64]{2,1,0:T(8,128)}, f32[3,1,64,128]{3,2,1,0:T(8,128)}, f32[3,1,64,128]{3,2,1,0:T(8,128)}) custom-call(f32[3,64,64,128]{3,2,1,0:T(8,128)} %refs_3_.3, f32[8,1,8,64,128]{4,3,2,1,0:T(8,128)} %into_levels.2._.refs_0_), custom_call_target="tpu_custom_call" | custom-call | bytes 629145600 | tf_op jit(solution)/shard_map/edges_of/pallas_call | solution.py:158
  29.7 7.7 %into_levels.3.refs_0_ = f32[8,2,8,64,128]{4,3,2,1,0:T(8,128)} custom-call(f32[3,64,64,128]{3,2,1,0:T(8,128)} %base_ref.3, bf16[2,64,192]{2,1,0:T(8,128)(2,1)} %pad_maximum_fusion.3.matrix_ref, f32[8,1,8,64,128]{4,3,2,1,0:T(8,128)} %into_levels.2._.refs_0_, bf16[2,64,192]{2,1,0:T(8,128)(2,1)} %get-tuple-element.137.refs_11_.refs_1_, ...), custom_call_target="tpu_custom_call" | custom-call | flops 40265318400 | bytes 838860800 | tf_op jit(solution)/shard_map/into_levels/pallas_call | solution.py:112
  40.2 4.6 all-to-all-start.1
  45.5 5.1 %x_forward.4 = (f32[8,128,128]{2,1,0:T(8,128)}, f32[8,128,128]{2,1,0:T(8,128)}, f32[8,128,128]{2,1,0:T(8,128)}, f32[8,128,128]{2,1,0:T(8,128)}) custom-call(s32[1]{0:T(128)} %bitcast.me_ref.group_ref, f32[8,1,8,64,128]{4,3,2,1,0:T(8,128)} %copy-done, bf16[2,4,128,512]{3,2,1,0:T(8,128)(2,1)} %constant.29.clone.table_ref, f32[3,1,64,128]{3,2,1,0:T(8,128)} %copy-done.10, ...), custom_call_target="tpu_custom_call" | custom-call | flops 161061273600 | bytes 524288000 | tf_op jit(solution)/shard_map/x_forward/pallas_call | solution.py:325
  56.1 9.1 %make_section.2 = (f32[3,64,64,128]{3,2,1,0:T(8,128)}, f32[3,64,64,128]{3,2,1,0:T(8,128)}, f32[8,1,8,64,128]{4,3,2,1,0:T(8,128)}) custom-call(f32[3,64,64,128]{3,2,1,0:T(8,128)} %refs_3_.3, f32[3,64,64,128]{3,2,1,0:T(8,128)} %refs_3_.3, f32[3,64,64,128]{3,2,1,0:T(8,128)} %refs_3_.3, f32[3,64,64,128]{3,2,1,0:T(8,128)} %refs_3_.3, ...), custom_call_target="tpu_custom_call" | custom-call | flops 40265318400 | bytes 1887436800 | tf_op jit(solution)/shard_map/make_section/pallas_call | solution.py:237
  65.2 16.3 %make_section.3 = (f32[3,64,64,128]{3,2,1,0:T(8,128)}, f32[3,64,64,128]{3,2,1,0:T(8,128)}, f32[8,2,8,64,128]{4,3,2,1,0:T(8,128)}) custom-call(f32[3,64,64,128]{3,2,1,0:T(8,128)} %refs_3_.3, f32[3,64,64,128]{3,2,1,0:T(8,128)} %refs_3_.3, f32[3,64,64,128]{3,2,1,0:T(8,128)} %refs_3_.3, ...), custom_call_target="tpu_custom_call", output_to_operand_aliasing={{0}: (12, {}), {1}: (13, {})} | custom-call | flops 80530636800 | bytes 3774873600 | tf_op jit(solution)/shard_map/make_section/pallas_call | solution.py:237
  81.5 12.4 %all-to-all-done.1.rows_ref = f32[8,2,8,64,128]{4,3,2,1,0:T(8,128)} async-done(((f32[8,2,8,64,128]{4,3,2,1,0:T(8,128)}), f32[8,2,8,64,128]{4,3,2,1,0:T(8,128)}, u32[]{:S(2)}, u32[]{:S(2)}) %all-to-all-start.1) | async-done | bytes 4194336 | tf_op jit(solution)/shard_map/all_to_all | solution.py:547
  93.9 7.1 %x_forward.5 = (f32[8,128,128]{2,1,0:T(8,128)}, f32[8,128,128]{2,1,0:T(8,128)}, f32[8,128,128]{2,1,0:T(8,128)}, f32[8,128,128]{2,1,0:T(8,128)}) custom-call(s32[1]{0:T(128)} %bitcast.me_ref.group_ref, f32[8,2,8,64,128]{4,3,2,1,0:T(8,128)} %all-to-all-done.1.rows_ref, bf16[2,4,128,1024]{3,2,1,0:T(8,128)(2,1)} %constant.30.clone.table_ref, ...), custom_call_target="tpu_custom_call" | custom-call | flops 322122547200 | bytes 838860800 | tf_op jit(solution)/shard_map/x_forward/pallas_call | solution.py:325
  101.0 3.6 all-to-all-start.2
  110.0 21.3 %all-to-all-done.2.refs_1_.rows_ref = f32[8,1,8,64,128]{4,3,2,1,0:T(8,128)S(1)} async-done(((f32[8,1,8,64,128]{4,3,2,1,0:T(8,128)}), f32[8,1,8,64,128]{4,3,2,1,0:T(8,128)S(1)}, u32[]{:S(2)}, u32[]{:S(2)}) %all-to-all-start.2) | async-done | bytes 2097184 | tf_op jit(solution)/shard_map/all_to_all | solution.py:547
  132.5 4.6 all-to-all-start.3
  137.1 5.1 %x_forward.7 = (f32[8,128,128]{2,1,0:T(8,128)}, f32[8,128,128]{2,1,0:T(8,128)}, f32[8,128,128]{2,1,0:T(8,128)}, f32[8,128,128]{2,1,0:T(8,128)}) custom-call(s32[1]{0:T(128)} %bitcast.me_ref.group_ref, f32[8,1,8,64,128]{4,3,2,1,0:T(8,128)} %copy-done.1, bf16[2,4,128,512]{3,2,1,0:T(8,128)(2,1)} %constant.29.clone.table_ref, ...), custom_call_target="tpu_custom_call" | custom-call | flops 161061273600 | bytes 524288000 | tf_op jit(solution)/shard_map/x_forward/pallas_call | solution.py:325
  142.3 11.8 %collective-permute-start.12 = (f32[8,128,128]{2,1,0:T(8,128)}, f32[8,128,128]{2,1,0:T(8,128)}, u32[]{:S(2)}, u32[]{:S(2)}) collective-permute-start(f32[8,128,128]{2,1,0:T(8,128)} %get-tuple-element.90), channel_id=1, source_target_pairs={{0,2},{1,3},{2,0},{3,1},{4,6},{5,7},{6,4},{7,5},{8,10},{9,11},{10,... | collective-permute-start | bytes 1572872 | tf_op jit(solution)/shard_map/ppermute | solution.py:543
  154.0 3.4 collective-permute-start.13
  157.4 28.8 %all-to-all-done.3.rows_ref = f32[8,2,8,64,128]{4,3,2,1,0:T(8,128)} async-done(((f32[8,2,8,64,128]{4,3,2,1,0:T(8,128)}), f32[8,2,8,64,128]{4,3,2,1,0:T(8,128)}, u32[]{:S(2)}, u32[]{:S(2)}) %all-to-all-start.3) | async-done | bytes 4194336 | tf_op jit(solution)/shard_map/all_to_all | solution.py:547
  186.2 7.1 %x_forward.6 = (f32[8,128,128]{2,1,0:T(8,128)}, f32[8,128,128]{2,1,0:T(8,128)}, f32[8,128,128]{2,1,0:T(8,128)}, f32[8,128,128]{2,1,0:T(8,128)}) custom-call(s32[1]{0:T(128)} %bitcast.me_ref.group_ref, f32[8,2,8,64,128]{4,3,2,1,0:T(8,128)} %all-to-all-done.3.rows_ref, bf16[2,4,128,1024]{3,2,1,0:T(8,128)(2,1)} %constant.30.clone.table_ref, ...), custom_call_target="tpu_custom_call" | custom-call | flops 322122547200 | bytes 838860800 | tf_op jit(solution)/shard_map/x_forward/pallas_call | solution.py:325
  193.3 6.2 %collective-permute-start.14 = (f32[8,128,128]{2,1,0:T(8,128)}, f32[8,128,128]{2,1,0:T(8,128)}, u32[]{:S(2)}, u32[]{:S(2)}) collective-permute-start(f32[8,128,128]{2,1,0:T(8,128)} %get-tuple-element.92), channel_id=1, source_target_pairs={{0,2},{1,3},{2,0},{3,1},{4,6},{5,7},{6,4},{7,5},{8,10},{9,11},{10,... | collective-permute-start | bytes 1572872 | tf_op jit(solution)/shard_map/ppermute | solution.py:543
  199.5 3.4 collective-permute-start.15
  202.9 14.7 %y_solve.2 = (f32[8,128,128]{2,1,0:T(8,128)}, f32[8,128,128]{2,1,0:T(8,128)}, f32[8,128,128]{2,1,0:T(8,128)}, f32[8,128,128]{2,1,0:T(8,128)}, f32[8,128,128]{2,1...) custom-call(s32[1]{0:T(128)} %bitcast.me_ref.group_ref, ...), custom_call_target="tpu_custom_call" | custom-call | flops 644245094400 | bytes 1258291200 | tf_op jit(solution)/shard_map/y_solve/pallas_call | solution.py:385
  217.6 7.5 %collective-permute-done.14.refs_2_ = f32[8,128,128]{2,1,0:T(8,128)} collective-permute-done((f32[8,128,128]{2,1,0:T(8,128)}, f32[8,128,128]{2,1,0:T(8,128)}, u32[]{:S(2)}, u32[]{:S(2)}) %collective-permute-start.14) | collective-permute-done | bytes 524320 | tf_op jit(solution)/shard_map/ppermute | solution.py:543
  225.1 19.9 %collective-permute-start.17 = (f32[8,128,128]{2,1,0:T(8,128)}, f32[8,128,128]{2,1,0:T(8,128)}, u32[]{:S(2)}, u32[]{:S(2)}) collective-permute-start(f32[8,128,128]{2,1,0:T(8,128)} %get-tuple-element.105), channel_id=1, source_target_pairs={{0,2},{1,3},{2,0},{3,1},{4,6},{5,7},{6,4},{7,5},{8,10},{9,11},{10,... | collective-permute-start | bytes 1572872 | tf_op jit(solution)/shard_map/ppermute | solution.py:543
  245.1 3.4 collective-permute-start.18
  248.4 19.6 %collective-permute-start.16 = (f32[8,128,128]{2,1,0:T(8,128)}, f32[8,128,128]{2,1,0:T(8,128)}, u32[]{:S(2)}, u32[]{:S(2)}) collective-permute-start(f32[8,128,128]{2,1,0:T(8,128)} %gate.26), channel_id=1, source_target_pairs={{0,1},{1,2},{2,3},{3,0},{4,5},{5,6},{6,7},{7,4},{8,9},{9,10},{10,1... | collective-permute-start | bytes 1572872 | tf_op jit(solution)/shard_map/ppermute | solution.py:543
  268.0 14.6 %y_solve.3 = (f32[8,128,128]{2,1,0:T(8,128)}, f32[8,128,128]{2,1,0:T(8,128)}, f32[8,128,128]{2,1,0:T(8,128)}, f32[8,128,128]{2,1,0:T(8,128)}, f32[8,128,128]{2,1...) custom-call(s32[1]{0:T(128)} %bitcast.me_ref.group_ref, ...), custom_call_target="tpu_custom_call" | custom-call | flops 644245094400 | bytes 1258291200 | tf_op jit(solution)/shard_map/y_solve/pallas_call | solution.py:385
  282.7 7.6 %collective-permute-start.19 = (f32[8,128,128]{2,1,0:T(8,128)}, f32[8,128,128]{2,1,0:T(8,128)}, u32[]{:S(2)}, u32[]{:S(2)}) collective-permute-start(f32[8,128,128]{2,1,0:T(8,128)} %get-tuple-element.107), channel_id=1, source_target_pairs={{0,1},{1,2},{2,3},{3,0},{4,5},{5,6},{6,7},{7,4},{8,9},{9,10},{10,1... | collective-permute-start | bytes 1572872 | tf_op jit(solution)/shard_map/ppermute | solution.py:543
  295.1 8.1 %x_inverse.4.refs_6_ = f32[8,2,64,8,128]{4,3,2,1,0:T(8,128)} custom-call(s32[1]{0:T(128)} %bitcast.me_ref.group_ref, f32[8,128,128]{2,1,0:T(8,128)} %get-tuple-element.110._.refs_0_, f32[8,128,128]{2,1,0:T(8,128)} %get-tuple-element.111.refs_0_, f32[8,128,128]{2,1,0:T(8,128)} %collective-permute-done.16.refs_3_.refs_1_, ...), custom_call_target="tpu_custom_call" | custom-call | flops 322122547200 | bytes 838860800 | tf_op jit(solution)/shard_map/x_inverse/pallas_call | solution.py:437
  303.2 4.6 all-to-all-start.4
  307.8 20.3 %collective-permute-done.20.refs_4_.refs_2_ = f32[8,128,128]{2,1,0:T(8,128)} collective-permute-done((f32[8,128,128]{2,1,0:T(8,128)}, f32[8,128,128]{2,1,0:T(8,128)}, u32[]{:S(2)}, u32[]{:S(2)}) %collective-permute-start.20) | collective-permute-done | bytes 524320 | tf_op jit(solution)/shard_map/ppermute | solution.py:543
  328.1 11.7 %collective-permute-start.22 = (f32[8,128,128]{2,1,0:T(8,128)}, f32[8,128,128]{2,1,0:T(8,128)}, u32[]{:S(2)}, u32[]{:S(2)}) collective-permute-start(f32[8,128,128]{2,1,0:T(8,128)} %get-tuple-element.112), channel_id=1, source_target_pairs={{0,1},{1,2},{2,3},{3,0},{4,5},{5,6},{6,7},{7,4},{8,9},{9,10},{10,1... | collective-permute-start | bytes 1572872 | tf_op jit(solution)/shard_map/ppermute | solution.py:543
  342.2 8.1 %x_inverse.6.refs_0_ = f32[8,2,64,8,128]{4,3,2,1,0:T(8,128)} custom-call(s32[1]{0:T(128)} %bitcast.me_ref.group_ref, f32[8,128,128]{2,1,0:T(8,128)} %get-tuple-element.83._.refs_0_, f32[8,128,128]{2,1,0:T(8,128)} %get-tuple-element.110._.refs_0_, f32[8,128,128]{2,1,0:T(8,128)} %collective-permute-done.19.refs_3_.refs_1_, ...), custom_call_target="tpu_custom_call" | custom-call | flops 322122547200 | bytes 838860800 | tf_op jit(solution)/shard_map/x_inverse/pallas_call | solution.py:437
  350.3 6.6 %all-to-all-done.4.refs_1_.rows_ref = f32[8,2,64,8,128]{4,3,2,1,0:T(8,128)} async-done(((f32[8,2,64,8,128]{4,3,2,1,0:T(8,128)}), f32[8,2,64,8,128]{4,3,2,1,0:T(8,128)}, u32[]{:S(2)}, u32[]{:S(2)}) %all-to-all-start.4) | async-done | bytes 4194336 | tf_op jit(solution)/shard_map/all_to_all | solution.py:547
  356.9 4.6 all-to-all-start.5
  361.5 8.4 %from_levels.3.refs_6_.done_ref = f32[3,64,64,128]{3,2,1,0:T(8,128)} custom-call(f32[8,2,64,8,128]{4,3,2,1,0:T(8,128)} %all-to-all-done.4.refs_1_.rows_ref, bf16[2,64,192]{2,1,0:T(8,128)(2,1)} %get-tuple-element.138.refs_2_.matrix_ref, f32[3,64,64,128]{3,2,1,0:T(8,128)} %base_ref.3), custom_call_target="tpu_custom_call" | custom-call | flops 40265318400 | bytes 1258291200 | tf_op jit(solution)/shard_map/from_levels/pallas_call | solution.py:478
  369.9 4.9 %collective-permute-done.23.refs_2_.refs_4_ = f32[8,128,128]{2,1,0:T(8,128)} collective-permute-done((f32[8,128,128]{2,1,0:T(8,128)}, f32[8,128,128]{2,1,0:T(8,128)}, u32[]{:S(2)}, u32[]{:S(2)}) %collective-permute-start.23) | collective-permute-done | bytes 524320 | tf_op jit(solution)/shard_map/ppermute | solution.py:543
  374.8 11.7 %collective-permute-start.25 = (f32[8,128,128]{2,1,0:T(8,128)}, f32[8,128,128]{2,1,0:T(8,128)S(1)}, u32[]{:S(2)}, u32[]{:S(2)}) collective-permute-start(f32[8,128,128]{2,1,0:T(8,128)} %get-tuple-element.118), channel_id=1, source_target_pairs={{0,1},{1,2},{2,3},{3,0},{4,5},{5,6},{6,7},{7,4},{8,9},{9,10},{10,1... | collective-permute-start | bytes 1572872 | tf_op jit(solution)/shard_map/ppermute | solution.py:543
  388.9 5.5 %x_inverse.5.refs_0_ = f32[8,1,64,8,128]{4,3,2,1,0:T(8,128)} custom-call(s32[1]{0:T(128)} %bitcast.me_ref.group_ref, f32[8,128,128]{2,1,0:T(8,128)} %get-tuple-element.95._.refs_0_, f32[8,128,128]{2,1,0:T(8,128)} %get-tuple-element.83._.refs_0_, f32[8,128,128]{2,1,0:T(8,128)} %collective-permute-done.22.refs_1_.refs_3_, ...), custom_call_target="tpu_custom_call" | custom-call | flops 16106127360 | bytes 52428800 | tf_op jit(solution)/shard_map/x_inverse/pallas_call | solution.py:437
  394.4 16.2 %all-to-all-done.5.refs_1_.rows_ref = f32[8,2,64,8,128]{4,3,2,1,0:T(8,128)} async-done(((f32[8,2,64,8,128]{4,3,2,1,0:T(8,128)}), f32[8,2,64,8,128]{4,3,2,1,0:T(8,128)}, u32[]{:S(2)}, u32[]{:S(2)}) %all-to-all-start.5) | async-done | bytes 4194336 | tf_op jit(solution)/shard_map/all_to_all | solution.py:547
  410.6 4.4 all-to-all-start.6
  415.0 7.7 %collective-permute-done.26.refs_2_ = f32[8,128,128]{2,1,0:T(8,128)S(1)} collective-permute-done((f32[8,128,128]{2,1,0:T(8,128)}, f32[8,128,128]{2,1,0:T(8,128)S(1)}, u32[]{:S(2)}, u32[]{:S(2)}) %collective-permute-start.26) | collective-permute-done | bytes 524320 | tf_op jit(solution)/shard_map/ppermute | solution.py:543
  424.3 5.5 %x_inverse.7.refs_0_ = f32[8,1,64,8,128]{4,3,2,1,0:T(8,128)} custom-call(s32[1]{0:T(128)} %bitcast.me_ref.group_ref, f32[8,1,64,8,128]{4,3,2,1,0:T(8,128)} %gate.31._, f32[8,128,128]{2,1,0:T(8,128)} %get-tuple-element.95._.refs_0_, f32[8,128,128]{2,1,0:T(8,128)} %copy-done.7, f32[8,128,128]{2,1,0:T(8,128)} %copy-done.8, f32[8,128,128]{2,1,0:T(8,128)} %copy-done.9, ...), custom_call_target="tpu_custom_call" | custom-call | flops 161061273600 | bytes 524288000 | tf_op jit(solution)/shard_map/x_inverse/pallas_call | solution.py:437
  429.8 11.8 %all-to-all-done.6.refs_1_.refs_0_.rows_ref = f32[8,1,64,8,128]{4,3,2,1,0:T(8,128)} async-done(((f32[8,1,64,8,128]{4,3,2,1,0:T(8,128)}), f32[8,1,64,8,128]{4,3,2,1,0:T(8,128)}, u32[]{:S(2)}, u32[]{:S(2)}) %all-to-all-start.6) | async-done | bytes 2097184 | tf_op jit(solution)/shard_map/all_to_all | solution.py:547
  441.6 3.6 all-to-all-start.7
  445.2 8.4 %from_levels.4.base_ref = f32[3,64,64,128]{3,2,1,0:T(8,128)} custom-call(f32[8,2,64,8,128]{4,3,2,1,0:T(8,128)} %all-to-all-done.5.refs_1_.rows_ref, bf16[2,64,192]{2,1,0:T(8,128)(2,1)} %pad_maximum_fusion.6.refs_3_.matrix_ref, f32[3,64,64,128]{3,2,1,0:T(8,128)} %get-tuple-element.121.base_ref, ...), custom_call_target="tpu_custom_call", output_to_operand_aliasing={{}: (2, {})} | custom-call | flops 40265318400 | bytes 1258291200 | tf_op jit(solution)/shard_map/from_levels/pallas_call | solution.py:478
  453.6 9.3 %gradient_of.1 = (f32[3,64,64,128]{3,2,1,0:T(8,128)}, f32[64,64,128]{2,1,0:T(8,128)}) custom-call(f32[8,1,64,8,128]{4,3,2,1,0:T(8,128)} %all-to-all-done.6.refs_1_.refs_0_.rows_ref, bf16[2,64,192]{2,1,0:T(8,128)(2,1)} %get-tuple-element.138.refs_2_.matrix_ref, f32[3,64,64,128]{3,2,1,0:T(8,128)} %base_ref.3, ...), custom_call_target="tpu_custom_call", output_to_operand_aliasing={{0}: (3, {})} | custom-call | flops 20132659200 | bytes 1887436800 | tf_op jit(solution)/shard_map/gradient_of/pallas_call | solution.py:518
  463.0 8.9 %all-to-all-done.7.rows_ref = f32[8,1,64,8,128]{4,3,2,1,0:T(8,128)S(1)} async-done(((f32[8,1,64,8,128]{4,3,2,1,0:T(8,128)}), f32[8,1,64,8,128]{4,3,2,1,0:T(8,128)S(1)}, u32[]{:S(2)}, u32[]{:S(2)}) %all-to-all-start.7) | async-done | bytes 2097184 | tf_op jit(solution)/shard_map/all_to_all | solution.py:547
  473.1 4.6 from_levels.5
  (108 shorter events, 40.7 us)
Async XLA Ops:
  6.6 32.3 %all-to-all-start = ((f32[8,1,8,64,128]{4,3,2,1,0:T(8,128)}), f32[8,1,8,64,128]{4,3,2,1,0:T(8,128)S(1)}, u32[]{:S(2)}, u32[]{:S(2)}) async-start(f32[8,1,8,64,128]{4,3,2,1,0:T(8,128)} %into_levels.2._.refs_0_), calls=%async_computation | async-start | bytes 4194304 | tf_op jit(solution)/shard_map/all_to_all | solution.py:547
  11.8 13.3 %copy-start.4 = (f32[64,64]{1,0:T(8,128)S(1)}, f32[64,64]{1,0:T(8,128)}, u32[]{:S(2)}) copy-start(f32[64,64]{1,0:T(8,128)} %param.20) | copy-start | bytes 49156
  11.8 13.4 %copy-start.3 = (f32[64,64]{1,0:T(8,128)S(1)}, f32[64,64]{1,0:T(8,128)}, u32[]{:S(2)}) copy-start(f32[64,64]{1,0:T(8,128)} %param.18) | copy-start | bytes 49156
  11.8 13.8 %copy-start.5 = (f32[64,64]{1,0:T(8,128)S(1)}, f32[64,64]{1,0:T(8,128)}, u32[]{:S(2)}) copy-start(f32[64,64]{1,0:T(8,128)} %param.19) | copy-start | bytes 49156
  11.8 17.2 %copy-start.6 = (f32[64]{0:T(128)S(1)}, f32[64]{0:T(128)}, u32[]{:S(2)}) copy-start(f32[64]{0:T(128)} %param.17) | copy-start | bytes 772
  18.6 18.8 %collective-permute-start.2 = (f32[3,64,64]{2,1,0:T(8,128)}, f32[3,64,64]{2,1,0:T(8,128)S(1)}, u32[]{:S(2)}, u32[]{:S(2)}) collective-permute-start(f32[3,64,64]{2,1,0:T(8,128)} %get-tuple-element.66), channel_id=1, source_target_pairs={{0,1},{1,2},{2,3},{3,0},{4,5},{5,6},{6,7},{7,4},{8,9},{9,10},{10,1... | collective-permute-start | bytes 147464 | tf_op jit(solution)/shard_map/ppermute | solution.py:543
  20.2 17.9 %collective-permute-start.3 = (f32[3,64,64]{2,1,0:T(8,128)}, f32[3,64,64]{2,1,0:T(8,128)S(1)}, u32[]{:S(2)}, u32[]{:S(2)}) collective-permute-start(f32[3,64,64]{2,1,0:T(8,128)} %get-tuple-element.67), channel_id=1, source_target_pairs={{0,3},{1,0},{2,1},{3,2},{4,7},{5,4},{6,5},{7,6},{8,11},{9,8},{10,9... | collective-permute-start | bytes 147464 | tf_op jit(solution)/shard_map/ppermute | solution.py:543
  22.4 22.3 %collective-permute-start = (f32[3,1,64,128]{3,2,1,0:T(8,128)}, f32[3,1,64,128]{3,2,1,0:T(8,128)S(1)}, u32[]{:S(2)}, u32[]{:S(2)}) collective-permute-start(f32[3,1,64,128]{3,2,1,0:T(8,128)} %get-tuple-element.64), channel_id=1, source_target_pairs={{0,4},{4,8},{8,12},{12,16},{16,20},{20,24},{24,28},{28,0},{1,5},{5... | collective-permute-start | bytes 294920 | tf_op jit(solution)/shard_map/ppermute | solution.py:543
  22.4 22.3 %collective-permute-start.1 = (f32[3,1,64,128]{3,2,1,0:T(8,128)}, f32[3,1,64,128]{3,2,1,0:T(8,128)S(1)}, u32[]{:S(2)}, u32[]{:S(2)}) collective-permute-start(f32[3,1,64,128]{3,2,1,0:T(8,128)} %get-tuple-element.65), channel_id=1, source_target_pairs={{0,28},{4,0},{8,4},{12,8},{16,12},{20,16},{24,20},{28,24},{1,29},{... | collective-permute-start | bytes 294920 | tf_op jit(solution)/shard_map/ppermute | solution.py:543
  38.9 1.3 copy-start
  40.2 53.7 %all-to-all-start.1 = ((f32[8,2,8,64,128]{4,3,2,1,0:T(8,128)}), f32[8,2,8,64,128]{4,3,2,1,0:T(8,128)}, u32[]{:S(2)}, u32[]{:S(2)}) async-start(f32[8,2,8,64,128]{4,3,2,1,0:T(8,128)} %gate.17), calls=%async_computation.1 | async-start | bytes 8388608 | tf_op jit(solution)/shard_map/all_to_all | solution.py:547
  44.8 0.7 copy-start.11
  50.6 50.4 %collective-permute-start.4 = (f32[8,128,128]{2,1,0:T(8,128)}, f32[8,128,128]{2,1,0:T(8,128)}, u32[]{:S(2)}, u32[]{:S(2)}) collective-permute-start(f32[8,128,128]{2,1,0:T(8,128)} %get-tuple-element.74), channel_id=1, source_target_pairs={{0,1},{1,2},{2,3},{3,0},{4,5},{5,6},{6,7},{7,4},{8,9},{9,10},{10,1... | collective-permute-start | bytes 1572872 | tf_op jit(solution)/shard_map/ppermute | solution.py:543
  52.2 48.8 %collective-permute-start.5 = (f32[8,128,128]{2,1,0:T(8,128)}, f32[8,128,128]{2,1,0:T(8,128)}, u32[]{:S(2)}, u32[]{:S(2)}) collective-permute-start(f32[8,128,128]{2,1,0:T(8,128)} %get-tuple-element.75), channel_id=1, source_target_pairs={{0,2},{1,3},{2,0},{3,1},{4,6},{5,7},{6,4},{7,5},{8,10},{9,11},{10,... | collective-permute-start | bytes 1572872 | tf_op jit(solution)/shard_map/ppermute | solution.py:543
  54.8 46.2 %collective-permute-start.6 = (f32[8,128,128]{2,1,0:T(8,128)}, f32[8,128,128]{2,1,0:T(8,128)}, u32[]{:S(2)}, u32[]{:S(2)}) collective-permute-start(f32[8,128,128]{2,1,0:T(8,128)} %get-tuple-element.76), channel_id=1, source_target_pairs={{0,3},{1,0},{2,1},{3,2},{4,7},{5,4},{6,5},{7,6},{8,11},{9,8},{10,9... | collective-permute-start | bytes 1572872 | tf_op jit(solution)/shard_map/ppermute | solution.py:543
  101.0 3.7 copy-start.12
  101.0 30.2 %all-to-all-start.2 = ((f32[8,1,8,64,128]{4,3,2,1,0:T(8,128)}), f32[8,1,8,64,128]{4,3,2,1,0:T(8,128)S(1)}, u32[]{:S(2)}, u32[]{:S(2)}) async-start(f32[8,1,8,64,128]{4,3,2,1,0:T(8,128)} %gate.18), calls=%async_computation.2 | async-start | bytes 4194304 | tf_op jit(solution)/shard_map/all_to_all | solution.py:547
  105.3 36.9 %collective-permute-start.8 = (f32[8,128,128]{2,1,0:T(8,128)}, f32[8,128,128]{2,1,0:T(8,128)}, u32[]{:S(2)}, u32[]{:S(2)}) collective-permute-start(f32[8,128,128]{2,1,0:T(8,128)} %get-tuple-element.80), channel_id=1, source_target_pairs={{0,2},{1,3},{2,0},{3,1},{4,6},{5,7},{6,4},{7,5},{8,10},{9,11},{10,... | collective-permute-start | bytes 1572872 | tf_op jit(solution)/shard_map/ppermute | solution.py:543
  107.9 34.3 %collective-permute-start.9 = (f32[8,128,128]{2,1,0:T(8,128)}, f32[8,128,128]{2,1,0:T(8,128)}, u32[]{:S(2)}, u32[]{:S(2)}) collective-permute-start(f32[8,128,128]{2,1,0:T(8,128)} %get-tuple-element.81), channel_id=1, source_target_pairs={{0,3},{1,0},{2,1},{3,2},{4,7},{5,4},{6,5},{7,6},{8,11},{9,8},{10,9... | collective-permute-start | bytes 1572872 | tf_op jit(solution)/shard_map/ppermute | solution.py:543
  109.3 48.1 %collective-permute-start.7 = (f32[8,128,128]{2,1,0:T(8,128)}, f32[8,128,128]{2,1,0:T(8,128)}, u32[]{:S(2)}, u32[]{:S(2)}) collective-permute-start(f32[8,128,128]{2,1,0:T(8,128)} %gate.20), channel_id=1, source_target_pairs={{0,1},{1,2},{2,3},{3,0},{4,5},{5,6},{6,7},{7,4},{8,9},{9,10},{10,1... | collective-permute-start | bytes 1572872 | tf_op jit(solution)/shard_map/ppermute | solution.py:543
  131.2 1.3 copy-start.1
  132.5 53.7 %all-to-all-start.3 = ((f32[8,2,8,64,128]{4,3,2,1,0:T(8,128)}), f32[8,2,8,64,128]{4,3,2,1,0:T(8,128)}, u32[]{:S(2)}, u32[]{:S(2)}) async-start(f32[8,2,8,64,128]{4,3,2,1,0:T(8,128)} %gate.19), calls=%async_computation.3 | async-start | bytes 8388608 | tf_op jit(solution)/shard_map/all_to_all | solution.py:547
  142.3 51.1 %collective-permute-start.12 = (f32[8,128,128]{2,1,0:T(8,128)}, f32[8,128,128]{2,1,0:T(8,128)}, u32[]{:S(2)}, u32[]{:S(2)}) collective-permute-start(f32[8,128,128]{2,1,0:T(8,128)} %get-tuple-element.90), channel_id=1, source_target_pairs={{0,2},{1,3},{2,0},{3,1},{4,6},{5,7},{6,4},{7,5},{8,10},{9,11},{10,... | collective-permute-start | bytes 1572872 | tf_op jit(solution)/shard_map/ppermute | solution.py:543
  154.0 39.3 %collective-permute-start.13 = (f32[8,128,128]{2,1,0:T(8,128)}, f32[8,128,128]{2,1,0:T(8,128)}, u32[]{:S(2)}, u32[]{:S(2)}) collective-permute-start(f32[8,128,128]{2,1,0:T(8,128)} %get-tuple-element.91), channel_id=1, source_target_pairs={{0,3},{1,0},{2,1},{3,2},{4,7},{5,4},{6,5},{7,6},{8,11},{9,8},{10,9... | collective-permute-start | bytes 1572872 | tf_op jit(solution)/shard_map/ppermute | solution.py:543
  157.4 45.5 %collective-permute-start.10 = (f32[8,128,128]{2,1,0:T(8,128)}, f32[8,128,128]{2,1,0:T(8,128)}, u32[]{:S(2)}, u32[]{:S(2)}) collective-permute-start(f32[8,128,128]{2,1,0:T(8,128)} %gate.22), channel_id=1, source_target_pairs={{0,1},{1,2},{2,3},{3,0},{4,5},{5,6},{6,7},{7,4},{8,9},{9,10},{10,1... | collective-permute-start | bytes 1572872 | tf_op jit(solution)/shard_map/ppermute | solution.py:543
  193.3 31.8 %collective-permute-start.14 = (f32[8,128,128]{2,1,0:T(8,128)}, f32[8,128,128]{2,1,0:T(8,128)}, u32[]{:S(2)}, u32[]{:S(2)}) collective-permute-start(f32[8,128,128]{2,1,0:T(8,128)} %get-tuple-element.92), channel_id=1, source_target_pairs={{0,2},{1,3},{2,0},{3,1},{4,6},{5,7},{6,4},{7,5},{8,10},{9,11},{10,... | collective-permute-start | bytes 1572872 | tf_op jit(solution)/shard_map/ppermute | solution.py:543
  199.5 25.6 %collective-permute-start.15 = (f32[8,128,128]{2,1,0:T(8,128)}, f32[8,128,128]{2,1,0:T(8,128)}, u32[]{:S(2)}, u32[]{:S(2)}) collective-permute-start(f32[8,128,128]{2,1,0:T(8,128)} %get-tuple-element.93), channel_id=1, source_target_pairs={{0,3},{1,0},{2,1},{3,2},{4,7},{5,4},{6,5},{7,6},{8,11},{9,8},{10,9... | collective-permute-start | bytes 1572872 | tf_op jit(solution)/shard_map/ppermute | solution.py:543
  202.9 45.5 %collective-permute-start.11 = (f32[8,128,128]{2,1,0:T(8,128)}, f32[8,128,128]{2,1,0:T(8,128)}, u32[]{:S(2)}, u32[]{:S(2)}) collective-permute-start(f32[8,128,128]{2,1,0:T(8,128)} %gate.23), channel_id=1, source_target_pairs={{0,1},{1,2},{2,3},{3,0},{4,5},{5,6},{6,7},{7,4},{8,9},{9,10},{10,1... | collective-permute-start | bytes 1572872 | tf_op jit(solution)/shard_map/ppermute | solution.py:543
  225.1 57.6 %collective-permute-start.17 = (f32[8,128,128]{2,1,0:T(8,128)}, f32[8,128,128]{2,1,0:T(8,128)}, u32[]{:S(2)}, u32[]{:S(2)}) collective-permute-start(f32[8,128,128]{2,1,0:T(8,128)} %get-tuple-element.105), channel_id=1, source_target_pairs={{0,2},{1,3},{2,0},{3,1},{4,6},{5,7},{6,4},{7,5},{8,10},{9,11},{10,... | collective-permute-start | bytes 1572872 | tf_op jit(solution)/shard_map/ppermute | solution.py:543
  245.1 37.6 %collective-permute-start.18 = (f32[8,128,128]{2,1,0:T(8,128)}, f32[8,128,128]{2,1,0:T(8,128)}, u32[]{:S(2)}, u32[]{:S(2)}) collective-permute-start(f32[8,128,128]{2,1,0:T(8,128)} %get-tuple-element.106), channel_id=1, source_target_pairs={{0,3},{1,0},{2,1},{3,2},{4,7},{5,4},{6,5},{7,6},{8,11},{9,8},{10,9... | collective-permute-start | bytes 1572872 | tf_op jit(solution)/shard_map/ppermute | solution.py:543
  248.4 34.3 %collective-permute-start.16 = (f32[8,128,128]{2,1,0:T(8,128)}, f32[8,128,128]{2,1,0:T(8,128)}, u32[]{:S(2)}, u32[]{:S(2)}) collective-permute-start(f32[8,128,128]{2,1,0:T(8,128)} %gate.26), channel_id=1, source_target_pairs={{0,1},{1,2},{2,3},{3,0},{4,5},{5,6},{6,7},{7,4},{8,9},{9,10},{10,1... | collective-permute-start | bytes 1572872 | tf_op jit(solution)/shard_map/ppermute | solution.py:543
  282.7 25.1 %collective-permute-start.19 = (f32[8,128,128]{2,1,0:T(8,128)}, f32[8,128,128]{2,1,0:T(8,128)}, u32[]{:S(2)}, u32[]{:S(2)}) collective-permute-start(f32[8,128,128]{2,1,0:T(8,128)} %get-tuple-element.107), channel_id=1, source_target_pairs={{0,1},{1,2},{2,3},{3,0},{4,5},{5,6},{6,7},{7,4},{8,9},{9,10},{10,1... | collective-permute-start | bytes 1572872 | tf_op jit(solution)/shard_map/ppermute | solution.py:543
  290.3 37.8 %collective-permute-start.20 = (f32[8,128,128]{2,1,0:T(8,128)}, f32[8,128,128]{2,1,0:T(8,128)}, u32[]{:S(2)}, u32[]{:S(2)}) collective-permute-start(f32[8,128,128]{2,1,0:T(8,128)} %get-tuple-element.108), channel_id=1, source_target_pairs={{0,2},{1,3},{2,0},{3,1},{4,6},{5,7},{6,4},{7,5},{8,10},{9,11},{10,... | collective-permute-start | bytes 1572872 | tf_op jit(solution)/shard_map/ppermute | solution.py:543
  293.6 34.5 %collective-permute-start.21 = (f32[8,128,128]{2,1,0:T(8,128)}, f32[8,128,128]{2,1,0:T(8,128)}, u32[]{:S(2)}, u32[]{:S(2)}) collective-permute-start(f32[8,128,128]{2,1,0:T(8,128)} %get-tuple-element.109), channel_id=1, source_target_pairs={{0,3},{1,0},{2,1},{3,2},{4,7},{5,4},{6,5},{7,6},{8,11},{9,8},{10,9... | collective-permute-start | bytes 1572872 | tf_op jit(solution)/shard_map/ppermute | solution.py:543
  303.2 53.7 %all-to-all-start.4 = ((f32[8,2,64,8,128]{4,3,2,1,0:T(8,128)}), f32[8,2,64,8,128]{4,3,2,1,0:T(8,128)}, u32[]{:S(2)}, u32[]{:S(2)}) async-start(f32[8,2,64,8,128]{4,3,2,1,0:T(8,128)} %x_inverse.4.refs_6_), calls=%async_computation.4 | async-start | bytes 8388608 | tf_op jit(solution)/shard_map/all_to_all | solution.py:547
  328.1 41.8 %collective-permute-start.22 = (f32[8,128,128]{2,1,0:T(8,128)}, f32[8,128,128]{2,1,0:T(8,128)}, u32[]{:S(2)}, u32[]{:S(2)}) collective-permute-start(f32[8,128,128]{2,1,0:T(8,128)} %get-tuple-element.112), channel_id=1, source_target_pairs={{0,1},{1,2},{2,3},{3,0},{4,5},{5,6},{6,7},{7,4},{8,9},{9,10},{10,1... | collective-permute-start | bytes 1572872 | tf_op jit(solution)/shard_map/ppermute | solution.py:543
  339.8 35.0 %collective-permute-start.23 = (f32[8,128,128]{2,1,0:T(8,128)}, f32[8,128,128]{2,1,0:T(8,128)}, u32[]{:S(2)}, u32[]{:S(2)}) collective-permute-start(f32[8,128,128]{2,1,0:T(8,128)} %get-tuple-element.113), channel_id=1, source_target_pairs={{0,2},{1,3},{2,0},{3,1},{4,6},{5,7},{6,4},{7,5},{8,10},{9,11},{10,... | collective-permute-start | bytes 1572872 | tf_op jit(solution)/shard_map/ppermute | solution.py:543
  341.4 33.4 %collective-permute-start.24 = (f32[8,128,128]{2,1,0:T(8,128)}, f32[8,128,128]{2,1,0:T(8,128)}, u32[]{:S(2)}, u32[]{:S(2)}) collective-permute-start(f32[8,128,128]{2,1,0:T(8,128)} %get-tuple-element.114), channel_id=1, source_target_pairs={{0,3},{1,0},{2,1},{3,2},{4,7},{5,4},{6,5},{7,6},{8,11},{9,8},{10,9... | collective-permute-start | bytes 1572872 | tf_op jit(solution)/shard_map/ppermute | solution.py:543
  356.9 53.7 %all-to-all-start.5 = ((f32[8,2,64,8,128]{4,3,2,1,0:T(8,128)}), f32[8,2,64,8,128]{4,3,2,1,0:T(8,128)}, u32[]{:S(2)}, u32[]{:S(2)}) async-start(f32[8,2,64,8,128]{4,3,2,1,0:T(8,128)} %gate.30), calls=%async_computation.5 | async-start | bytes 8388608 | tf_op jit(solution)/shard_map/all_to_all | solution.py:547
  374.8 40.2 %collective-permute-start.25 = (f32[8,128,128]{2,1,0:T(8,128)}, f32[8,128,128]{2,1,0:T(8,128)S(1)}, u32[]{:S(2)}, u32[]{:S(2)}) collective-permute-start(f32[8,128,128]{2,1,0:T(8,128)} %get-tuple-element.118), channel_id=1, source_target_pairs={{0,1},{1,2},{2,3},{3,0},{4,5},{5,6},{6,7},{7,4},{8,9},{9,10},{10,1... | collective-permute-start | bytes 1572872 | tf_op jit(solution)/shard_map/ppermute | solution.py:543
  386.5 36.2 %collective-permute-start.26 = (f32[8,128,128]{2,1,0:T(8,128)}, f32[8,128,128]{2,1,0:T(8,128)S(1)}, u32[]{:S(2)}, u32[]{:S(2)}) collective-permute-start(f32[8,128,128]{2,1,0:T(8,128)} %get-tuple-element.119), channel_id=1, source_target_pairs={{0,2},{1,3},{2,0},{3,1},{4,6},{5,7},{6,4},{7,5},{8,10},{9,11},{10,... | collective-permute-start | bytes 1572872 | tf_op jit(solution)/shard_map/ppermute | solution.py:543
  388.9 33.8 %collective-permute-start.27 = (f32[8,128,128]{2,1,0:T(8,128)}, f32[8,128,128]{2,1,0:T(8,128)S(1)}, u32[]{:S(2)}, u32[]{:S(2)}) collective-permute-start(f32[8,128,128]{2,1,0:T(8,128)} %get-tuple-element.120), channel_id=1, source_target_pairs={{0,3},{1,0},{2,1},{3,2},{4,7},{5,4},{6,5},{7,6},{8,11},{9,8},{10,9... | collective-permute-start | bytes 1572872 | tf_op jit(solution)/shard_map/ppermute | solution.py:543
  410.6 31.0 %all-to-all-start.6 = ((f32[8,1,64,8,128]{4,3,2,1,0:T(8,128)}), f32[8,1,64,8,128]{4,3,2,1,0:T(8,128)}, u32[]{:S(2)}, u32[]{:S(2)}) async-start(f32[8,1,64,8,128]{4,3,2,1,0:T(8,128)} %gate.31._), calls=%async_computation.6 | async-start | bytes 4194304 | tf_op jit(solution)/shard_map/all_to_all | solution.py:547
  415.0 7.7 %copy-start.7 = (f32[8,128,128]{2,1,0:T(8,128)}, f32[8,128,128]{2,1,0:T(8,128)S(1)}, u32[]{:S(2)}) copy-start(f32[8,128,128]{2,1,0:T(8,128)S(1)} %collective-permute-done.25.refs_1_._) | copy-start | bytes 1572868
  422.7 0.8 copy-start.8
  423.5 0.8 copy-start.9
  441.6 30.2 %all-to-all-start.7 = ((f32[8,1,64,8,128]{4,3,2,1,0:T(8,128)}), f32[8,1,64,8,128]{4,3,2,1,0:T(8,128)S(1)}, u32[]{:S(2)}, u32[]{:S(2)}) async-start(f32[8,1,64,8,128]{4,3,2,1,0:T(8,128)} %gate.33), calls=%async_computation.7 | async-start | bytes 4194304 | tf_op jit(solution)/shard_map/all_to_all | solution.py:547
  471.8 1.3 copy-start.2
  (1 other events, 0.6 us)

commit v4 on v3

--- a/solution.py
+++ b/solution.py
@@ -89,12 +89,18 @@
 scalars = pl.BlockSpec(memory_space=pltpu.SMEM)
 
 
-def into_kernel(field_ref, matrix_ref, *refs):
+def into_kernel(plain, field_ref, matrix_ref, *refs):
     out_ref, rows_ref = refs[-2:]
     sublanes, levels, part_y = field_ref.shape[1:]
+    if plain:
+        matrix = -matrix_ref[...]
+        high = matrix.astype(half).astype(jnp.float32)
+        matrix = jnp.concatenate([high, high, matrix - high], axis=0).T.astype(half)
+    else:
+        matrix = matrix_ref[0]
     for pair in range(0, sublanes, 2):
         fields = jnp.concatenate([field_ref[0, pair], field_ref[0, pair + 1]], axis=1)
-        turned = narrow_product(matrix_ref[0], fields)
+        turned = narrow_product(matrix, fields)
         for x in (pair, pair + 1):
             rows_ref[pl.ds(x, levels, stride=sublanes), :] = turned[
                 :, (x - pair) * part_y : (x - pair + 1) * part_y
@@ -106,17 +112,20 @@
     _, part_x, levels, part_y = fields.shape
     sublanes = block_x(part_x)
     count = len(components)
+    plain = matrices.ndim == 2
     per = levels // groups
     first, step = components[0], (components[1] - components[0] if count > 1 else 1)
     size = count * part_x * levels * part_y
     return pl.pallas_call(
-        into_kernel,
+        functools.partial(into_kernel, plain),
         grid=(count, part_x // sublanes),
         in_specs=[
             pl.BlockSpec(
                 (1, sublanes, levels, part_y), lambda f, i: (first + f * step, i, 0, 0)
             ),
-            pl.BlockSpec((1, levels, 3 * levels), lambda f, i: (f, 0, 0)),
+            pl.BlockSpec((levels, levels), lambda f, i: (0, 0))
+            if plain
+            else pl.BlockSpec((1, levels, 3 * levels), lambda f, i: (f, 0, 0)),
         ]
         + [anywhere] * len(follow),
         out_specs=pl.BlockSpec((groups, 1, per, sublanes, part_y), lambda f, i: (0, f, 0, i, 0)),
@@ -630,7 +639,7 @@
     leave_forward = wide(-jnp.stack([eigen_vectors, matmul(vert_deriv, eigen_vectors)]))
     slope = wide(vert_deriv)
 
-    a_one = into_levels(cotangent, wide(-vectors_t[None]), (1,), count_x)
+    a_one = into_levels(cotangent, eigen_vectors, (1,), count_x)
     a_two = into_levels(
         cotangent,
         enter_adjoint,

time: 480 us -> 478 us (level)
  no operation moved by 1% of the time
where the time goes in v4:
time: 478 us; the launch traced here: 476 us
  starting transfers between devices  160 us (33%)
  Pallas kernels  156 us (33%)
  waiting for transfers between devices  147 us (31%)
  local copies, waits for them, and re-layouts  8.99 us (2%)
    ppermute x28, starting transfers between devices, shifted(): lax.ppermute(cells, axis, [(i, (i + shift) % count) for i in range(count)])  125 us
    all_to_all x8, waiting for transfers between devices, swap_x(): return lax.all_to_all(rows, 'gx', split_axis=0, concat_axis=0, tiled=True)  106 us
    ppermute x28, waiting for transfers between devices, shifted(): lax.ppermute(cells, axis, [(i, (i + shift) % count) for i in range(count)])  40.6 us
    all_to_all x8, starting transfers between devices, swap_x(): return lax.all_to_all(rows, 'gx', split_axis=0, concat_axis=0, tiled=True)  34.9 us
    pallas_call x2, Pallas kernels, y_solve(): pl.pallas_call(functools.partial(solve_kernel, sources, full), grid=(leve...  29.3 us
    pallas_call x4, Pallas kernels, x_inverse(): pl.pallas_call(functools.partial(x_inverse_kernel, sources), grid=(count,...  27.2 us
    pallas_call x2, Pallas kernels, make_section(): pl.pallas_call(section_kernel, grid=(count, part_x // sublanes), in_specs...  25.4 us
    pallas_call x4, Pallas kernels, x_forward(): pl.pallas_call(x_kernel, grid=(levels // block,), in_specs=[scalars, pl.B...  24.3 us
  transfers between devices with their start and end apart: 36, of which 12 were waited for; matrix products, arithmetic and copies ran while one was open for 1% of the time, Pallas kernels for 31%

profile of v4, /device:TPU:0, one launch (start us, length us, event | category | flops | bytes accessed | tf_op | source)
XLA Modules:
  0.0 476.2 jit_solution(15566511420290294643)
XLA Ops:
  0.6 4.5 into_levels.2._.refs_0_
  5.2 5.2 %all-to-all-start = ((f32[8,1,8,64,128]{4,3,2,1,0:T(8,128)}), f32[8,1,8,64,128]{4,3,2,1,0:T(8,128)S(1)}, u32[]{:S(2)}, u32[]{:S(2)}) async-start(f32[8,1,8,64,128]{4,3,2,1,0:T(8,128)} %into_levels.2._.refs_0_), calls=%async_computation | async-start | bytes 4194304 | tf_op jit(solution)/shard_map/all_to_all | solution.py:556
  10.4 6.8 %edges_of.1 = (f32[3,64,64]{2,1,0:T(8,128)}, f32[3,64,64]{2,1,0:T(8,128)}, f32[3,1,64,128]{3,2,1,0:T(8,128)}, f32[3,1,64,128]{3,2,1,0:T(8,128)}) custom-call(f32[3,64,64,128]{3,2,1,0:T(8,128)} %refs_3_.3, f32[8,1,8,64,128]{4,3,2,1,0:T(8,128)} %into_levels.2._.refs_0_), custom_call_target="tpu_custom_call" | custom-call | bytes 629145600 | tf_op jit(solution)/shard_map/edges_of/pallas_call | solution.py:167
  28.3 7.7 %into_levels.3.refs_0_ = f32[8,2,8,64,128]{4,3,2,1,0:T(8,128)} custom-call(f32[3,64,64,128]{3,2,1,0:T(8,128)} %base_ref.3, bf16[2,64,192]{2,1,0:T(8,128)(2,1)} %pad_maximum_fusion.3.matrix_ref, f32[8,1,8,64,128]{4,3,2,1,0:T(8,128)} %into_levels.2._.refs_0_, bf16[2,64,192]{2,1,0:T(8,128)(2,1)} %get-tuple-element.135.refs_11_.refs_1_, ...), custom_call_target="tpu_custom_call" | custom-call | flops 40265318400 | bytes 838860800 | tf_op jit(solution)/shard_map/into_levels/pallas_call | solution.py:119
  38.8 4.6 all-to-all-start.1
  44.0 5.1 %x_forward.4 = (f32[8,128,128]{2,1,0:T(8,128)}, f32[8,128,128]{2,1,0:T(8,128)}, f32[8,128,128]{2,1,0:T(8,128)}, f32[8,128,128]{2,1,0:T(8,128)}) custom-call(s32[1]{0:T(128)} %bitcast.me_ref.group_ref, f32[8,1,8,64,128]{4,3,2,1,0:T(8,128)} %copy-done, bf16[2,4,128,512]{3,2,1,0:T(8,128)(2,1)} %constant.29.clone.table_ref, f32[3,1,64,128]{3,2,1,0:T(8,128)} %copy-done.10, ...), custom_call_target="tpu_custom_call" | custom-call | flops 161061273600 | bytes 524288000 | tf_op jit(solution)/shard_map/x_forward/pallas_call | solution.py:334
  54.6 9.1 %make_section.2 = (f32[3,64,64,128]{3,2,1,0:T(8,128)}, f32[3,64,64,128]{3,2,1,0:T(8,128)}, f32[8,1,8,64,128]{4,3,2,1,0:T(8,128)}) custom-call(f32[3,64,64,128]{3,2,1,0:T(8,128)} %refs_3_.3, f32[3,64,64,128]{3,2,1,0:T(8,128)} %refs_3_.3, f32[3,64,64,128]{3,2,1,0:T(8,128)} %refs_3_.3, f32[3,64,64,128]{3,2,1,0:T(8,128)} %refs_3_.3, ...), custom_call_target="tpu_custom_call" | custom-call | flops 40265318400 | bytes 1887436800 | tf_op jit(solution)/shard_map/make_section/pallas_call | solution.py:246
  63.7 16.3 %make_section.3 = (f32[3,64,64,128]{3,2,1,0:T(8,128)}, f32[3,64,64,128]{3,2,1,0:T(8,128)}, f32[8,2,8,64,128]{4,3,2,1,0:T(8,128)}) custom-call(f32[3,64,64,128]{3,2,1,0:T(8,128)} %refs_3_.3, f32[3,64,64,128]{3,2,1,0:T(8,128)} %refs_3_.3, f32[3,64,64,128]{3,2,1,0:T(8,128)} %refs_3_.3, ...), custom_call_target="tpu_custom_call", output_to_operand_aliasing={{0}: (12, {}), {1}: (13, {})} | custom-call | flops 80530636800 | bytes 3774873600 | tf_op jit(solution)/shard_map/make_section/pallas_call | solution.py:246
  80.0 12.4 %all-to-all-done.1.rows_ref = f32[8,2,8,64,128]{4,3,2,1,0:T(8,128)} async-done(((f32[8,2,8,64,128]{4,3,2,1,0:T(8,128)}), f32[8,2,8,64,128]{4,3,2,1,0:T(8,128)}, u32[]{:S(2)}, u32[]{:S(2)}) %all-to-all-start.1) | async-done | bytes 4194336 | tf_op jit(solution)/shard_map/all_to_all | solution.py:556
  92.4 7.1 %x_forward.5 = (f32[8,128,128]{2,1,0:T(8,128)}, f32[8,128,128]{2,1,0:T(8,128)}, f32[8,128,128]{2,1,0:T(8,128)}, f32[8,128,128]{2,1,0:T(8,128)}) custom-call(s32[1]{0:T(128)} %bitcast.me_ref.group_ref, f32[8,2,8,64,128]{4,3,2,1,0:T(8,128)} %all-to-all-done.1.rows_ref, bf16[2,4,128,1024]{3,2,1,0:T(8,128)(2,1)} %constant.30.clone.table_ref, ...), custom_call_target="tpu_custom_call" | custom-call | flops 322122547200 | bytes 838860800 | tf_op jit(solution)/shard_map/x_forward/pallas_call | solution.py:334
  99.6 3.6 all-to-all-start.2
  108.5 21.3 %all-to-all-done.2.refs_1_.rows_ref = f32[8,1,8,64,128]{4,3,2,1,0:T(8,128)S(1)} async-done(((f32[8,1,8,64,128]{4,3,2,1,0:T(8,128)}), f32[8,1,8,64,128]{4,3,2,1,0:T(8,128)S(1)}, u32[]{:S(2)}, u32[]{:S(2)}) %all-to-all-start.2) | async-done | bytes 2097184 | tf_op jit(solution)/shard_map/all_to_all | solution.py:556
  131.1 4.6 all-to-all-start.3
  135.6 5.1 %x_forward.7 = (f32[8,128,128]{2,1,0:T(8,128)}, f32[8,128,128]{2,1,0:T(8,128)}, f32[8,128,128]{2,1,0:T(8,128)}, f32[8,128,128]{2,1,0:T(8,128)}) custom-call(s32[1]{0:T(128)} %bitcast.me_ref.group_ref, f32[8,1,8,64,128]{4,3,2,1,0:T(8,128)} %copy-done.1, bf16[2,4,128,512]{3,2,1,0:T(8,128)(2,1)} %constant.29.clone.table_ref, ...), custom_call_target="tpu_custom_call" | custom-call | flops 161061273600 | bytes 524288000 | tf_op jit(solution)/shard_map/x_forward/pallas_call | solution.py:334
  140.8 11.8 %collective-permute-start.12 = (f32[8,128,128]{2,1,0:T(8,128)}, f32[8,128,128]{2,1,0:T(8,128)}, u32[]{:S(2)}, u32[]{:S(2)}) collective-permute-start(f32[8,128,128]{2,1,0:T(8,128)} %get-tuple-element.90), channel_id=1, source_target_pairs={{0,2},{1,3},{2,0},{3,1},{4,6},{5,7},{6,4},{7,5},{8,10},{9,11},{10,... | collective-permute-start | bytes 1572872 | tf_op jit(solution)/shard_map/ppermute | solution.py:552
  152.5 3.4 collective-permute-start.13
  155.9 28.8 %all-to-all-done.3.rows_ref = f32[8,2,8,64,128]{4,3,2,1,0:T(8,128)} async-done(((f32[8,2,8,64,128]{4,3,2,1,0:T(8,128)}), f32[8,2,8,64,128]{4,3,2,1,0:T(8,128)}, u32[]{:S(2)}, u32[]{:S(2)}) %all-to-all-start.3) | async-done | bytes 4194336 | tf_op jit(solution)/shard_map/all_to_all | solution.py:556
  184.8 7.1 %x_forward.6 = (f32[8,128,128]{2,1,0:T(8,128)}, f32[8,128,128]{2,1,0:T(8,128)}, f32[8,128,128]{2,1,0:T(8,128)}, f32[8,128,128]{2,1,0:T(8,128)}) custom-call(s32[1]{0:T(128)} %bitcast.me_ref.group_ref, f32[8,2,8,64,128]{4,3,2,1,0:T(8,128)} %all-to-all-done.3.rows_ref, bf16[2,4,128,1024]{3,2,1,0:T(8,128)(2,1)} %constant.30.clone.table_ref, ...), custom_call_target="tpu_custom_call" | custom-call | flops 322122547200 | bytes 838860800 | tf_op jit(solution)/shard_map/x_forward/pallas_call | solution.py:334
  191.8 6.2 %collective-permute-start.14 = (f32[8,128,128]{2,1,0:T(8,128)}, f32[8,128,128]{2,1,0:T(8,128)}, u32[]{:S(2)}, u32[]{:S(2)}) collective-permute-start(f32[8,128,128]{2,1,0:T(8,128)} %get-tuple-element.92), channel_id=1, source_target_pairs={{0,2},{1,3},{2,0},{3,1},{4,6},{5,7},{6,4},{7,5},{8,10},{9,11},{10,... | collective-permute-start | bytes 1572872 | tf_op jit(solution)/shard_map/ppermute | solution.py:552
  198.0 3.4 collective-permute-start.15
  201.4 14.6 %y_solve.2 = (f32[8,128,128]{2,1,0:T(8,128)}, f32[8,128,128]{2,1,0:T(8,128)}, f32[8,128,128]{2,1,0:T(8,128)}, f32[8,128,128]{2,1,0:T(8,128)}, f32[8,128,128]{2,1...) custom-call(s32[1]{0:T(128)} %bitcast.me_ref.group_ref, ...), custom_call_target="tpu_custom_call" | custom-call | flops 644245094400 | bytes 1258291200 | tf_op jit(solution)/shard_map/y_solve/pallas_call | solution.py:394
  216.1 7.5 %collective-permute-done.14.refs_2_ = f32[8,128,128]{2,1,0:T(8,128)} collective-permute-done((f32[8,128,128]{2,1,0:T(8,128)}, f32[8,128,128]{2,1,0:T(8,128)}, u32[]{:S(2)}, u32[]{:S(2)}) %collective-permute-start.14) | collective-permute-done | bytes 524320 | tf_op jit(solution)/shard_map/ppermute | solution.py:552
  223.6 19.9 %collective-permute-start.17 = (f32[8,128,128]{2,1,0:T(8,128)}, f32[8,128,128]{2,1,0:T(8,128)}, u32[]{:S(2)}, u32[]{:S(2)}) collective-permute-start(f32[8,128,128]{2,1,0:T(8,128)} %get-tuple-element.105), channel_id=1, source_target_pairs={{0,2},{1,3},{2,0},{3,1},{4,6},{5,7},{6,4},{7,5},{8,10},{9,11},{10,... | collective-permute-start | bytes 1572872 | tf_op jit(solution)/shard_map/ppermute | solution.py:552
  243.6 3.4 collective-permute-start.18
  246.9 19.6 %collective-permute-start.16 = (f32[8,128,128]{2,1,0:T(8,128)}, f32[8,128,128]{2,1,0:T(8,128)}, u32[]{:S(2)}, u32[]{:S(2)}) collective-permute-start(f32[8,128,128]{2,1,0:T(8,128)} %gate.26), channel_id=1, source_target_pairs={{0,1},{1,2},{2,3},{3,0},{4,5},{5,6},{6,7},{7,4},{8,9},{9,10},{10,1... | collective-permute-start | bytes 1572872 | tf_op jit(solution)/shard_map/ppermute | solution.py:552
  266.5 14.6 %y_solve.3 = (f32[8,128,128]{2,1,0:T(8,128)}, f32[8,128,128]{2,1,0:T(8,128)}, f32[8,128,128]{2,1,0:T(8,128)}, f32[8,128,128]{2,1,0:T(8,128)}, f32[8,128,128]{2,1...) custom-call(s32[1]{0:T(128)} %bitcast.me_ref.group_ref, ...), custom_call_target="tpu_custom_call" | custom-call | flops 644245094400 | bytes 1258291200 | tf_op jit(solution)/shard_map/y_solve/pallas_call | solution.py:394
  281.2 7.6 %collective-permute-start.19 = (f32[8,128,128]{2,1,0:T(8,128)}, f32[8,128,128]{2,1,0:T(8,128)}, u32[]{:S(2)}, u32[]{:S(2)}) collective-permute-start(f32[8,128,128]{2,1,0:T(8,128)} %get-tuple-element.107), channel_id=1, source_target_pairs={{0,1},{1,2},{2,3},{3,0},{4,5},{5,6},{6,7},{7,4},{8,9},{9,10},{10,1... | collective-permute-start | bytes 1572872 | tf_op jit(solution)/shard_map/ppermute | solution.py:552
  293.6 8.1 %x_inverse.4.refs_6_ = f32[8,2,64,8,128]{4,3,2,1,0:T(8,128)} custom-call(s32[1]{0:T(128)} %bitcast.me_ref.group_ref, f32[8,128,128]{2,1,0:T(8,128)} %get-tuple-element.110._.refs_0_, f32[8,128,128]{2,1,0:T(8,128)} %get-tuple-element.111.refs_0_, f32[8,128,128]{2,1,0:T(8,128)} %collective-permute-done.16.refs_3_.refs_1_, ...), custom_call_target="tpu_custom_call" | custom-call | flops 322122547200 | bytes 838860800 | tf_op jit(solution)/shard_map/x_inverse/pallas_call | solution.py:446
  301.7 4.6 all-to-all-start.4
  306.3 20.3 %collective-permute-done.20.refs_4_.refs_2_ = f32[8,128,128]{2,1,0:T(8,128)} collective-permute-done((f32[8,128,128]{2,1,0:T(8,128)}, f32[8,128,128]{2,1,0:T(8,128)}, u32[]{:S(2)}, u32[]{:S(2)}) %collective-permute-start.20) | collective-permute-done | bytes 524320 | tf_op jit(solution)/shard_map/ppermute | solution.py:552
  326.6 11.7 %collective-permute-start.22 = (f32[8,128,128]{2,1,0:T(8,128)}, f32[8,128,128]{2,1,0:T(8,128)}, u32[]{:S(2)}, u32[]{:S(2)}) collective-permute-start(f32[8,128,128]{2,1,0:T(8,128)} %get-tuple-element.112), channel_id=1, source_target_pairs={{0,1},{1,2},{2,3},{3,0},{4,5},{5,6},{6,7},{7,4},{8,9},{9,10},{10,1... | collective-permute-start | bytes 1572872 | tf_op jit(solution)/shard_map/ppermute | solution.py:552
  340.7 8.1 %x_inverse.6.refs_0_ = f32[8,2,64,8,128]{4,3,2,1,0:T(8,128)} custom-call(s32[1]{0:T(128)} %bitcast.me_ref.group_ref, f32[8,128,128]{2,1,0:T(8,128)} %get-tuple-element.83._.refs_0_, f32[8,128,128]{2,1,0:T(8,128)} %get-tuple-element.110._.refs_0_, f32[8,128,128]{2,1,0:T(8,128)} %collective-permute-done.19.refs_3_.refs_1_, ...), custom_call_target="tpu_custom_call" | custom-call | flops 322122547200 | bytes 838860800 | tf_op jit(solution)/shard_map/x_inverse/pallas_call | solution.py:446
  348.8 6.6 %all-to-all-done.4.refs_1_.rows_ref = f32[8,2,64,8,128]{4,3,2,1,0:T(8,128)} async-done(((f32[8,2,64,8,128]{4,3,2,1,0:T(8,128)}), f32[8,2,64,8,128]{4,3,2,1,0:T(8,128)}, u32[]{:S(2)}, u32[]{:S(2)}) %all-to-all-start.4) | async-done | bytes 4194336 | tf_op jit(solution)/shard_map/all_to_all | solution.py:556
  355.4 4.6 all-to-all-start.5
  360.0 8.4 %from_levels.3.refs_6_.done_ref = f32[3,64,64,128]{3,2,1,0:T(8,128)} custom-call(f32[8,2,64,8,128]{4,3,2,1,0:T(8,128)} %all-to-all-done.4.refs_1_.rows_ref, bf16[2,64,192]{2,1,0:T(8,128)(2,1)} %get-tuple-element.136.refs_2_.matrix_ref, f32[3,64,64,128]{3,2,1,0:T(8,128)} %base_ref.3), custom_call_target="tpu_custom_call" | custom-call | flops 40265318400 | bytes 1258291200 | tf_op jit(solution)/shard_map/from_levels/pallas_call | solution.py:487
  368.4 5.0 %collective-permute-done.23.refs_2_.refs_4_ = f32[8,128,128]{2,1,0:T(8,128)} collective-permute-done((f32[8,128,128]{2,1,0:T(8,128)}, f32[8,128,128]{2,1,0:T(8,128)}, u32[]{:S(2)}, u32[]{:S(2)}) %collective-permute-start.23) | collective-permute-done | bytes 524320 | tf_op jit(solution)/shard_map/ppermute | solution.py:552
  373.3 11.7 %collective-permute-start.25 = (f32[8,128,128]{2,1,0:T(8,128)}, f32[8,128,128]{2,1,0:T(8,128)S(1)}, u32[]{:S(2)}, u32[]{:S(2)}) collective-permute-start(f32[8,128,128]{2,1,0:T(8,128)} %get-tuple-element.118), channel_id=1, source_target_pairs={{0,1},{1,2},{2,3},{3,0},{4,5},{5,6},{6,7},{7,4},{8,9},{9,10},{10,1... | collective-permute-start | bytes 1572872 | tf_op jit(solution)/shard_map/ppermute | solution.py:552
  387.4 5.5 %x_inverse.5.refs_0_ = f32[8,1,64,8,128]{4,3,2,1,0:T(8,128)} custom-call(s32[1]{0:T(128)} %bitcast.me_ref.group_ref, f32[8,128,128]{2,1,0:T(8,128)} %get-tuple-element.95._.refs_0_, f32[8,128,128]{2,1,0:T(8,128)} %get-tuple-element.83._.refs_0_, f32[8,128,128]{2,1,0:T(8,128)} %collective-permute-done.22.refs_1_.refs_3_, ...), custom_call_target="tpu_custom_call" | custom-call | flops 16106127360 | bytes 52428800 | tf_op jit(solution)/shard_map/x_inverse/pallas_call | solution.py:446
  392.9 16.2 %all-to-all-done.5.refs_1_.rows_ref = f32[8,2,64,8,128]{4,3,2,1,0:T(8,128)} async-done(((f32[8,2,64,8,128]{4,3,2,1,0:T(8,128)}), f32[8,2,64,8,128]{4,3,2,1,0:T(8,128)}, u32[]{:S(2)}, u32[]{:S(2)}) %all-to-all-start.5) | async-done | bytes 4194336 | tf_op jit(solution)/shard_map/all_to_all | solution.py:556
  409.1 4.3 all-to-all-start.6
  413.5 7.7 %collective-permute-done.26.refs_2_ = f32[8,128,128]{2,1,0:T(8,128)S(1)} collective-permute-done((f32[8,128,128]{2,1,0:T(8,128)}, f32[8,128,128]{2,1,0:T(8,128)S(1)}, u32[]{:S(2)}, u32[]{:S(2)}) %collective-permute-start.26) | collective-permute-done | bytes 524320 | tf_op jit(solution)/shard_map/ppermute | solution.py:552
  422.8 5.5 %x_inverse.7.refs_0_ = f32[8,1,64,8,128]{4,3,2,1,0:T(8,128)} custom-call(s32[1]{0:T(128)} %bitcast.me_ref.group_ref, f32[8,1,64,8,128]{4,3,2,1,0:T(8,128)} %gate.31._, f32[8,128,128]{2,1,0:T(8,128)} %get-tuple-element.95._.refs_0_, f32[8,128,128]{2,1,0:T(8,128)} %copy-done.7, f32[8,128,128]{2,1,0:T(8,128)} %copy-done.8, f32[8,128,128]{2,1,0:T(8,128)} %copy-done.9, ...), custom_call_target="tpu_custom_call" | custom-call | flops 161061273600 | bytes 524288000 | tf_op jit(solution)/shard_map/x_inverse/pallas_call | solution.py:446
  428.3 11.8 %all-to-all-done.6.refs_1_.refs_0_.rows_ref = f32[8,1,64,8,128]{4,3,2,1,0:T(8,128)} async-done(((f32[8,1,64,8,128]{4,3,2,1,0:T(8,128)}), f32[8,1,64,8,128]{4,3,2,1,0:T(8,128)}, u32[]{:S(2)}, u32[]{:S(2)}) %all-to-all-start.6) | async-done | bytes 2097184 | tf_op jit(solution)/shard_map/all_to_all | solution.py:556
  440.1 3.6 all-to-all-start.7
  443.7 8.4 %from_levels.4.base_ref = f32[3,64,64,128]{3,2,1,0:T(8,128)} custom-call(f32[8,2,64,8,128]{4,3,2,1,0:T(8,128)} %all-to-all-done.5.refs_1_.rows_ref, bf16[2,64,192]{2,1,0:T(8,128)(2,1)} %pad_maximum_fusion.6.refs_3_.matrix_ref, f32[3,64,64,128]{3,2,1,0:T(8,128)} %get-tuple-element.121.base_ref, ...), custom_call_target="tpu_custom_call", output_to_operand_aliasing={{}: (2, {})} | custom-call | flops 40265318400 | bytes 1258291200 | tf_op jit(solution)/shard_map/from_levels/pallas_call | solution.py:487
  452.1 9.3 %gradient_of.1 = (f32[3,64,64,128]{3,2,1,0:T(8,128)}, f32[64,64,128]{2,1,0:T(8,128)}) custom-call(f32[8,1,64,8,128]{4,3,2,1,0:T(8,128)} %all-to-all-done.6.refs_1_.refs_0_.rows_ref, bf16[2,64,192]{2,1,0:T(8,128)(2,1)} %get-tuple-element.136.refs_2_.matrix_ref, f32[3,64,64,128]{3,2,1,0:T(8,128)} %base_ref.3, ...), custom_call_target="tpu_custom_call", output_to_operand_aliasing={{0}: (3, {})} | custom-call | flops 20132659200 | bytes 1887436800 | tf_op jit(solution)/shard_map/gradient_of/pallas_call | solution.py:527
  461.4 8.9 %all-to-all-done.7.rows_ref = f32[8,1,64,8,128]{4,3,2,1,0:T(8,128)S(1)} async-done(((f32[8,1,64,8,128]{4,3,2,1,0:T(8,128)}), f32[8,1,64,8,128]{4,3,2,1,0:T(8,128)S(1)}, u32[]{:S(2)}, u32[]{:S(2)}) %all-to-all-start.7) | async-done | bytes 2097184 | tf_op jit(solution)/shard_map/all_to_all | solution.py:556
  471.6 4.6 from_levels.5
  (106 shorter events, 39.1 us)
Async XLA Ops:
  5.2 32.3 %all-to-all-start = ((f32[8,1,8,64,128]{4,3,2,1,0:T(8,128)}), f32[8,1,8,64,128]{4,3,2,1,0:T(8,128)S(1)}, u32[]{:S(2)}, u32[]{:S(2)}) async-start(f32[8,1,8,64,128]{4,3,2,1,0:T(8,128)} %into_levels.2._.refs_0_), calls=%async_computation | async-start | bytes 4194304 | tf_op jit(solution)/shard_map/all_to_all | solution.py:556
  10.3 13.3 %copy-start.4 = (f32[64,64]{1,0:T(8,128)S(1)}, f32[64,64]{1,0:T(8,128)}, u32[]{:S(2)}) copy-start(f32[64,64]{1,0:T(8,128)} %param.20) | copy-start | bytes 49156
  10.3 13.4 %copy-start.3 = (f32[64,64]{1,0:T(8,128)S(1)}, f32[64,64]{1,0:T(8,128)}, u32[]{:S(2)}) copy-start(f32[64,64]{1,0:T(8,128)} %param.18) | copy-start | bytes 49156
  10.3 13.8 %copy-start.5 = (f32[64,64]{1,0:T(8,128)S(1)}, f32[64,64]{1,0:T(8,128)}, u32[]{:S(2)}) copy-start(f32[64,64]{1,0:T(8,128)} %matrix_ref.1) | copy-start | bytes 49156
  10.3 17.3 %copy-start.6 = (f32[64]{0:T(128)S(1)}, f32[64]{0:T(128)}, u32[]{:S(2)}) copy-start(f32[64]{0:T(128)} %param.17) | copy-start | bytes 772
  17.2 18.9 %collective-permute-start.2 = (f32[3,64,64]{2,1,0:T(8,128)}, f32[3,64,64]{2,1,0:T(8,128)S(1)}, u32[]{:S(2)}, u32[]{:S(2)}) collective-permute-start(f32[3,64,64]{2,1,0:T(8,128)} %get-tuple-element.66), channel_id=1, source_target_pairs={{0,1},{1,2},{2,3},{3,0},{4,5},{5,6},{6,7},{7,4},{8,9},{9,10},{10,1... | collective-permute-start | bytes 147464 | tf_op jit(solution)/shard_map/ppermute | solution.py:552
  18.8 17.9 %collective-permute-start.3 = (f32[3,64,64]{2,1,0:T(8,128)}, f32[3,64,64]{2,1,0:T(8,128)S(1)}, u32[]{:S(2)}, u32[]{:S(2)}) collective-permute-start(f32[3,64,64]{2,1,0:T(8,128)} %get-tuple-element.67), channel_id=1, source_target_pairs={{0,3},{1,0},{2,1},{3,2},{4,7},{5,4},{6,5},{7,6},{8,11},{9,8},{10,9... | collective-permute-start | bytes 147464 | tf_op jit(solution)/shard_map/ppermute | solution.py:552
  21.0 22.3 %collective-permute-start = (f32[3,1,64,128]{3,2,1,0:T(8,128)}, f32[3,1,64,128]{3,2,1,0:T(8,128)S(1)}, u32[]{:S(2)}, u32[]{:S(2)}) collective-permute-start(f32[3,1,64,128]{3,2,1,0:T(8,128)} %get-tuple-element.64), channel_id=1, source_target_pairs={{0,4},{4,8},{8,12},{12,16},{16,20},{20,24},{24,28},{28,0},{1,5},{5... | collective-permute-start | bytes 294920 | tf_op jit(solution)/shard_map/ppermute | solution.py:552
  21.0 22.3 %collective-permute-start.1 = (f32[3,1,64,128]{3,2,1,0:T(8,128)}, f32[3,1,64,128]{3,2,1,0:T(8,128)S(1)}, u32[]{:S(2)}, u32[]{:S(2)}) collective-permute-start(f32[3,1,64,128]{3,2,1,0:T(8,128)} %get-tuple-element.65), channel_id=1, source_target_pairs={{0,28},{4,0},{8,4},{12,8},{16,12},{20,16},{24,20},{28,24},{1,29},{... | collective-permute-start | bytes 294920 | tf_op jit(solution)/shard_map/ppermute | solution.py:552
  37.4 1.3 copy-start
  38.8 53.7 %all-to-all-start.1 = ((f32[8,2,8,64,128]{4,3,2,1,0:T(8,128)}), f32[8,2,8,64,128]{4,3,2,1,0:T(8,128)}, u32[]{:S(2)}, u32[]{:S(2)}) async-start(f32[8,2,8,64,128]{4,3,2,1,0:T(8,128)} %gate.17), calls=%async_computation.1 | async-start | bytes 8388608 | tf_op jit(solution)/shard_map/all_to_all | solution.py:556
  43.3 0.7 copy-start.11
  49.1 50.4 %collective-permute-start.4 = (f32[8,128,128]{2,1,0:T(8,128)}, f32[8,128,128]{2,1,0:T(8,128)}, u32[]{:S(2)}, u32[]{:S(2)}) collective-permute-start(f32[8,128,128]{2,1,0:T(8,128)} %get-tuple-element.74), channel_id=1, source_target_pairs={{0,1},{1,2},{2,3},{3,0},{4,5},{5,6},{6,7},{7,4},{8,9},{9,10},{10,1... | collective-permute-start | bytes 1572872 | tf_op jit(solution)/shard_map/ppermute | solution.py:552
  50.7 48.8 %collective-permute-start.5 = (f32[8,128,128]{2,1,0:T(8,128)}, f32[8,128,128]{2,1,0:T(8,128)}, u32[]{:S(2)}, u32[]{:S(2)}) collective-permute-start(f32[8,128,128]{2,1,0:T(8,128)} %get-tuple-element.75), channel_id=1, source_target_pairs={{0,2},{1,3},{2,0},{3,1},{4,6},{5,7},{6,4},{7,5},{8,10},{9,11},{10,... | collective-permute-start | bytes 1572872 | tf_op jit(solution)/shard_map/ppermute | solution.py:552
  53.3 46.2 %collective-permute-start.6 = (f32[8,128,128]{2,1,0:T(8,128)}, f32[8,128,128]{2,1,0:T(8,128)}, u32[]{:S(2)}, u32[]{:S(2)}) collective-permute-start(f32[8,128,128]{2,1,0:T(8,128)} %get-tuple-element.76), channel_id=1, source_target_pairs={{0,3},{1,0},{2,1},{3,2},{4,7},{5,4},{6,5},{7,6},{8,11},{9,8},{10,9... | collective-permute-start | bytes 1572872 | tf_op jit(solution)/shard_map/ppermute | solution.py:552
  99.5 3.7 copy-start.12
  99.6 30.2 %all-to-all-start.2 = ((f32[8,1,8,64,128]{4,3,2,1,0:T(8,128)}), f32[8,1,8,64,128]{4,3,2,1,0:T(8,128)S(1)}, u32[]{:S(2)}, u32[]{:S(2)}) async-start(f32[8,1,8,64,128]{4,3,2,1,0:T(8,128)} %gate.18), calls=%async_computation.2 | async-start | bytes 4194304 | tf_op jit(solution)/shard_map/all_to_all | solution.py:556
  103.8 36.9 %collective-permute-start.8 = (f32[8,128,128]{2,1,0:T(8,128)}, f32[8,128,128]{2,1,0:T(8,128)}, u32[]{:S(2)}, u32[]{:S(2)}) collective-permute-start(f32[8,128,128]{2,1,0:T(8,128)} %get-tuple-element.80), channel_id=1, source_target_pairs={{0,2},{1,3},{2,0},{3,1},{4,6},{5,7},{6,4},{7,5},{8,10},{9,11},{10,... | collective-permute-start | bytes 1572872 | tf_op jit(solution)/shard_map/ppermute | solution.py:552
  106.4 34.3 %collective-permute-start.9 = (f32[8,128,128]{2,1,0:T(8,128)}, f32[8,128,128]{2,1,0:T(8,128)}, u32[]{:S(2)}, u32[]{:S(2)}) collective-permute-start(f32[8,128,128]{2,1,0:T(8,128)} %get-tuple-element.81), channel_id=1, source_target_pairs={{0,3},{1,0},{2,1},{3,2},{4,7},{5,4},{6,5},{7,6},{8,11},{9,8},{10,9... | collective-permute-start | bytes 1572872 | tf_op jit(solution)/shard_map/ppermute | solution.py:552
  107.8 48.1 %collective-permute-start.7 = (f32[8,128,128]{2,1,0:T(8,128)}, f32[8,128,128]{2,1,0:T(8,128)}, u32[]{:S(2)}, u32[]{:S(2)}) collective-permute-start(f32[8,128,128]{2,1,0:T(8,128)} %gate.20), channel_id=1, source_target_pairs={{0,1},{1,2},{2,3},{3,0},{4,5},{5,6},{6,7},{7,4},{8,9},{9,10},{10,1... | collective-permute-start | bytes 1572872 | tf_op jit(solution)/shard_map/ppermute | solution.py:552
  129.8 1.3 copy-start.1
  131.1 53.7 %all-to-all-start.3 = ((f32[8,2,8,64,128]{4,3,2,1,0:T(8,128)}), f32[8,2,8,64,128]{4,3,2,1,0:T(8,128)}, u32[]{:S(2)}, u32[]{:S(2)}) async-start(f32[8,2,8,64,128]{4,3,2,1,0:T(8,128)} %gate.19), calls=%async_computation.3 | async-start | bytes 8388608 | tf_op jit(solution)/shard_map/all_to_all | solution.py:556
  140.8 51.0 %collective-permute-start.12 = (f32[8,128,128]{2,1,0:T(8,128)}, f32[8,128,128]{2,1,0:T(8,128)}, u32[]{:S(2)}, u32[]{:S(2)}) collective-permute-start(f32[8,128,128]{2,1,0:T(8,128)} %get-tuple-element.90), channel_id=1, source_target_pairs={{0,2},{1,3},{2,0},{3,1},{4,6},{5,7},{6,4},{7,5},{8,10},{9,11},{10,... | collective-permute-start | bytes 1572872 | tf_op jit(solution)/shard_map/ppermute | solution.py:552
  152.5 39.3 %collective-permute-start.13 = (f32[8,128,128]{2,1,0:T(8,128)}, f32[8,128,128]{2,1,0:T(8,128)}, u32[]{:S(2)}, u32[]{:S(2)}) collective-permute-start(f32[8,128,128]{2,1,0:T(8,128)} %get-tuple-element.91), channel_id=1, source_target_pairs={{0,3},{1,0},{2,1},{3,2},{4,7},{5,4},{6,5},{7,6},{8,11},{9,8},{10,9... | collective-permute-start | bytes 1572872 | tf_op jit(solution)/shard_map/ppermute | solution.py:552
  155.9 45.5 %collective-permute-start.10 = (f32[8,128,128]{2,1,0:T(8,128)}, f32[8,128,128]{2,1,0:T(8,128)}, u32[]{:S(2)}, u32[]{:S(2)}) collective-permute-start(f32[8,128,128]{2,1,0:T(8,128)} %gate.22), channel_id=1, source_target_pairs={{0,1},{1,2},{2,3},{3,0},{4,5},{5,6},{6,7},{7,4},{8,9},{9,10},{10,1... | collective-permute-start | bytes 1572872 | tf_op jit(solution)/shard_map/ppermute | solution.py:552
  191.8 31.8 %collective-permute-start.14 = (f32[8,128,128]{2,1,0:T(8,128)}, f32[8,128,128]{2,1,0:T(8,128)}, u32[]{:S(2)}, u32[]{:S(2)}) collective-permute-start(f32[8,128,128]{2,1,0:T(8,128)} %get-tuple-element.92), channel_id=1, source_target_pairs={{0,2},{1,3},{2,0},{3,1},{4,6},{5,7},{6,4},{7,5},{8,10},{9,11},{10,... | collective-permute-start | bytes 1572872 | tf_op jit(solution)/shard_map/ppermute | solution.py:552
  198.0 25.6 %collective-permute-start.15 = (f32[8,128,128]{2,1,0:T(8,128)}, f32[8,128,128]{2,1,0:T(8,128)}, u32[]{:S(2)}, u32[]{:S(2)}) collective-permute-start(f32[8,128,128]{2,1,0:T(8,128)} %get-tuple-element.93), channel_id=1, source_target_pairs={{0,3},{1,0},{2,1},{3,2},{4,7},{5,4},{6,5},{7,6},{8,11},{9,8},{10,9... | collective-permute-start | bytes 1572872 | tf_op jit(solution)/shard_map/ppermute | solution.py:552
  201.4 45.5 %collective-permute-start.11 = (f32[8,128,128]{2,1,0:T(8,128)}, f32[8,128,128]{2,1,0:T(8,128)}, u32[]{:S(2)}, u32[]{:S(2)}) collective-permute-start(f32[8,128,128]{2,1,0:T(8,128)} %gate.23), channel_id=1, source_target_pairs={{0,1},{1,2},{2,3},{3,0},{4,5},{5,6},{6,7},{7,4},{8,9},{9,10},{10,1... | collective-permute-start | bytes 1572872 | tf_op jit(solution)/shard_map/ppermute | solution.py:552
  223.6 57.6 %collective-permute-start.17 = (f32[8,128,128]{2,1,0:T(8,128)}, f32[8,128,128]{2,1,0:T(8,128)}, u32[]{:S(2)}, u32[]{:S(2)}) collective-permute-start(f32[8,128,128]{2,1,0:T(8,128)} %get-tuple-element.105), channel_id=1, source_target_pairs={{0,2},{1,3},{2,0},{3,1},{4,6},{5,7},{6,4},{7,5},{8,10},{9,11},{10,... | collective-permute-start | bytes 1572872 | tf_op jit(solution)/shard_map/ppermute | solution.py:552
  243.6 37.6 %collective-permute-start.18 = (f32[8,128,128]{2,1,0:T(8,128)}, f32[8,128,128]{2,1,0:T(8,128)}, u32[]{:S(2)}, u32[]{:S(2)}) collective-permute-start(f32[8,128,128]{2,1,0:T(8,128)} %get-tuple-element.106), channel_id=1, source_target_pairs={{0,3},{1,0},{2,1},{3,2},{4,7},{5,4},{6,5},{7,6},{8,11},{9,8},{10,9... | collective-permute-start | bytes 1572872 | tf_op jit(solution)/shard_map/ppermute | solution.py:552
  246.9 34.3 %collective-permute-start.16 = (f32[8,128,128]{2,1,0:T(8,128)}, f32[8,128,128]{2,1,0:T(8,128)}, u32[]{:S(2)}, u32[]{:S(2)}) collective-permute-start(f32[8,128,128]{2,1,0:T(8,128)} %gate.26), channel_id=1, source_target_pairs={{0,1},{1,2},{2,3},{3,0},{4,5},{5,6},{6,7},{7,4},{8,9},{9,10},{10,1... | collective-permute-start | bytes 1572872 | tf_op jit(solution)/shard_map/ppermute | solution.py:552
  281.2 25.1 %collective-permute-start.19 = (f32[8,128,128]{2,1,0:T(8,128)}, f32[8,128,128]{2,1,0:T(8,128)}, u32[]{:S(2)}, u32[]{:S(2)}) collective-permute-start(f32[8,128,128]{2,1,0:T(8,128)} %get-tuple-element.107), channel_id=1, source_target_pairs={{0,1},{1,2},{2,3},{3,0},{4,5},{5,6},{6,7},{7,4},{8,9},{9,10},{10,1... | collective-permute-start | bytes 1572872 | tf_op jit(solution)/shard_map/ppermute | solution.py:552
  288.8 37.8 %collective-permute-start.20 = (f32[8,128,128]{2,1,0:T(8,128)}, f32[8,128,128]{2,1,0:T(8,128)}, u32[]{:S(2)}, u32[]{:S(2)}) collective-permute-start(f32[8,128,128]{2,1,0:T(8,128)} %get-tuple-element.108), channel_id=1, source_target_pairs={{0,2},{1,3},{2,0},{3,1},{4,6},{5,7},{6,4},{7,5},{8,10},{9,11},{10,... | collective-permute-start | bytes 1572872 | tf_op jit(solution)/shard_map/ppermute | solution.py:552
  292.1 34.5 %collective-permute-start.21 = (f32[8,128,128]{2,1,0:T(8,128)}, f32[8,128,128]{2,1,0:T(8,128)}, u32[]{:S(2)}, u32[]{:S(2)}) collective-permute-start(f32[8,128,128]{2,1,0:T(8,128)} %get-tuple-element.109), channel_id=1, source_target_pairs={{0,3},{1,0},{2,1},{3,2},{4,7},{5,4},{6,5},{7,6},{8,11},{9,8},{10,9... | collective-permute-start | bytes 1572872 | tf_op jit(solution)/shard_map/ppermute | solution.py:552
  301.7 53.7 %all-to-all-start.4 = ((f32[8,2,64,8,128]{4,3,2,1,0:T(8,128)}), f32[8,2,64,8,128]{4,3,2,1,0:T(8,128)}, u32[]{:S(2)}, u32[]{:S(2)}) async-start(f32[8,2,64,8,128]{4,3,2,1,0:T(8,128)} %x_inverse.4.refs_6_), calls=%async_computation.4 | async-start | bytes 8388608 | tf_op jit(solution)/shard_map/all_to_all | solution.py:556
  326.6 41.8 %collective-permute-start.22 = (f32[8,128,128]{2,1,0:T(8,128)}, f32[8,128,128]{2,1,0:T(8,128)}, u32[]{:S(2)}, u32[]{:S(2)}) collective-permute-start(f32[8,128,128]{2,1,0:T(8,128)} %get-tuple-element.112), channel_id=1, source_target_pairs={{0,1},{1,2},{2,3},{3,0},{4,5},{5,6},{6,7},{7,4},{8,9},{9,10},{10,1... | collective-permute-start | bytes 1572872 | tf_op jit(solution)/shard_map/ppermute | solution.py:552
  338.3 35.0 %collective-permute-start.23 = (f32[8,128,128]{2,1,0:T(8,128)}, f32[8,128,128]{2,1,0:T(8,128)}, u32[]{:S(2)}, u32[]{:S(2)}) collective-permute-start(f32[8,128,128]{2,1,0:T(8,128)} %get-tuple-element.113), channel_id=1, source_target_pairs={{0,2},{1,3},{2,0},{3,1},{4,6},{5,7},{6,4},{7,5},{8,10},{9,11},{10,... | collective-permute-start | bytes 1572872 | tf_op jit(solution)/shard_map/ppermute | solution.py:552
  339.9 33.4 %collective-permute-start.24 = (f32[8,128,128]{2,1,0:T(8,128)}, f32[8,128,128]{2,1,0:T(8,128)}, u32[]{:S(2)}, u32[]{:S(2)}) collective-permute-start(f32[8,128,128]{2,1,0:T(8,128)} %get-tuple-element.114), channel_id=1, source_target_pairs={{0,3},{1,0},{2,1},{3,2},{4,7},{5,4},{6,5},{7,6},{8,11},{9,8},{10,9... | collective-permute-start | bytes 1572872 | tf_op jit(solution)/shard_map/ppermute | solution.py:552
  355.4 53.7 %all-to-all-start.5 = ((f32[8,2,64,8,128]{4,3,2,1,0:T(8,128)}), f32[8,2,64,8,128]{4,3,2,1,0:T(8,128)}, u32[]{:S(2)}, u32[]{:S(2)}) async-start(f32[8,2,64,8,128]{4,3,2,1,0:T(8,128)} %gate.30), calls=%async_computation.5 | async-start | bytes 8388608 | tf_op jit(solution)/shard_map/all_to_all | solution.py:556
  373.3 40.1 %collective-permute-start.25 = (f32[8,128,128]{2,1,0:T(8,128)}, f32[8,128,128]{2,1,0:T(8,128)S(1)}, u32[]{:S(2)}, u32[]{:S(2)}) collective-permute-start(f32[8,128,128]{2,1,0:T(8,128)} %get-tuple-element.118), channel_id=1, source_target_pairs={{0,1},{1,2},{2,3},{3,0},{4,5},{5,6},{6,7},{7,4},{8,9},{9,10},{10,1... | collective-permute-start | bytes 1572872 | tf_op jit(solution)/shard_map/ppermute | solution.py:552
  385.0 36.2 %collective-permute-start.26 = (f32[8,128,128]{2,1,0:T(8,128)}, f32[8,128,128]{2,1,0:T(8,128)S(1)}, u32[]{:S(2)}, u32[]{:S(2)}) collective-permute-start(f32[8,128,128]{2,1,0:T(8,128)} %get-tuple-element.119), channel_id=1, source_target_pairs={{0,2},{1,3},{2,0},{3,1},{4,6},{5,7},{6,4},{7,5},{8,10},{9,11},{10,... | collective-permute-start | bytes 1572872 | tf_op jit(solution)/shard_map/ppermute | solution.py:552
  387.4 33.8 %collective-permute-start.27 = (f32[8,128,128]{2,1,0:T(8,128)}, f32[8,128,128]{2,1,0:T(8,128)S(1)}, u32[]{:S(2)}, u32[]{:S(2)}) collective-permute-start(f32[8,128,128]{2,1,0:T(8,128)} %get-tuple-element.120), channel_id=1, source_target_pairs={{0,3},{1,0},{2,1},{3,2},{4,7},{5,4},{6,5},{7,6},{8,11},{9,8},{10,9... | collective-permute-start | bytes 1572872 | tf_op jit(solution)/shard_map/ppermute | solution.py:552
  409.1 31.0 %all-to-all-start.6 = ((f32[8,1,64,8,128]{4,3,2,1,0:T(8,128)}), f32[8,1,64,8,128]{4,3,2,1,0:T(8,128)}, u32[]{:S(2)}, u32[]{:S(2)}) async-start(f32[8,1,64,8,128]{4,3,2,1,0:T(8,128)} %gate.31._), calls=%async_computation.6 | async-start | bytes 4194304 | tf_op jit(solution)/shard_map/all_to_all | solution.py:556
  413.5 7.7 %copy-start.7 = (f32[8,128,128]{2,1,0:T(8,128)}, f32[8,128,128]{2,1,0:T(8,128)S(1)}, u32[]{:S(2)}) copy-start(f32[8,128,128]{2,1,0:T(8,128)S(1)} %collective-permute-done.25.refs_1_._) | copy-start | bytes 1572868
  421.2 0.8 copy-start.8
  422.0 0.8 copy-start.9
  440.1 30.2 %all-to-all-start.7 = ((f32[8,1,64,8,128]{4,3,2,1,0:T(8,128)}), f32[8,1,64,8,128]{4,3,2,1,0:T(8,128)S(1)}, u32[]{:S(2)}, u32[]{:S(2)}) async-start(f32[8,1,64,8,128]{4,3,2,1,0:T(8,128)} %gate.33), calls=%async_computation.7 | async-start | bytes 4194304 | tf_op jit(solution)/shard_map/all_to_all | solution.py:556
  470.3 1.3 copy-start.2
  (1 other events, 0.6 us)

commit v5 on v4

--- a/solution.py
+++ b/solution.py
@@ -440,7 +440,7 @@
     levels, lines, part_y = pieces[0].shape
     count, full_x = table.shape[1], table.shape[3]
     part_x = full_x // groups
-    steps = 2 if groups % 2 == 0 else 1
+    steps = 1
     rows = full_x // steps
     size = levels * full_x * part_y
     return pl.pallas_call(

time: 478 us -> 478 us (level)
  no operation moved by 1% of the time
where the time goes in v5:
time: 478 us; the launch traced here: 476 us
  starting transfers between devices  160 us (33%)
  Pallas kernels  155 us (32%)
  waiting for transfers between devices  147 us (31%)
  local copies, waits for them, and re-layouts  8.99 us (2%)
    ppermute x28, starting transfers between devices, shifted(): lax.ppermute(cells, axis, [(i, (i + shift) % count) for i in range(count)])  125 us
    all_to_all x8, waiting for transfers between devices, swap_x(): return lax.all_to_all(rows, 'gx', split_axis=0, concat_axis=0, tiled=True)  106 us
    ppermute x28, waiting for transfers between devices, shifted(): lax.ppermute(cells, axis, [(i, (i + shift) % count) for i in range(count)])  41 us
    all_to_all x8, starting transfers between devices, swap_x(): return lax.all_to_all(rows, 'gx', split_axis=0, concat_axis=0, tiled=True)  35.2 us
    pallas_call x2, Pallas kernels, y_solve(): pl.pallas_call(functools.partial(solve_kernel, sources, full), grid=(leve...  29.3 us
    pallas_call x4, Pallas kernels, x_inverse(): pl.pallas_call(functools.partial(x_inverse_kernel, sources), grid=(count,...  26.6 us
    pallas_call x2, Pallas kernels, make_section(): pl.pallas_call(section_kernel, grid=(count, part_x // sublanes), in_specs...  25.4 us
    pallas_call x4, Pallas kernels, x_forward(): pl.pallas_call(x_kernel, grid=(levels // block,), in_specs=[scalars, pl.B...  24.3 us
  transfers between devices with their start and end apart: 36, of which 12 were waited for; matrix products, arithmetic and copies ran while one was open for 1% of the time, Pallas kernels for 31%

profile of v5, /device:TPU:0, one launch (start us, length us, event | category | flops | bytes accessed | tf_op | source)
XLA Modules:
  0.0 476.2 jit_solution(3199682752135746986)
XLA Ops:
  0.6 4.5 into_levels.2._.refs_0_
  5.2 5.2 %all-to-all-start = ((f32[8,1,8,64,128]{4,3,2,1,0:T(8,128)}), f32[8,1,8,64,128]{4,3,2,1,0:T(8,128)S(1)}, u32[]{:S(2)}, u32[]{:S(2)}) async-start(f32[8,1,8,64,128]{4,3,2,1,0:T(8,128)} %into_levels.2._.refs_0_), calls=%async_computation | async-start | bytes 4194304 | tf_op jit(solution)/shard_map/all_to_all | solution.py:556
  10.4 6.8 %edges_of.1 = (f32[3,64,64]{2,1,0:T(8,128)}, f32[3,64,64]{2,1,0:T(8,128)}, f32[3,1,64,128]{3,2,1,0:T(8,128)}, f32[3,1,64,128]{3,2,1,0:T(8,128)}) custom-call(f32[3,64,64,128]{3,2,1,0:T(8,128)} %refs_3_.3, f32[8,1,8,64,128]{4,3,2,1,0:T(8,128)} %into_levels.2._.refs_0_), custom_call_target="tpu_custom_call" | custom-call | bytes 629145600 | tf_op jit(solution)/shard_map/edges_of/pallas_call | solution.py:167
  28.3 7.7 %into_levels.3.refs_0_ = f32[8,2,8,64,128]{4,3,2,1,0:T(8,128)} custom-call(f32[3,64,64,128]{3,2,1,0:T(8,128)} %base_ref.3, bf16[2,64,192]{2,1,0:T(8,128)(2,1)} %pad_maximum_fusion.3.matrix_ref, f32[8,1,8,64,128]{4,3,2,1,0:T(8,128)} %into_levels.2._.refs_0_, bf16[2,64,192]{2,1,0:T(8,128)(2,1)} %get-tuple-element.135.refs_11_.refs_1_, ...), custom_call_target="tpu_custom_call" | custom-call | flops 40265318400 | bytes 838860800 | tf_op jit(solution)/shard_map/into_levels/pallas_call | solution.py:119
  38.8 4.6 all-to-all-start.1
  44.0 5.1 %x_forward.4 = (f32[8,128,128]{2,1,0:T(8,128)}, f32[8,128,128]{2,1,0:T(8,128)}, f32[8,128,128]{2,1,0:T(8,128)}, f32[8,128,128]{2,1,0:T(8,128)}) custom-call(s32[1]{0:T(128)} %bitcast.me_ref.group_ref, f32[8,1,8,64,128]{4,3,2,1,0:T(8,128)} %copy-done, bf16[2,4,128,512]{3,2,1,0:T(8,128)(2,1)} %constant.29.clone.table_ref, f32[3,1,64,128]{3,2,1,0:T(8,128)} %copy-done.10, ...), custom_call_target="tpu_custom_call" | custom-call | flops 161061273600 | bytes 524288000 | tf_op jit(solution)/shard_map/x_forward/pallas_call | solution.py:334
  54.6 9.1 %make_section.2 = (f32[3,64,64,128]{3,2,1,0:T(8,128)}, f32[3,64,64,128]{3,2,1,0:T(8,128)}, f32[8,1,8,64,128]{4,3,2,1,0:T(8,128)}) custom-call(f32[3,64,64,128]{3,2,1,0:T(8,128)} %refs_3_.3, f32[3,64,64,128]{3,2,1,0:T(8,128)} %refs_3_.3, f32[3,64,64,128]{3,2,1,0:T(8,128)} %refs_3_.3, f32[3,64,64,128]{3,2,1,0:T(8,128)} %refs_3_.3, ...), custom_call_target="tpu_custom_call" | custom-call | flops 40265318400 | bytes 1887436800 | tf_op jit(solution)/shard_map/make_section/pallas_call | solution.py:246
  63.7 16.3 %make_section.3 = (f32[3,64,64,128]{3,2,1,0:T(8,128)}, f32[3,64,64,128]{3,2,1,0:T(8,128)}, f32[8,2,8,64,128]{4,3,2,1,0:T(8,128)}) custom-call(f32[3,64,64,128]{3,2,1,0:T(8,128)} %refs_3_.3, f32[3,64,64,128]{3,2,1,0:T(8,128)} %refs_3_.3, f32[3,64,64,128]{3,2,1,0:T(8,128)} %refs_3_.3, ...), custom_call_target="tpu_custom_call", output_to_operand_aliasing={{0}: (12, {}), {1}: (13, {})} | custom-call | flops 80530636800 | bytes 3774873600 | tf_op jit(solution)/shard_map/make_section/pallas_call | solution.py:246
  80.0 12.4 %all-to-all-done.1.rows_ref = f32[8,2,8,64,128]{4,3,2,1,0:T(8,128)} async-done(((f32[8,2,8,64,128]{4,3,2,1,0:T(8,128)}), f32[8,2,8,64,128]{4,3,2,1,0:T(8,128)}, u32[]{:S(2)}, u32[]{:S(2)}) %all-to-all-start.1) | async-done | bytes 4194336 | tf_op jit(solution)/shard_map/all_to_all | solution.py:556
  92.4 7.1 %x_forward.5 = (f32[8,128,128]{2,1,0:T(8,128)}, f32[8,128,128]{2,1,0:T(8,128)}, f32[8,128,128]{2,1,0:T(8,128)}, f32[8,128,128]{2,1,0:T(8,128)}) custom-call(s32[1]{0:T(128)} %bitcast.me_ref.group_ref, f32[8,2,8,64,128]{4,3,2,1,0:T(8,128)} %all-to-all-done.1.rows_ref, bf16[2,4,128,1024]{3,2,1,0:T(8,128)(2,1)} %constant.30.clone.table_ref, ...), custom_call_target="tpu_custom_call" | custom-call | flops 322122547200 | bytes 838860800 | tf_op jit(solution)/shard_map/x_forward/pallas_call | solution.py:334
  99.6 3.6 all-to-all-start.2
  108.5 21.3 %all-to-all-done.2.refs_1_.rows_ref = f32[8,1,8,64,128]{4,3,2,1,0:T(8,128)S(1)} async-done(((f32[8,1,8,64,128]{4,3,2,1,0:T(8,128)}), f32[8,1,8,64,128]{4,3,2,1,0:T(8,128)S(1)}, u32[]{:S(2)}, u32[]{:S(2)}) %all-to-all-start.2) | async-done | bytes 2097184 | tf_op jit(solution)/shard_map/all_to_all | solution.py:556
  131.1 4.6 all-to-all-start.3
  135.6 5.1 %x_forward.7 = (f32[8,128,128]{2,1,0:T(8,128)}, f32[8,128,128]{2,1,0:T(8,128)}, f32[8,128,128]{2,1,0:T(8,128)}, f32[8,128,128]{2,1,0:T(8,128)}) custom-call(s32[1]{0:T(128)} %bitcast.me_ref.group_ref, f32[8,1,8,64,128]{4,3,2,1,0:T(8,128)} %copy-done.1, bf16[2,4,128,512]{3,2,1,0:T(8,128)(2,1)} %constant.29.clone.table_ref, ...), custom_call_target="tpu_custom_call" | custom-call | flops 161061273600 | bytes 524288000 | tf_op jit(solution)/shard_map/x_forward/pallas_call | solution.py:334
  140.8 11.8 %collective-permute-start.12 = (f32[8,128,128]{2,1,0:T(8,128)}, f32[8,128,128]{2,1,0:T(8,128)}, u32[]{:S(2)}, u32[]{:S(2)}) collective-permute-start(f32[8,128,128]{2,1,0:T(8,128)} %get-tuple-element.90), channel_id=1, source_target_pairs={{0,2},{1,3},{2,0},{3,1},{4,6},{5,7},{6,4},{7,5},{8,10},{9,11},{10,... | collective-permute-start | bytes 1572872 | tf_op jit(solution)/shard_map/ppermute | solution.py:552
  152.5 3.4 collective-permute-start.13
  155.9 28.8 %all-to-all-done.3.rows_ref = f32[8,2,8,64,128]{4,3,2,1,0:T(8,128)} async-done(((f32[8,2,8,64,128]{4,3,2,1,0:T(8,128)}), f32[8,2,8,64,128]{4,3,2,1,0:T(8,128)}, u32[]{:S(2)}, u32[]{:S(2)}) %all-to-all-start.3) | async-done | bytes 4194336 | tf_op jit(solution)/shard_map/all_to_all | solution.py:556
  184.8 7.1 %x_forward.6 = (f32[8,128,128]{2,1,0:T(8,128)}, f32[8,128,128]{2,1,0:T(8,128)}, f32[8,128,128]{2,1,0:T(8,128)}, f32[8,128,128]{2,1,0:T(8,128)}) custom-call(s32[1]{0:T(128)} %bitcast.me_ref.group_ref, f32[8,2,8,64,128]{4,3,2,1,0:T(8,128)} %all-to-all-done.3.rows_ref, bf16[2,4,128,1024]{3,2,1,0:T(8,128)(2,1)} %constant.30.clone.table_ref, ...), custom_call_target="tpu_custom_call" | custom-call | flops 322122547200 | bytes 838860800 | tf_op jit(solution)/shard_map/x_forward/pallas_call | solution.py:334
  191.8 6.2 %collective-permute-start.14 = (f32[8,128,128]{2,1,0:T(8,128)}, f32[8,128,128]{2,1,0:T(8,128)}, u32[]{:S(2)}, u32[]{:S(2)}) collective-permute-start(f32[8,128,128]{2,1,0:T(8,128)} %get-tuple-element.92), channel_id=1, source_target_pairs={{0,2},{1,3},{2,0},{3,1},{4,6},{5,7},{6,4},{7,5},{8,10},{9,11},{10,... | collective-permute-start | bytes 1572872 | tf_op jit(solution)/shard_map/ppermute | solution.py:552
  198.0 3.4 collective-permute-start.15
  201.4 14.6 %y_solve.2 = (f32[8,128,128]{2,1,0:T(8,128)}, f32[8,128,128]{2,1,0:T(8,128)}, f32[8,128,128]{2,1,0:T(8,128)}, f32[8,128,128]{2,1,0:T(8,128)}, f32[8,128,128]{2,1...) custom-call(s32[1]{0:T(128)} %bitcast.me_ref.group_ref, ...), custom_call_target="tpu_custom_call" | custom-call | flops 644245094400 | bytes 1258291200 | tf_op jit(solution)/shard_map/y_solve/pallas_call | solution.py:394
  216.1 7.5 %collective-permute-done.14.refs_2_ = f32[8,128,128]{2,1,0:T(8,128)} collective-permute-done((f32[8,128,128]{2,1,0:T(8,128)}, f32[8,128,128]{2,1,0:T(8,128)}, u32[]{:S(2)}, u32[]{:S(2)}) %collective-permute-start.14) | collective-permute-done | bytes 524320 | tf_op jit(solution)/shard_map/ppermute | solution.py:552
  223.6 19.9 %collective-permute-start.17 = (f32[8,128,128]{2,1,0:T(8,128)}, f32[8,128,128]{2,1,0:T(8,128)}, u32[]{:S(2)}, u32[]{:S(2)}) collective-permute-start(f32[8,128,128]{2,1,0:T(8,128)} %get-tuple-element.105), channel_id=1, source_target_pairs={{0,2},{1,3},{2,0},{3,1},{4,6},{5,7},{6,4},{7,5},{8,10},{9,11},{10,... | collective-permute-start | bytes 1572872 | tf_op jit(solution)/shard_map/ppermute | solution.py:552
  243.6 3.4 collective-permute-start.18
  246.9 19.6 %collective-permute-start.16 = (f32[8,128,128]{2,1,0:T(8,128)}, f32[8,128,128]{2,1,0:T(8,128)}, u32[]{:S(2)}, u32[]{:S(2)}) collective-permute-start(f32[8,128,128]{2,1,0:T(8,128)} %gate.26), channel_id=1, source_target_pairs={{0,1},{1,2},{2,3},{3,0},{4,5},{5,6},{6,7},{7,4},{8,9},{9,10},{10,1... | collective-permute-start | bytes 1572872 | tf_op jit(solution)/shard_map/ppermute | solution.py:552
  266.5 14.6 %y_solve.3 = (f32[8,128,128]{2,1,0:T(8,128)}, f32[8,128,128]{2,1,0:T(8,128)}, f32[8,128,128]{2,1,0:T(8,128)}, f32[8,128,128]{2,1,0:T(8,128)}, f32[8,128,128]{2,1...) custom-call(s32[1]{0:T(128)} %bitcast.me_ref.group_ref, ...), custom_call_target="tpu_custom_call" | custom-call | flops 644245094400 | bytes 1258291200 | tf_op jit(solution)/shard_map/y_solve/pallas_call | solution.py:394
  281.2 7.6 %collective-permute-start.19 = (f32[8,128,128]{2,1,0:T(8,128)}, f32[8,128,128]{2,1,0:T(8,128)}, u32[]{:S(2)}, u32[]{:S(2)}) collective-permute-start(f32[8,128,128]{2,1,0:T(8,128)} %get-tuple-element.107), channel_id=1, source_target_pairs={{0,1},{1,2},{2,3},{3,0},{4,5},{5,6},{6,7},{7,4},{8,9},{9,10},{10,1... | collective-permute-start | bytes 1572872 | tf_op jit(solution)/shard_map/ppermute | solution.py:552
  293.6 7.9 %x_inverse.4.refs_6_ = f32[8,2,64,8,128]{4,3,2,1,0:T(8,128)} custom-call(s32[1]{0:T(128)} %bitcast.me_ref.group_ref, f32[8,128,128]{2,1,0:T(8,128)} %get-tuple-element.110._.refs_0_, f32[8,128,128]{2,1,0:T(8,128)} %get-tuple-element.111.refs_0_, f32[8,128,128]{2,1,0:T(8,128)} %collective-permute-done.16.refs_3_.refs_1_, ...), custom_call_target="tpu_custom_call" | custom-call | flops 322122547200 | bytes 838860800 | tf_op jit(solution)/shard_map/x_inverse/pallas_call | solution.py:446
  301.5 4.6 all-to-all-start.4
  306.1 20.5 %collective-permute-done.20.refs_4_.refs_2_ = f32[8,128,128]{2,1,0:T(8,128)} collective-permute-done((f32[8,128,128]{2,1,0:T(8,128)}, f32[8,128,128]{2,1,0:T(8,128)}, u32[]{:S(2)}, u32[]{:S(2)}) %collective-permute-start.20) | collective-permute-done | bytes 524320 | tf_op jit(solution)/shard_map/ppermute | solution.py:552
  326.6 11.7 %collective-permute-start.22 = (f32[8,128,128]{2,1,0:T(8,128)}, f32[8,128,128]{2,1,0:T(8,128)}, u32[]{:S(2)}, u32[]{:S(2)}) collective-permute-start(f32[8,128,128]{2,1,0:T(8,128)} %get-tuple-element.112), channel_id=1, source_target_pairs={{0,1},{1,2},{2,3},{3,0},{4,5},{5,6},{6,7},{7,4},{8,9},{9,10},{10,1... | collective-permute-start | bytes 1572872 | tf_op jit(solution)/shard_map/ppermute | solution.py:552
  340.7 7.9 %x_inverse.6.refs_0_ = f32[8,2,64,8,128]{4,3,2,1,0:T(8,128)} custom-call(s32[1]{0:T(128)} %bitcast.me_ref.group_ref, f32[8,128,128]{2,1,0:T(8,128)} %get-tuple-element.83._.refs_0_, f32[8,128,128]{2,1,0:T(8,128)} %get-tuple-element.110._.refs_0_, f32[8,128,128]{2,1,0:T(8,128)} %collective-permute-done.19.refs_3_.refs_1_, ...), custom_call_target="tpu_custom_call" | custom-call | flops 322122547200 | bytes 838860800 | tf_op jit(solution)/shard_map/x_inverse/pallas_call | solution.py:446
  348.6 6.6 %all-to-all-done.4.refs_1_.rows_ref = f32[8,2,64,8,128]{4,3,2,1,0:T(8,128)} async-done(((f32[8,2,64,8,128]{4,3,2,1,0:T(8,128)}), f32[8,2,64,8,128]{4,3,2,1,0:T(8,128)}, u32[]{:S(2)}, u32[]{:S(2)}) %all-to-all-start.4) | async-done | bytes 4194336 | tf_op jit(solution)/shard_map/all_to_all | solution.py:556
  355.2 4.6 all-to-all-start.5
  359.8 8.4 %from_levels.3.refs_6_.done_ref = f32[3,64,64,128]{3,2,1,0:T(8,128)} custom-call(f32[8,2,64,8,128]{4,3,2,1,0:T(8,128)} %all-to-all-done.4.refs_1_.rows_ref, bf16[2,64,192]{2,1,0:T(8,128)(2,1)} %get-tuple-element.136.refs_2_.matrix_ref, f32[3,64,64,128]{3,2,1,0:T(8,128)} %base_ref.3), custom_call_target="tpu_custom_call" | custom-call | flops 40265318400 | bytes 1258291200 | tf_op jit(solution)/shard_map/from_levels/pallas_call | solution.py:487
  368.2 5.2 %collective-permute-done.23.refs_2_.refs_4_ = f32[8,128,128]{2,1,0:T(8,128)} collective-permute-done((f32[8,128,128]{2,1,0:T(8,128)}, f32[8,128,128]{2,1,0:T(8,128)}, u32[]{:S(2)}, u32[]{:S(2)}) %collective-permute-start.23) | collective-permute-done | bytes 524320 | tf_op jit(solution)/shard_map/ppermute | solution.py:552
  373.3 11.7 %collective-permute-start.25 = (f32[8,128,128]{2,1,0:T(8,128)}, f32[8,128,128]{2,1,0:T(8,128)S(1)}, u32[]{:S(2)}, u32[]{:S(2)}) collective-permute-start(f32[8,128,128]{2,1,0:T(8,128)} %get-tuple-element.118), channel_id=1, source_target_pairs={{0,1},{1,2},{2,3},{3,0},{4,5},{5,6},{6,7},{7,4},{8,9},{9,10},{10,1... | collective-permute-start | bytes 1572872 | tf_op jit(solution)/shard_map/ppermute | solution.py:552
  387.4 5.4 %x_inverse.5.refs_0_ = f32[8,1,64,8,128]{4,3,2,1,0:T(8,128)} custom-call(s32[1]{0:T(128)} %bitcast.me_ref.group_ref, f32[8,128,128]{2,1,0:T(8,128)} %get-tuple-element.95._.refs_0_, f32[8,128,128]{2,1,0:T(8,128)} %get-tuple-element.83._.refs_0_, f32[8,128,128]{2,1,0:T(8,128)} %collective-permute-done.22.refs_1_.refs_3_, ...), custom_call_target="tpu_custom_call" | custom-call | flops 16106127360 | bytes 52428800 | tf_op jit(solution)/shard_map/x_inverse/pallas_call | solution.py:446
  392.8 16.1 %all-to-all-done.5.refs_1_.rows_ref = f32[8,2,64,8,128]{4,3,2,1,0:T(8,128)} async-done(((f32[8,2,64,8,128]{4,3,2,1,0:T(8,128)}), f32[8,2,64,8,128]{4,3,2,1,0:T(8,128)}, u32[]{:S(2)}, u32[]{:S(2)}) %all-to-all-start.5) | async-done | bytes 4194336 | tf_op jit(solution)/shard_map/all_to_all | solution.py:556
  408.9 4.6 all-to-all-start.6
  413.5 7.7 %collective-permute-done.26.refs_2_ = f32[8,128,128]{2,1,0:T(8,128)S(1)} collective-permute-done((f32[8,128,128]{2,1,0:T(8,128)}, f32[8,128,128]{2,1,0:T(8,128)S(1)}, u32[]{:S(2)}, u32[]{:S(2)}) %collective-permute-start.26) | collective-permute-done | bytes 524320 | tf_op jit(solution)/shard_map/ppermute | solution.py:552
  422.8 5.4 %x_inverse.7.refs_0_ = f32[8,1,64,8,128]{4,3,2,1,0:T(8,128)} custom-call(s32[1]{0:T(128)} %bitcast.me_ref.group_ref, f32[8,1,64,8,128]{4,3,2,1,0:T(8,128)} %gate.31._, f32[8,128,128]{2,1,0:T(8,128)} %get-tuple-element.95._.refs_0_, f32[8,128,128]{2,1,0:T(8,128)} %copy-done.7, f32[8,128,128]{2,1,0:T(8,128)} %copy-done.8, f32[8,128,128]{2,1,0:T(8,128)} %copy-done.9, ...), custom_call_target="tpu_custom_call" | custom-call | flops 161061273600 | bytes 524288000 | tf_op jit(solution)/shard_map/x_inverse/pallas_call | solution.py:446
  428.2 11.9 %all-to-all-done.6.refs_1_.refs_0_.rows_ref = f32[8,1,64,8,128]{4,3,2,1,0:T(8,128)} async-done(((f32[8,1,64,8,128]{4,3,2,1,0:T(8,128)}), f32[8,1,64,8,128]{4,3,2,1,0:T(8,128)}, u32[]{:S(2)}, u32[]{:S(2)}) %all-to-all-start.6) | async-done | bytes 2097184 | tf_op jit(solution)/shard_map/all_to_all | solution.py:556
  440.1 3.6 all-to-all-start.7
  443.7 8.4 %from_levels.4.base_ref = f32[3,64,64,128]{3,2,1,0:T(8,128)} custom-call(f32[8,2,64,8,128]{4,3,2,1,0:T(8,128)} %all-to-all-done.5.refs_1_.rows_ref, bf16[2,64,192]{2,1,0:T(8,128)(2,1)} %pad_maximum_fusion.6.refs_3_.matrix_ref, f32[3,64,64,128]{3,2,1,0:T(8,128)} %get-tuple-element.121.base_ref, ...), custom_call_target="tpu_custom_call", output_to_operand_aliasing={{}: (2, {})} | custom-call | flops 40265318400 | bytes 1258291200 | tf_op jit(solution)/shard_map/from_levels/pallas_call | solution.py:487
  452.1 9.3 %gradient_of.1 = (f32[3,64,64,128]{3,2,1,0:T(8,128)}, f32[64,64,128]{2,1,0:T(8,128)}) custom-call(f32[8,1,64,8,128]{4,3,2,1,0:T(8,128)} %all-to-all-done.6.refs_1_.refs_0_.rows_ref, bf16[2,64,192]{2,1,0:T(8,128)(2,1)} %get-tuple-element.136.refs_2_.matrix_ref, f32[3,64,64,128]{3,2,1,0:T(8,128)} %base_ref.3, ...), custom_call_target="tpu_custom_call", output_to_operand_aliasing={{0}: (3, {})} | custom-call | flops 20132659200 | bytes 1887436800 | tf_op jit(solution)/shard_map/gradient_of/pallas_call | solution.py:527
  461.5 8.9 %all-to-all-done.7.rows_ref = f32[8,1,64,8,128]{4,3,2,1,0:T(8,128)S(1)} async-done(((f32[8,1,64,8,128]{4,3,2,1,0:T(8,128)}), f32[8,1,64,8,128]{4,3,2,1,0:T(8,128)S(1)}, u32[]{:S(2)}, u32[]{:S(2)}) %all-to-all-start.7) | async-done | bytes 2097184 | tf_op jit(solution)/shard_map/all_to_all | solution.py:556
  471.6 4.6 from_levels.5
  (106 shorter events, 39.1 us)
Async XLA Ops:
  5.2 32.3 %all-to-all-start = ((f32[8,1,8,64,128]{4,3,2,1,0:T(8,128)}), f32[8,1,8,64,128]{4,3,2,1,0:T(8,128)S(1)}, u32[]{:S(2)}, u32[]{:S(2)}) async-start(f32[8,1,8,64,128]{4,3,2,1,0:T(8,128)} %into_levels.2._.refs_0_), calls=%async_computation | async-start | bytes 4194304 | tf_op jit(solution)/shard_map/all_to_all | solution.py:556
  10.3 13.3 %copy-start.4 = (f32[64,64]{1,0:T(8,128)S(1)}, f32[64,64]{1,0:T(8,128)}, u32[]{:S(2)}) copy-start(f32[64,64]{1,0:T(8,128)} %param.20) | copy-start | bytes 49156
  10.3 13.4 %copy-start.3 = (f32[64,64]{1,0:T(8,128)S(1)}, f32[64,64]{1,0:T(8,128)}, u32[]{:S(2)}) copy-start(f32[64,64]{1,0:T(8,128)} %param.18) | copy-start | bytes 49156
  10.3 13.8 %copy-start.5 = (f32[64,64]{1,0:T(8,128)S(1)}, f32[64,64]{1,0:T(8,128)}, u32[]{:S(2)}) copy-start(f32[64,64]{1,0:T(8,128)} %matrix_ref.1) | copy-start | bytes 49156
  10.3 17.3 %copy-start.6 = (f32[64]{0:T(128)S(1)}, f32[64]{0:T(128)}, u32[]{:S(2)}) copy-start(f32[64]{0:T(128)} %param.17) | copy-start | bytes 772
  17.2 18.9 %collective-permute-start.2 = (f32[3,64,64]{2,1,0:T(8,128)}, f32[3,64,64]{2,1,0:T(8,128)S(1)}, u32[]{:S(2)}, u32[]{:S(2)}) collective-permute-start(f32[3,64,64]{2,1,0:T(8,128)} %get-tuple-element.66), channel_id=1, source_target_pairs={{0,1},{1,2},{2,3},{3,0},{4,5},{5,6},{6,7},{7,4},{8,9},{9,10},{10,1... | collective-permute-start | bytes 147464 | tf_op jit(solution)/shard_map/ppermute | solution.py:552
  18.8 17.9 %collective-permute-start.3 = (f32[3,64,64]{2,1,0:T(8,128)}, f32[3,64,64]{2,1,0:T(8,128)S(1)}, u32[]{:S(2)}, u32[]{:S(2)}) collective-permute-start(f32[3,64,64]{2,1,0:T(8,128)} %get-tuple-element.67), channel_id=1, source_target_pairs={{0,3},{1,0},{2,1},{3,2},{4,7},{5,4},{6,5},{7,6},{8,11},{9,8},{10,9... | collective-permute-start | bytes 147464 | tf_op jit(solution)/shard_map/ppermute | solution.py:552
  21.0 22.3 %collective-permute-start = (f32[3,1,64,128]{3,2,1,0:T(8,128)}, f32[3,1,64,128]{3,2,1,0:T(8,128)S(1)}, u32[]{:S(2)}, u32[]{:S(2)}) collective-permute-start(f32[3,1,64,128]{3,2,1,0:T(8,128)} %get-tuple-element.64), channel_id=1, source_target_pairs={{0,4},{4,8},{8,12},{12,16},{16,20},{20,24},{24,28},{28,0},{1,5},{5... | collective-permute-start | bytes 294920 | tf_op jit(solution)/shard_map/ppermute | solution.py:552
  21.0 22.3 %collective-permute-start.1 = (f32[3,1,64,128]{3,2,1,0:T(8,128)}, f32[3,1,64,128]{3,2,1,0:T(8,128)S(1)}, u32[]{:S(2)}, u32[]{:S(2)}) collective-permute-start(f32[3,1,64,128]{3,2,1,0:T(8,128)} %get-tuple-element.65), channel_id=1, source_target_pairs={{0,28},{4,0},{8,4},{12,8},{16,12},{20,16},{24,20},{28,24},{1,29},{... | collective-permute-start | bytes 294920 | tf_op jit(solution)/shard_map/ppermute | solution.py:552
  37.4 1.3 copy-start
  38.8 53.7 %all-to-all-start.1 = ((f32[8,2,8,64,128]{4,3,2,1,0:T(8,128)}), f32[8,2,8,64,128]{4,3,2,1,0:T(8,128)}, u32[]{:S(2)}, u32[]{:S(2)}) async-start(f32[8,2,8,64,128]{4,3,2,1,0:T(8,128)} %gate.17), calls=%async_computation.1 | async-start | bytes 8388608 | tf_op jit(solution)/shard_map/all_to_all | solution.py:556
  43.3 0.7 copy-start.11
  49.1 50.4 %collective-permute-start.4 = (f32[8,128,128]{2,1,0:T(8,128)}, f32[8,128,128]{2,1,0:T(8,128)}, u32[]{:S(2)}, u32[]{:S(2)}) collective-permute-start(f32[8,128,128]{2,1,0:T(8,128)} %get-tuple-element.74), channel_id=1, source_target_pairs={{0,1},{1,2},{2,3},{3,0},{4,5},{5,6},{6,7},{7,4},{8,9},{9,10},{10,1... | collective-permute-start | bytes 1572872 | tf_op jit(solution)/shard_map/ppermute | solution.py:552
  50.7 48.8 %collective-permute-start.5 = (f32[8,128,128]{2,1,0:T(8,128)}, f32[8,128,128]{2,1,0:T(8,128)}, u32[]{:S(2)}, u32[]{:S(2)}) collective-permute-start(f32[8,128,128]{2,1,0:T(8,128)} %get-tuple-element.75), channel_id=1, source_target_pairs={{0,2},{1,3},{2,0},{3,1},{4,6},{5,7},{6,4},{7,5},{8,10},{9,11},{10,... | collective-permute-start | bytes 1572872 | tf_op jit(solution)/shard_map/ppermute | solution.py:552
  53.3 46.2 %collective-permute-start.6 = (f32[8,128,128]{2,1,0:T(8,128)}, f32[8,128,128]{2,1,0:T(8,128)}, u32[]{:S(2)}, u32[]{:S(2)}) collective-permute-start(f32[8,128,128]{2,1,0:T(8,128)} %get-tuple-element.76), channel_id=1, source_target_pairs={{0,3},{1,0},{2,1},{3,2},{4,7},{5,4},{6,5},{7,6},{8,11},{9,8},{10,9... | collective-permute-start | bytes 1572872 | tf_op jit(solution)/shard_map/ppermute | solution.py:552
  99.5 3.7 copy-start.12
  99.6 30.2 %all-to-all-start.2 = ((f32[8,1,8,64,128]{4,3,2,1,0:T(8,128)}), f32[8,1,8,64,128]{4,3,2,1,0:T(8,128)S(1)}, u32[]{:S(2)}, u32[]{:S(2)}) async-start(f32[8,1,8,64,128]{4,3,2,1,0:T(8,128)} %gate.18), calls=%async_computation.2 | async-start | bytes 4194304 | tf_op jit(solution)/shard_map/all_to_all | solution.py:556
  103.8 36.9 %collective-permute-start.8 = (f32[8,128,128]{2,1,0:T(8,128)}, f32[8,128,128]{2,1,0:T(8,128)}, u32[]{:S(2)}, u32[]{:S(2)}) collective-permute-start(f32[8,128,128]{2,1,0:T(8,128)} %get-tuple-element.80), channel_id=1, source_target_pairs={{0,2},{1,3},{2,0},{3,1},{4,6},{5,7},{6,4},{7,5},{8,10},{9,11},{10,... | collective-permute-start | bytes 1572872 | tf_op jit(solution)/shard_map/ppermute | solution.py:552
  106.4 34.3 %collective-permute-start.9 = (f32[8,128,128]{2,1,0:T(8,128)}, f32[8,128,128]{2,1,0:T(8,128)}, u32[]{:S(2)}, u32[]{:S(2)}) collective-permute-start(f32[8,128,128]{2,1,0:T(8,128)} %get-tuple-element.81), channel_id=1, source_target_pairs={{0,3},{1,0},{2,1},{3,2},{4,7},{5,4},{6,5},{7,6},{8,11},{9,8},{10,9... | collective-permute-start | bytes 1572872 | tf_op jit(solution)/shard_map/ppermute | solution.py:552
  107.8 48.1 %collective-permute-start.7 = (f32[8,128,128]{2,1,0:T(8,128)}, f32[8,128,128]{2,1,0:T(8,128)}, u32[]{:S(2)}, u32[]{:S(2)}) collective-permute-start(f32[8,128,128]{2,1,0:T(8,128)} %gate.20), channel_id=1, source_target_pairs={{0,1},{1,2},{2,3},{3,0},{4,5},{5,6},{6,7},{7,4},{8,9},{9,10},{10,1... | collective-permute-start | bytes 1572872 | tf_op jit(solution)/shard_map/ppermute | solution.py:552
  129.8 1.3 copy-start.1
  131.1 53.7 %all-to-all-start.3 = ((f32[8,2,8,64,128]{4,3,2,1,0:T(8,128)}), f32[8,2,8,64,128]{4,3,2,1,0:T(8,128)}, u32[]{:S(2)}, u32[]{:S(2)}) async-start(f32[8,2,8,64,128]{4,3,2,1,0:T(8,128)} %gate.19), calls=%async_computation.3 | async-start | bytes 8388608 | tf_op jit(solution)/shard_map/all_to_all | solution.py:556
  140.8 51.0 %collective-permute-start.12 = (f32[8,128,128]{2,1,0:T(8,128)}, f32[8,128,128]{2,1,0:T(8,128)}, u32[]{:S(2)}, u32[]{:S(2)}) collective-permute-start(f32[8,128,128]{2,1,0:T(8,128)} %get-tuple-element.90), channel_id=1, source_target_pairs={{0,2},{1,3},{2,0},{3,1},{4,6},{5,7},{6,4},{7,5},{8,10},{9,11},{10,... | collective-permute-start | bytes 1572872 | tf_op jit(solution)/shard_map/ppermute | solution.py:552
  152.5 39.3 %collective-permute-start.13 = (f32[8,128,128]{2,1,0:T(8,128)}, f32[8,128,128]{2,1,0:T(8,128)}, u32[]{:S(2)}, u32[]{:S(2)}) collective-permute-start(f32[8,128,128]{2,1,0:T(8,128)} %get-tuple-element.91), channel_id=1, source_target_pairs={{0,3},{1,0},{2,1},{3,2},{4,7},{5,4},{6,5},{7,6},{8,11},{9,8},{10,9... | collective-permute-start | bytes 1572872 | tf_op jit(solution)/shard_map/ppermute | solution.py:552
  155.9 45.5 %collective-permute-start.10 = (f32[8,128,128]{2,1,0:T(8,128)}, f32[8,128,128]{2,1,0:T(8,128)}, u32[]{:S(2)}, u32[]{:S(2)}) collective-permute-start(f32[8,128,128]{2,1,0:T(8,128)} %gate.22), channel_id=1, source_target_pairs={{0,1},{1,2},{2,3},{3,0},{4,5},{5,6},{6,7},{7,4},{8,9},{9,10},{10,1... | collective-permute-start | bytes 1572872 | tf_op jit(solution)/shard_map/ppermute | solution.py:552
  191.8 31.8 %collective-permute-start.14 = (f32[8,128,128]{2,1,0:T(8,128)}, f32[8,128,128]{2,1,0:T(8,128)}, u32[]{:S(2)}, u32[]{:S(2)}) collective-permute-start(f32[8,128,128]{2,1,0:T(8,128)} %get-tuple-element.92), channel_id=1, source_target_pairs={{0,2},{1,3},{2,0},{3,1},{4,6},{5,7},{6,4},{7,5},{8,10},{9,11},{10,... | collective-permute-start | bytes 1572872 | tf_op jit(solution)/shard_map/ppermute | solution.py:552
  198.0 25.6 %collective-permute-start.15 = (f32[8,128,128]{2,1,0:T(8,128)}, f32[8,128,128]{2,1,0:T(8,128)}, u32[]{:S(2)}, u32[]{:S(2)}) collective-permute-start(f32[8,128,128]{2,1,0:T(8,128)} %get-tuple-element.93), channel_id=1, source_target_pairs={{0,3},{1,0},{2,1},{3,2},{4,7},{5,4},{6,5},{7,6},{8,11},{9,8},{10,9... | collective-permute-start | bytes 1572872 | tf_op jit(solution)/shard_map/ppermute | solution.py:552
  201.4 45.5 %collective-permute-start.11 = (f32[8,128,128]{2,1,0:T(8,128)}, f32[8,128,128]{2,1,0:T(8,128)}, u32[]{:S(2)}, u32[]{:S(2)}) collective-permute-start(f32[8,128,128]{2,1,0:T(8,128)} %gate.23), channel_id=1, source_target_pairs={{0,1},{1,2},{2,3},{3,0},{4,5},{5,6},{6,7},{7,4},{8,9},{9,10},{10,1... | collective-permute-start | bytes 1572872 | tf_op jit(solution)/shard_map/ppermute | solution.py:552
  223.6 57.6 %collective-permute-start.17 = (f32[8,128,128]{2,1,0:T(8,128)}, f32[8,128,128]{2,1,0:T(8,128)}, u32[]{:S(2)}, u32[]{:S(2)}) collective-permute-start(f32[8,128,128]{2,1,0:T(8,128)} %get-tuple-element.105), channel_id=1, source_target_pairs={{0,2},{1,3},{2,0},{3,1},{4,6},{5,7},{6,4},{7,5},{8,10},{9,11},{10,... | collective-permute-start | bytes 1572872 | tf_op jit(solution)/shard_map/ppermute | solution.py:552
  243.6 37.6 %collective-permute-start.18 = (f32[8,128,128]{2,1,0:T(8,128)}, f32[8,128,128]{2,1,0:T(8,128)}, u32[]{:S(2)}, u32[]{:S(2)}) collective-permute-start(f32[8,128,128]{2,1,0:T(8,128)} %get-tuple-element.106), channel_id=1, source_target_pairs={{0,3},{1,0},{2,1},{3,2},{4,7},{5,4},{6,5},{7,6},{8,11},{9,8},{10,9... | collective-permute-start | bytes 1572872 | tf_op jit(solution)/shard_map/ppermute | solution.py:552
  246.9 34.3 %collective-permute-start.16 = (f32[8,128,128]{2,1,0:T(8,128)}, f32[8,128,128]{2,1,0:T(8,128)}, u32[]{:S(2)}, u32[]{:S(2)}) collective-permute-start(f32[8,128,128]{2,1,0:T(8,128)} %gate.26), channel_id=1, source_target_pairs={{0,1},{1,2},{2,3},{3,0},{4,5},{5,6},{6,7},{7,4},{8,9},{9,10},{10,1... | collective-permute-start | bytes 1572872 | tf_op jit(solution)/shard_map/ppermute | solution.py:552
  281.2 24.9 %collective-permute-start.19 = (f32[8,128,128]{2,1,0:T(8,128)}, f32[8,128,128]{2,1,0:T(8,128)}, u32[]{:S(2)}, u32[]{:S(2)}) collective-permute-start(f32[8,128,128]{2,1,0:T(8,128)} %get-tuple-element.107), channel_id=1, source_target_pairs={{0,1},{1,2},{2,3},{3,0},{4,5},{5,6},{6,7},{7,4},{8,9},{9,10},{10,1... | collective-permute-start | bytes 1572872 | tf_op jit(solution)/shard_map/ppermute | solution.py:552
  288.8 37.8 %collective-permute-start.20 = (f32[8,128,128]{2,1,0:T(8,128)}, f32[8,128,128]{2,1,0:T(8,128)}, u32[]{:S(2)}, u32[]{:S(2)}) collective-permute-start(f32[8,128,128]{2,1,0:T(8,128)} %get-tuple-element.108), channel_id=1, source_target_pairs={{0,2},{1,3},{2,0},{3,1},{4,6},{5,7},{6,4},{7,5},{8,10},{9,11},{10,... | collective-permute-start | bytes 1572872 | tf_op jit(solution)/shard_map/ppermute | solution.py:552
  292.1 34.5 %collective-permute-start.21 = (f32[8,128,128]{2,1,0:T(8,128)}, f32[8,128,128]{2,1,0:T(8,128)}, u32[]{:S(2)}, u32[]{:S(2)}) collective-permute-start(f32[8,128,128]{2,1,0:T(8,128)} %get-tuple-element.109), channel_id=1, source_target_pairs={{0,3},{1,0},{2,1},{3,2},{4,7},{5,4},{6,5},{7,6},{8,11},{9,8},{10,9... | collective-permute-start | bytes 1572872 | tf_op jit(solution)/shard_map/ppermute | solution.py:552
  301.5 53.7 %all-to-all-start.4 = ((f32[8,2,64,8,128]{4,3,2,1,0:T(8,128)}), f32[8,2,64,8,128]{4,3,2,1,0:T(8,128)}, u32[]{:S(2)}, u32[]{:S(2)}) async-start(f32[8,2,64,8,128]{4,3,2,1,0:T(8,128)} %x_inverse.4.refs_6_), calls=%async_computation.4 | async-start | bytes 8388608 | tf_op jit(solution)/shard_map/all_to_all | solution.py:556
  326.6 41.6 %collective-permute-start.22 = (f32[8,128,128]{2,1,0:T(8,128)}, f32[8,128,128]{2,1,0:T(8,128)}, u32[]{:S(2)}, u32[]{:S(2)}) collective-permute-start(f32[8,128,128]{2,1,0:T(8,128)} %get-tuple-element.112), channel_id=1, source_target_pairs={{0,1},{1,2},{2,3},{3,0},{4,5},{5,6},{6,7},{7,4},{8,9},{9,10},{10,1... | collective-permute-start | bytes 1572872 | tf_op jit(solution)/shard_map/ppermute | solution.py:552
  338.3 35.0 %collective-permute-start.23 = (f32[8,128,128]{2,1,0:T(8,128)}, f32[8,128,128]{2,1,0:T(8,128)}, u32[]{:S(2)}, u32[]{:S(2)}) collective-permute-start(f32[8,128,128]{2,1,0:T(8,128)} %get-tuple-element.113), channel_id=1, source_target_pairs={{0,2},{1,3},{2,0},{3,1},{4,6},{5,7},{6,4},{7,5},{8,10},{9,11},{10,... | collective-permute-start | bytes 1572872 | tf_op jit(solution)/shard_map/ppermute | solution.py:552
  339.9 33.4 %collective-permute-start.24 = (f32[8,128,128]{2,1,0:T(8,128)}, f32[8,128,128]{2,1,0:T(8,128)}, u32[]{:S(2)}, u32[]{:S(2)}) collective-permute-start(f32[8,128,128]{2,1,0:T(8,128)} %get-tuple-element.114), channel_id=1, source_target_pairs={{0,3},{1,0},{2,1},{3,2},{4,7},{5,4},{6,5},{7,6},{8,11},{9,8},{10,9... | collective-permute-start | bytes 1572872 | tf_op jit(solution)/shard_map/ppermute | solution.py:552
  355.2 53.7 %all-to-all-start.5 = ((f32[8,2,64,8,128]{4,3,2,1,0:T(8,128)}), f32[8,2,64,8,128]{4,3,2,1,0:T(8,128)}, u32[]{:S(2)}, u32[]{:S(2)}) async-start(f32[8,2,64,8,128]{4,3,2,1,0:T(8,128)} %gate.30), calls=%async_computation.5 | async-start | bytes 8388608 | tf_op jit(solution)/shard_map/all_to_all | solution.py:556
  373.3 40.2 %collective-permute-start.25 = (f32[8,128,128]{2,1,0:T(8,128)}, f32[8,128,128]{2,1,0:T(8,128)S(1)}, u32[]{:S(2)}, u32[]{:S(2)}) collective-permute-start(f32[8,128,128]{2,1,0:T(8,128)} %get-tuple-element.118), channel_id=1, source_target_pairs={{0,1},{1,2},{2,3},{3,0},{4,5},{5,6},{6,7},{7,4},{8,9},{9,10},{10,1... | collective-permute-start | bytes 1572872 | tf_op jit(solution)/shard_map/ppermute | solution.py:552
  385.0 36.2 %collective-permute-start.26 = (f32[8,128,128]{2,1,0:T(8,128)}, f32[8,128,128]{2,1,0:T(8,128)S(1)}, u32[]{:S(2)}, u32[]{:S(2)}) collective-permute-start(f32[8,128,128]{2,1,0:T(8,128)} %get-tuple-element.119), channel_id=1, source_target_pairs={{0,2},{1,3},{2,0},{3,1},{4,6},{5,7},{6,4},{7,5},{8,10},{9,11},{10,... | collective-permute-start | bytes 1572872 | tf_op jit(solution)/shard_map/ppermute | solution.py:552
  387.4 33.8 %collective-permute-start.27 = (f32[8,128,128]{2,1,0:T(8,128)}, f32[8,128,128]{2,1,0:T(8,128)S(1)}, u32[]{:S(2)}, u32[]{:S(2)}) collective-permute-start(f32[8,128,128]{2,1,0:T(8,128)} %get-tuple-element.120), channel_id=1, source_target_pairs={{0,3},{1,0},{2,1},{3,2},{4,7},{5,4},{6,5},{7,6},{8,11},{9,8},{10,9... | collective-permute-start | bytes 1572872 | tf_op jit(solution)/shard_map/ppermute | solution.py:552
  408.9 31.2 %all-to-all-start.6 = ((f32[8,1,64,8,128]{4,3,2,1,0:T(8,128)}), f32[8,1,64,8,128]{4,3,2,1,0:T(8,128)}, u32[]{:S(2)}, u32[]{:S(2)}) async-start(f32[8,1,64,8,128]{4,3,2,1,0:T(8,128)} %gate.31._), calls=%async_computation.6 | async-start | bytes 4194304 | tf_op jit(solution)/shard_map/all_to_all | solution.py:556
  413.5 7.7 %copy-start.7 = (f32[8,128,128]{2,1,0:T(8,128)}, f32[8,128,128]{2,1,0:T(8,128)S(1)}, u32[]{:S(2)}) copy-start(f32[8,128,128]{2,1,0:T(8,128)S(1)} %collective-permute-done.25.refs_1_._) | copy-start | bytes 1572868
  421.2 0.8 copy-start.8
  422.0 0.8 copy-start.9
  440.1 30.2 %all-to-all-start.7 = ((f32[8,1,64,8,128]{4,3,2,1,0:T(8,128)}), f32[8,1,64,8,128]{4,3,2,1,0:T(8,128)S(1)}, u32[]{:S(2)}, u32[]{:S(2)}) async-start(f32[8,1,64,8,128]{4,3,2,1,0:T(8,128)} %gate.33), calls=%async_computation.7 | async-start | bytes 4194304 | tf_op jit(solution)/shard_map/all_to_all | solution.py:556
  470.3 1.3 copy-start.2
  (1 other events, 0.6 us)
